TPU v7x, 256 devices: a whole 4x4x8 slice. The times are simulated.
256 devices in a mesh: px: 16 (over z, core), py: 16 (over y, x).
Axes of the slice: x: 4, y: 4, z: 8, core: 2. Of those that a mesh axis runs over, the one named last changes fastest.
Arguments:
- right_side: float32 [256, 512, 512], P('px', 'py'), may hold values from -10 to 10
- shift: float32 [256, 512, 512], P('px', 'py'), may hold values from 0.5 to 4
- coarse_inverse: float32 [2048, 2048], P(('px', 'py')), may hold values from -1 to 1, as said below
Outputs:
- solution_field: float32 [256, 512, 512], P('px', 'py')
- residual: float32 [256, 512, 512], P('px', 'py')
Inputs may be any that keep to these rules, and one draw needn't show every extreme that they name: `coarse_inverse`: exactly symmetric and positive definite.
All inputs are finite; a program needn't handle non-finite values.
Results may differ from a plain program's by a relative error of at most 0.00022.
Values sent between devices are 32-bit elements; how exact they have to be, the bound alone decides.
No kernel may reach another device: no remote copies, remote signals or barrier semaphores. Data moves between devices by JAX's collectives and lax.ppermute only.
A program may use at most 64 MiB of HBM per device.

v0:
```python
import jax
import jax.numpy as jnp
from jax import lax
from jax.sharding import PartitionSpec as P

ITERS = 2
SWEEPS = 3


def extended(cells, sides, width):
    for axis, dim in sides:
        count = lax.axis_size(axis)
        ends = count - 1
        head = lax.slice_in_dim(cells, 0, width, axis=dim)
        tail = lax.slice_in_dim(cells, cells.shape[dim] - width, cells.shape[dim], axis=dim)
        cells = jnp.concatenate(
            [
                lax.ppermute(tail, axis, [(i, (i + 1) % count) for i in range(ends)]),
                cells,
                lax.ppermute(head, axis, [((i + 1) % count, i) for i in range(ends)]),
            ],
            axis=dim,
        )
    return cells


def extend(field):
    return extended(field, (("px", 0), ("py", 1)), 1)


def operate(field, shift):
    padded = jnp.pad(extend(field), ((0, 0), (0, 0), (1, 1)))
    total = padded[:-2] + padded[1:-1] + padded[2:]
    total = total[:, :-2] + total[:, 1:-1] + total[:, 2:]
    total = total[:, :, :-2] + total[:, :, 1:-1] + total[:, :, 2:]
    return (27.0 + shift) * field - total


def inner_alignment(first, second):
    return lax.psum(jnp.sum(first * second), ("px", "py"))


def inner_curvature(first, second):
    return lax.psum(jnp.sum(first * second), ("px", "py"))


def coarse_values(resid, inverse_rows):
    groups = inverse_rows.shape[0]
    slab = resid.shape[2] // groups
    columns = jnp.sum(resid, axis=(0, 1))
    own_means = jnp.sum(columns.reshape(groups, slab), axis=1) / (
        resid.shape[0] * resid.shape[1] * slab
    )
    every = lax.all_gather(own_means, ("px", "py"), axis=0, tiled=True)
    return jnp.dot(inverse_rows, every, precision=lax.Precision.HIGHEST)


def precondition(resid, shift, inverse_rows):
    scale = 26.0 + shift
    smooth = resid / scale
    for sweep in range(SWEEPS - 1):
        smooth = smooth + (resid - operate(smooth, shift)) / scale
    values = coarse_values(resid, inverse_rows)
    groups = inverse_rows.shape[0]
    slab = resid.shape[2] // groups
    spread = jnp.broadcast_to(values[:, None], (groups, slab)).reshape(-1)
    return smooth + spread[None, None, :]


def per_device(right_side, shift, coarse_inverse):
    solution_field = jnp.zeros_like(right_side)
    residual = right_side
    zvalue = precondition(residual, shift, coarse_inverse)
    direction = zvalue
    rz_now = inner_alignment(residual, zvalue)
    for step in range(ITERS):
        image = operate(direction, shift)
        alpha = rz_now / inner_curvature(direction, image)
        solution_field = solution_field + alpha * direction
        residual = residual - alpha * image
        if step + 1 < ITERS:
            zvalue = precondition(residual, shift, coarse_inverse)
            rz_next = inner_alignment(residual, zvalue)
            direction = zvalue + rz_next / rz_now * direction
            rz_now = rz_next
    return (solution_field, residual)


def solution(mesh):
    placed = (P("px", "py", None), P("px", "py", None), P(("px", "py"), None))
    return jax.shard_map(
        per_device,
        mesh=mesh,
        in_specs=placed,
        out_specs=(P("px", "py", None), P("px", "py", None)),
        check_vma=False,
    )
```

profile of v0, /device:TPU:1, one launch (start us, length us, event | category | flops | bytes accessed | tf_op | source)
XLA Modules:
  0.0 525.1 jit_solution(7898365509412370300)
XLA Ops:
  0.6 1.8 add_divide_fusion.1
  2.5 4.9 collective-permute-start
  7.4 1.9 collective-permute-start.1
  9.4 3.6 collective-permute-done.1
  13.1 3.1 collective-permute-start.2
  16.2 1.3 collective-permute-start.3
  17.5 3.4 collective-permute-done.3
  20.9 0.8 select_maximum_fusion.20
  21.9 0.3 slice_add_fusion.22
  22.2 0.9 copy-done.1
  23.1 0.3 copy-done.2
  23.4 0.7 fusion.29
  24.3 3.3 collective-permute-start.4
  27.6 1.9 collective-permute-start.5
  29.7 81.6 %all-reduce.6 = f32[2048]{0:T(1024)S(1)} all-reduce(f32[2048]{0:T(1024)S(1)} %multiply_dynamic-update-slice_fusion.1), channel_id=1, replica_groups=mesh['px'=16,'py'=16] {'px','py'}, use_global_device_ids=true, to_apply=%add.6 | all-reduce | flops 2048 | bytes 16384
  111.4 2.3 collective-permute-start.6
  113.7 1.3 collective-permute-start.7
  115.4 3.0 collective-permute-done.7
  118.4 0.8 select_maximum_fusion.16
  119.7 1.0 copy-done.6
  120.6 0.8 fusion.16
  121.4 3.8 collective-permute-start.8
  125.2 1.9 collective-permute-start.9
  127.1 3.6 collective-permute-done.9
  130.8 3.0 collective-permute-start.10
  133.8 1.3 collective-permute-start.11
  135.1 3.4 collective-permute-done.11
  138.5 0.8 select_maximum_fusion.12
  139.7 2.3 multiply_reduce_fusion.2
  142.0 79.8 %all-reduce.8 = (f32[]{:T(128)}, f32[]{:T(128)}) all-reduce(f32[]{:T(128)} %get-tuple-element.3, f32[]{:T(128)} %get-tuple-element.2), channel_id=1, replica_groups=mesh['px'=16,'py'=16] {'px','py'}, use_global_device_ids=true, to_apply=%region_3.4 | all-reduce | flops 2 | bytes 16 | tf_op jit(solution)/shard_map/psum | solution.py:40
  223.2 1.4 fusion.23
  224.6 0.3 add_divide_fusion
  224.9 2.3 collective-permute-start.12
  227.2 2.0 collective-permute-start.13
  229.3 3.6 collective-permute-done.13
  232.9 2.6 collective-permute-start.14
  235.5 1.5 collective-permute-start.15
  237.2 3.0 collective-permute-done.15
  240.2 0.8 select_maximum_fusion.8
  241.5 1.0 copy-done.4
  242.4 0.8 fusion.10
  243.2 1.0 copy-done.7
  244.2 3.7 collective-permute-start.16
  247.9 1.9 collective-permute-start.17
  250.0 78.5 %all-reduce.7 = f32[2048]{0:T(1024)S(1)} all-reduce(f32[2048]{0:T(1024)S(1)} %multiply_dynamic-update-slice_fusion), channel_id=1, replica_groups=mesh['px'=16,'py'=16] {'px','py'}, use_global_device_ids=true, to_apply=%add.7 | all-reduce | flops 2048 | bytes 16384
  328.5 1.1 pad_maximum_fusion.5
  329.6 3.2 collective-permute-start.18
  332.8 1.3 collective-permute-start.19
  334.4 3.0 collective-permute-done.19
  337.5 2.1 select_maximum_fusion.4
  339.9 1.0 copy-done.8
  340.9 2.3 multiply_reduce_fusion.1
  343.2 77.1 %psum.30 = f32[]{:T(128)} all-reduce(f32[]{:T(128)} %get-tuple-element.8), channel_id=1, replica_groups=mesh['px'=16,'py'=16] {'px','py'}, use_global_device_ids=true, to_apply=%region_9.10 | all-reduce | flops 1 | bytes 8 | tf_op jit(solution)/shard_map/psum | solution.py:40
  421.5 1.5 multiply_add_fusion.1
  423.0 4.5 collective-permute-start.20
  427.5 1.9 collective-permute-start.21
  429.5 3.6 collective-permute-done.21
  433.2 1.3 collective-permute-start.22
  434.5 1.3 collective-permute-start.23
  435.8 3.4 collective-permute-done.23
  439.2 0.8 select_maximum_fusion
  440.4 2.4 multiply_reduce_fusion
  442.8 77.6 %psum.31 = f32[]{:T(128)} all-reduce(f32[]{:T(128)} %get-tuple-element.6), channel_id=1, replica_groups=mesh['px'=16,'py'=16] {'px','py'}, use_global_device_ids=true, to_apply=%region_11.12 | all-reduce | flops 1 | bytes 8 | tf_op jit(solution)/shard_map/psum | solution.py:44
  521.6 3.4 multiply_subtract_fusion
  (62 shorter events, 3.9 us)
Async XLA Ops:
  0.6 114.4 %copy-start = (f32[8,2048]{1,0:T(8,128)S(1)}, f32[8,2048]{1,0:T(8,128)}, u32[]{:S(2)}) copy-start(f32[8,2048]{1,0:T(8,128)} %param.5) | copy-start | bytes 196612
  2.5 6.9 %collective-permute-start = (f32[1,32,512]{2,1,0:T(8,128)S(1)}, f32[1,32,512]{2,1,0:T(8,128)S(1)}, u32[]{:S(2)}, u32[]{:S(2)}) collective-permute-start(f32[1,32,512]{2,1,0:T(8,128)S(1)} %get-tuple-element.37), channel_id=1, source_target_pairs={{0,16},{16,32},{32,48},{48,64},{64,80},{80,96},{96,112},{112,128},... | collective-permute-start | bytes 196616 | tf_op jit(solution)/shard_map/ppermute | solution.py:18
  7.4 5.6 %collective-permute-start.1 = (f32[1,32,512]{2,1,0:T(8,128)S(1)}, f32[1,32,512]{2,1,0:T(8,128)S(1)}, u32[]{:S(2)}, u32[]{:S(2)}) collective-permute-start(f32[1,32,512]{2,1,0:T(8,128)S(1)} %get-tuple-element.38), channel_id=1, source_target_pairs={{16,0},{32,16},{48,32},{64,48},{80,64},{96,80},{112,96},{128,112},... | collective-permute-start | bytes 196616 | tf_op jit(solution)/shard_map/ppermute | solution.py:20
  13.1 4.4 collective-permute-start.2
  16.2 4.7 collective-permute-start.3
  21.9 1.2 copy-start.1
  21.9 1.5 copy-start.2
  24.2 95.1 %copy-start.5 = (f32[16,32,512]{2,1,0:T(8,128)}, f32[16,32,512]{2,1,0:T(8,128)S(1)}, u32[]{:S(2)}) copy-start(f32[16,32,512]{2,1,0:T(8,128)S(1)} %get-tuple-element.34) | copy-start | bytes 3145732
  24.3 87.1 %collective-permute-start.4 = (f32[1,32,512]{2,1,0:T(8,128)S(1)}, f32[1,32,512]{2,1,0:T(8,128)S(1)}, u32[]{:S(2)}, u32[]{:S(2)}) collective-permute-start(f32[1,32,512]{2,1,0:T(8,128)S(1)} %get-tuple-element.35), channel_id=1, source_target_pairs={{0,16},{16,32},{32,48},{48,64},{64,80},{80,96},{96,112},{112,128},... | collective-permute-start | bytes 196616 | tf_op jit(solution)/shard_map/ppermute | solution.py:18
  27.6 83.8 %collective-permute-start.5 = (f32[1,32,512]{2,1,0:T(8,128)S(1)}, f32[1,32,512]{2,1,0:T(8,128)S(1)}, u32[]{:S(2)}, u32[]{:S(2)}) collective-permute-start(f32[1,32,512]{2,1,0:T(8,128)S(1)} %get-tuple-element.36), channel_id=1, source_target_pairs={{16,0},{32,16},{48,32},{64,48},{80,64},{96,80},{112,96},{128,112},... | collective-permute-start | bytes 196616 | tf_op jit(solution)/shard_map/ppermute | solution.py:20
  111.4 4.0 collective-permute-start.6
  113.7 4.7 collective-permute-start.7
  119.4 1.2 copy-start.6
  121.4 5.7 %collective-permute-start.8 = (f32[1,32,512]{2,1,0:T(8,128)S(1)}, f32[1,32,512]{2,1,0:T(8,128)S(1)}, u32[]{:S(2)}, u32[]{:S(2)}) collective-permute-start(f32[1,32,512]{2,1,0:T(8,128)S(1)} %get-tuple-element.31), channel_id=1, source_target_pairs={{0,16},{16,32},{32,48},{48,64},{64,80},{80,96},{96,112},{112,128},... | collective-permute-start | bytes 196616 | tf_op jit(solution)/shard_map/ppermute | solution.py:18
  125.2 5.6 %collective-permute-start.9 = (f32[1,32,512]{2,1,0:T(8,128)S(1)}, f32[1,32,512]{2,1,0:T(8,128)S(1)}, u32[]{:S(2)}, u32[]{:S(2)}) collective-permute-start(f32[1,32,512]{2,1,0:T(8,128)S(1)} %get-tuple-element.32), channel_id=1, source_target_pairs={{16,0},{32,16},{48,32},{64,48},{80,64},{96,80},{112,96},{128,112},... | collective-permute-start | bytes 196616 | tf_op jit(solution)/shard_map/ppermute | solution.py:20
  130.8 4.3 collective-permute-start.10
  133.8 4.7 collective-permute-start.11
  224.6 8.3 %copy-start.3 = (f32[16,32,512]{2,1,0:T(8,128)}, f32[16,32,512]{2,1,0:T(8,128)S(1)}, u32[]{:S(2)}) copy-start(f32[16,32,512]{2,1,0:T(8,128)S(1)} %get-tuple-element.11) | copy-start | bytes 3145732
  224.9 4.3 collective-permute-start.12
  227.2 5.6 %collective-permute-start.13 = (f32[1,32,512]{2,1,0:T(8,128)S(1)}, f32[1,32,512]{2,1,0:T(8,128)S(1)}, u32[]{:S(2)}, u32[]{:S(2)}) collective-permute-start(f32[1,32,512]{2,1,0:T(8,128)S(1)} %get-tuple-element.30), channel_id=1, source_target_pairs={{16,0},{32,16},{48,32},{64,48},{80,64},{96,80},{112,96},{128,112},... | collective-permute-start | bytes 196616 | tf_op jit(solution)/shard_map/ppermute | solution.py:20
  232.9 4.3 collective-permute-start.14
  235.5 4.7 collective-permute-start.15
  241.2 1.2 copy-start.4
  243.2 1.0 copy-start.7
  244.2 84.3 %collective-permute-start.16 = (f32[1,32,512]{2,1,0:T(8,128)S(1)}, f32[1,32,512]{2,1,0:T(8,128)S(1)}, u32[]{:S(2)}, u32[]{:S(2)}) collective-permute-start(f32[1,32,512]{2,1,0:T(8,128)S(1)} %get-tuple-element.27), channel_id=1, source_target_pairs={{0,16},{16,32},{32,48},{48,64},{64,80},{80,96},{96,112},{112,128},... | collective-permute-start | bytes 196616 | tf_op jit(solution)/shard_map/ppermute | solution.py:18
  247.9 80.6 %collective-permute-start.17 = (f32[1,32,512]{2,1,0:T(8,128)S(1)}, f32[1,32,512]{2,1,0:T(8,128)S(1)}, u32[]{:S(2)}, u32[]{:S(2)}) collective-permute-start(f32[1,32,512]{2,1,0:T(8,128)S(1)} %get-tuple-element.28), channel_id=1, source_target_pairs={{16,0},{32,16},{48,32},{64,48},{80,64},{96,80},{112,96},{128,112},... | collective-permute-start | bytes 196616 | tf_op jit(solution)/shard_map/ppermute | solution.py:20
  329.6 4.8 collective-permute-start.18
  332.8 4.7 collective-permute-start.19
  339.7 1.2 copy-start.8
  423.0 6.4 %collective-permute-start.20 = (f32[1,32,512]{2,1,0:T(8,128)S(1)}, f32[1,32,512]{2,1,0:T(8,128)S(1)}, u32[]{:S(2)}, u32[]{:S(2)}) collective-permute-start(f32[1,32,512]{2,1,0:T(8,128)S(1)} %get-tuple-element.25), channel_id=1, source_target_pairs={{0,16},{16,32},{32,48},{48,64},{64,80},{80,96},{96,112},{112,128},... | collective-permute-start | bytes 196616 | tf_op jit(solution)/shard_map/ppermute | solution.py:18
  427.5 5.6 %collective-permute-start.21 = (f32[1,32,512]{2,1,0:T(8,128)S(1)}, f32[1,32,512]{2,1,0:T(8,128)S(1)}, u32[]{:S(2)}, u32[]{:S(2)}) collective-permute-start(f32[1,32,512]{2,1,0:T(8,128)S(1)} %get-tuple-element.26), channel_id=1, source_target_pairs={{16,0},{32,16},{48,32},{64,48},{80,64},{96,80},{112,96},{128,112},... | collective-permute-start | bytes 196616 | tf_op jit(solution)/shard_map/ppermute | solution.py:20
  433.2 2.6 collective-permute-start.22
  434.5 4.7 collective-permute-start.23
where the time goes:
time: 527 us; the launch traced here: 525 us
  blocking collectives  395 us (75%)
  starting transfers between devices  57.5 us (11%)
  waiting for transfers between devices  33.8 us (6%)
  other arithmetic  28.1 us (5%)
  local copies, waits for them, and re-layouts  5.64 us (1%)
    unnamed x2, blocking collectives  160 us
    psum x2, blocking collectives, inner_alignment(): return lax.psum(jnp.sum(first * second), ('px', 'py'))  157 us
    psum x1, blocking collectives, inner_curvature(): return lax.psum(jnp.sum(first * second), ('px', 'py'))  77.6 us
    ppermute x12, starting transfers between devices, extended(): lax.ppermute(tail, axis, [(i, (i + 1) % count) for i in range(ends)])  37.9 us
    ppermute x12, waiting for transfers between devices, extended(): lax.ppermute(head, axis, [((i + 1) % count, i) for i in range(ends)])  33.8 us
    ppermute x12, starting transfers between devices, extended(): lax.ppermute(head, axis, [((i + 1) % count, i) for i in range(ends)])  19.5 us
  transfers between devices with their start and end apart: 24, of which 10 were waited for; matrix products, arithmetic and copies ran while one was open for 0% of the time, Pallas kernels for 0%

commit v1 on v0

v1 whole, which is shorter than its diff:
```python
import functools

import jax
import jax.numpy as jnp
from jax import lax
from jax.experimental import pallas as pl
from jax.experimental.pallas import tpu as pltpu
from jax.sharding import PartitionSpec as P

CX, CY, NZ = 16, 32, 512
AGG = 8
SLAB = NZ // AGG
CELLS = CX * CY * SLAB
W = 3
XE = CX + 2 * W
Y0 = 8
YE = CY + 2 * Y0
LANES = 128
F32 = jnp.float32
HIGH = lax.Precision.HIGHEST


def lane_sum(plane):
    lane = lax.broadcasted_iota(jnp.int32, (plane.shape[0], LANES), 1)
    parts = [plane[:, k * LANES : (k + 1) * LANES] for k in range(NZ // LANES)]
    up = [pltpu.roll(p, 1, axis=1) for p in parts]
    down = [pltpu.roll(p, LANES - 1, axis=1) for p in parts]
    zero = jnp.zeros_like(parts[0])
    out = []
    for k, p in enumerate(parts):
        left = jnp.where(lane == 0, up[k - 1] if k else zero, up[k])
        right = jnp.where(
            lane == LANES - 1, down[k + 1] if k + 1 < len(parts) else zero, down[k]
        )
        out.append(left + p + right)
    return jnp.concatenate(out, axis=1)


def plane_box(plane):
    rows = plane.shape[0]
    plane = plane + pltpu.roll(plane, 1, axis=0) + pltpu.roll(plane, rows - 1, axis=0)
    return lane_sum(plane)


def neighbours(ref, i):
    mid = ref[i]
    return plane_box(ref[i - 1] + mid + ref[i + 1]) - mid


def each(low, high, body):
    lax.fori_loop(low, high, lambda i, carry: (body(i), carry)[1], 0)


def total(x):
    return jnp.sum(x, keepdims=True)


def slab_matrix(offset):
    cell = lax.broadcasted_iota(jnp.int32, (NZ, LANES), 0)
    lane = lax.broadcasted_iota(jnp.int32, (NZ, LANES), 1)
    return jnp.where(cell // SLAB + offset == lane, 1.0, 0.0).astype(F32)


def spread_matrix():
    lane = lax.broadcasted_iota(jnp.int32, (LANES, NZ), 0)
    cell = lax.broadcasted_iota(jnp.int32, (LANES, NZ), 1)
    return jnp.where(cell // SLAB == lane, 1.0, 0.0).astype(F32)


def slab_sums(acc, offset):
    return jnp.dot(
        jnp.sum(acc, axis=0, keepdims=True), slab_matrix(offset),
        precision=HIGH, preferred_element_type=F32,
    )


def first_lanes(x):
    lane = lax.broadcasted_iota(jnp.int32, x.shape, 1)
    return jnp.where(lane < AGG, x, 0.0)


def coarse_rows(columns, vector):
    prod = lax.dot_general(
        columns, vector, (((0,), (0,)), ((), ())), precision=HIGH,
        preferred_element_type=F32,
    )
    row = lax.broadcasted_iota(jnp.int32, prod.shape, 0)
    lane = lax.broadcasted_iota(jnp.int32, prod.shape, 1)
    each_row = jnp.sum(
        jnp.where((row & (AGG - 1)) == lane, prod, 0.0), axis=1, keepdims=True
    )
    return jnp.sum(
        jnp.where((row // AGG) == lane, each_row, 0.0), axis=0, keepdims=True
    )


def coarse_operator(c, shift_sums, n_py):
    n = c.shape[0]
    row = lax.broadcasted_iota(jnp.int32, c.shape, 0)
    inner = row & (n_py - 1)
    t = (3.0 * SLAB - 2.0) * c + first_lanes(
        pltpu.roll(c, 1, axis=1) + pltpu.roll(c, LANES - 1, axis=1)
    )
    t = (
        (3.0 * CY - 2.0) * t
        + jnp.where(inner == 0, 0.0, pltpu.roll(t, 1, axis=0))
        + jnp.where(inner == n_py - 1, 0.0, pltpu.roll(t, n - 1, axis=0))
    )
    t = (
        (3.0 * CX - 2.0) * t
        + jnp.where(row < n_py, 0.0, pltpu.roll(t, n_py, axis=0))
        + jnp.where(row >= n - n_py, 0.0, pltpu.roll(t, n - n_py, axis=0))
    )
    return (27.0 * CELLS + shift_sums) * c - t


def assemble(ref, own, px_lo, px_hi, py_lo, py_hi, base=0):
    ref[...] = jnp.zeros_like(ref)
    ref[W : W + CX, Y0 : Y0 + CY] = own[...]
    ref[:W, Y0 : Y0 + CY] = px_lo[...]
    ref[W + CX :, Y0 : Y0 + CY] = px_hi[...]
    for i in range(XE):
        at = base + i * W
        ref[i, Y0 - W : Y0] = py_lo[at : at + W]
        ref[i, Y0 + CY : Y0 + CY + W] = py_hi[at : at + W]


def own_rows(plane):
    return plane[Y0 : Y0 + CY]


def smooth(rref, iref, zref, yref):
    def first(i):
        zref[i] = rref[i] * iref[i]

    def second(i):
        yref[i] = (rref[i] + neighbours(zref, i)) * iref[i]

    def third(i):
        zref[i] = (rref[i] + neighbours(yref, i)) * iref[i]

    each(0, XE, first)
    each(1, XE - 1, second)
    each(2, XE - 2, third)


def coarse_planes(where, cref, n_px, n_py, rows9):
    a, b = where[0], where[1]
    rows9[...] = jnp.zeros_like(rows9)
    for da in (-1, 0, 1):
        for db in (-1, 0, 1):
            aa, bb = a + da, b + db
            inside = (aa >= 0) & (aa < n_px) & (bb >= 0) & (bb < n_py)
            k = jnp.clip(aa, 0, n_px - 1) * n_py + jnp.clip(bb, 0, n_py - 1)
            at = (da + 1) * 3 + db + 1
            rows9[at : at + 1] = jnp.where(inside, cref[pl.ds(k, 1), :], 0.0)
    spread = jnp.dot(rows9[...], spread_matrix(), precision=HIGH, preferred_element_type=F32)
    t = lax.broadcasted_iota(jnp.int32, (YE, NZ), 0)
    planes = []
    for da in range(3):
        lo, mid, hi = (spread[da * 3 + k : da * 3 + k + 1] for k in range(3))
        planes.append(jnp.where(t < Y0, lo, jnp.where(t < Y0 + CY, mid, hi)))
    return planes, [plane_box(p) for p in planes]


def box_plane(boxes, i):
    x = i - W
    lo, mid, hi = boxes
    if x <= -2:
        return 3.0 * lo
    if x == -1:
        return 2.0 * lo + mid
    if x == 0:
        return lo + 2.0 * mid
    if x < CX - 1:
        return 3.0 * mid
    if x == CX - 1:
        return 2.0 * mid + hi
    if x == CX:
        return mid + 2.0 * hi
    return 3.0 * hi


def block_plane(planes, i):
    return planes[0 if i < W else 1 if i < W + CX else 2]


def kernel_a(where, r, s, rlo, rhi, slo, shi, ylo, yhi, columns, g1,
             rext, sext, iext, u, v, row, zref, yref, accv, accs, *, n_px, n_py):
    assemble(rext, r, rlo, rhi, ylo, yhi)
    assemble(sext, s, slo, shi, ylo, yhi, XE * W)
    a, b = where[0], where[1]
    t = lax.broadcasted_iota(jnp.int32, (YE, NZ), 0)
    low = jnp.where(b > 0, Y0 - W, Y0)
    high = jnp.where(b < n_py - 1, Y0 + CY + W, Y0 + CY)
    first = jnp.where(a > 0, 0, W)
    last = jnp.where(a < n_px - 1, XE, W + CX)
    inside = (t >= low) & (t < high)

    def invert(i):
        keep = inside & (i >= first) & (i < last)
        iext[i] = jnp.where(keep, 1.0 / (26.0 + sext[i]), 0.0)

    each(0, XE, invert)
    smooth(rext, iext, zref, yref)
    accv[...] = jnp.zeros_like(accv)
    accs[...] = jnp.zeros_like(accs)

    def apply(i, carry):
        ru, uv = carry
        uu = own_rows(zref[i])
        ss = own_rows(sext[i])
        vv = (26.0 + ss) * uu - own_rows(neighbours(zref, i))
        u[i - W] = uu
        v[i - W] = vv
        accv[...] += vv
        accs[...] += ss
        return ru + own_rows(rext[i]) * uu, uv + uu * vv

    zero = jnp.zeros((CY, NZ), F32)
    ru, uv = lax.fori_loop(W, W + CX, apply, (zero, zero))
    c = coarse_rows(columns[...], g1[...])
    lane = lax.broadcasted_iota(jnp.int32, (1, LANES), 1)
    out = c + slab_sums(accv[...], AGG) * (1.0 / CELLS) + slab_sums(accs[...], 2 * AGG)
    out = out + jnp.where(lane == 24, total(ru), 0.0) + jnp.where(lane == 25, total(uv), 0.0)
    row[...] = jnp.broadcast_to(out, row.shape)


def kernel_b(where, rext, sext, iext, v, vlo, vhi, ylo, yhi, columns, g1, g2,
             r1o, uo, vo, qo, row, scal, rref, qref, zref, yref, cref, rows9, accv, *,
             n_px, n_py):
    g = g2[...]
    m = first_lanes(g1[...])
    c = first_lanes(g)
    w = first_lanes(pltpu.roll(g, LANES - AGG, axis=1))
    shifts = first_lanes(pltpu.roll(g, LANES - 2 * AGG, axis=1))
    lane = lax.broadcasted_iota(jnp.int32, g.shape, 1)
    tc = coarse_operator(c, shifts, n_py)
    rz = total(jnp.where(lane == 24, g, 0.0) + CELLS * (m * c))
    curv = total(jnp.where(lane == 25, g, 0.0) + (2.0 * CELLS) * (c * w) + c * tc)
    alpha = rz / curv
    e = w + tc * (1.0 / CELLS)
    mnew = m - alpha * e
    cref[...] = c
    cnew = coarse_rows(columns[...], mnew)
    planes, boxes = coarse_planes(where, cref, n_px, n_py, rows9)
    assemble(qref, v, vlo, vhi, ylo, yhi)

    def image(i, pc, bc):
        q = qref[i] + (27.0 + sext[i]) * pc - bc
        qref[i] = q
        rref[i] = rext[i] - alpha * q

    for i in (0, 1, 2, 3, W + CX - 1, W + CX, W + CX + 1, W + CX + 2):
        image(i, block_plane(planes, i), box_plane(boxes, i))
    pc, bc = planes[1], 3.0 * boxes[1]
    each(W + 1, W + CX - 1, lambda i: image(i, pc, bc))
    smooth(rref, iext, zref, yref)
    accv[...] = jnp.zeros_like(accv)

    def apply(i, carry):
        ru, uv, uq = carry
        uu = own_rows(zref[i])
        rr = own_rows(rref[i])
        qq = own_rows(qref[i])
        vv = (26.0 + own_rows(sext[i])) * uu - own_rows(neighbours(zref, i))
        uo[i - W] = uu
        vo[i - W] = vv
        r1o[i - W] = rr
        qo[i - W] = qq
        accv[...] += vv
        return ru + rr * uu, uv + uu * vv, uq + uu * qq

    zero = jnp.zeros((CY, NZ), F32)
    ru, uv, uq = lax.fori_loop(W, W + CX, apply, (zero, zero, zero))
    me = where[0] * n_py + where[1]
    cref[...] = e
    e_own = cref[pl.ds(me, 1), :]
    cref[...] = mnew
    m_own = cref[pl.ds(me, 1), :]
    lane = lax.broadcasted_iota(jnp.int32, (1, LANES), 1)
    out = cnew + slab_sums(accv[...], AGG) * (1.0 / CELLS)
    out = out + jnp.where(lane == 24, total(ru) + CELLS * total(m_own * cnew), 0.0)
    out = out + jnp.where(lane == 25, total(uv), 0.0)
    out = out + jnp.where(lane == 26, total(uq) + CELLS * total(e_own * cnew), 0.0)
    row[...] = jnp.broadcast_to(out, row.shape)
    at = lax.broadcasted_iota(jnp.int32, (8, LANES), 0)
    scal[...] = jnp.where(at == 0, rz, jnp.where(at == 1, curv, alpha))


def kernel_c(where, s, u, r1, un, vn, q, g2, g3, scal, x, r2, cref, rows9, *, n_px, n_py):
    g = g3[...]
    c = first_lanes(g)
    w = first_lanes(pltpu.roll(g, LANES - AGG, axis=1))
    shifts = first_lanes(pltpu.roll(g2[...], LANES - 2 * AGG, axis=1))
    lane = lax.broadcasted_iota(jnp.int32, g.shape, 1)
    tc = coarse_operator(c, shifts, n_py)
    rz, curv, alpha = scal[0:1, 0:1], scal[1:2, 0:1], scal[2:3, 0:1]
    rz1 = total(jnp.where(lane == 24, g, 0.0))
    zaz = total(jnp.where(lane == 25, g, 0.0) + (2.0 * CELLS) * (c * w) + c * tc)
    zq = total(jnp.where(lane == 26, g, 0.0))
    beta = rz1 / rz
    alpha2 = rz1 / (zaz + 2.0 * beta * zq + beta * beta * curv)
    first = alpha + alpha2 * beta
    me = where[0] * n_py + where[1]
    cref[...] = c
    planes, boxes = coarse_planes(where, cref, n_px, n_py, rows9)
    c_old = jnp.dot(
        jnp.broadcast_to(first_lanes(g2[pl.ds(me, 1), :]), (8, LANES)), spread_matrix(),
        precision=HIGH, preferred_element_type=F32,
    )
    pc = own_rows(planes[1])
    base = first * c_old[0:1] + alpha2 * pc

    def finish(i, bc):
        j = i - W
        x[j] = first * u[j] + alpha2 * un[j] + base
        image = vn[j] + (27.0 + s[j]) * pc - bc + beta * q[j]
        r2[j] = r1[j] - alpha2 * image

    for i in (W, W + CX - 1):
        finish(i, own_rows(box_plane(boxes, i)))
    bc = own_rows(3.0 * boxes[1])
    each(W + 1, W + CX - 1, lambda i: finish(i, bc))


VMEM = pl.BlockSpec(memory_space=pltpu.VMEM)
SMEM = pl.BlockSpec(memory_space=pltpu.SMEM)


def call(body, n_in, outs, scratch, name, **sizes):
    return pl.pallas_call(
        functools.partial(body, **sizes),
        in_specs=[SMEM] + [VMEM] * (n_in - 1),
        out_specs=[VMEM] * len(outs),
        out_shape=[jax.ShapeDtypeStruct(o, F32) for o in outs],
        scratch_shapes=[pltpu.VMEM(x, F32) for x in scratch],
        compiler_params=pltpu.CompilerParams(vmem_limit_bytes=48 * 1024 * 1024),
        name=name,
    )


EXT = (XE, YE, NZ)
OWN = (CX, CY, NZ)


def to_next(x, axis, n):
    return lax.ppermute(x, axis, [(i, i + 1) for i in range(n - 1)])


def to_previous(x, axis, n):
    return lax.ppermute(x, axis, [(i + 1, i) for i in range(n - 1)])


def halo(fields, n_px, n_py):
    lo = to_next(jnp.concatenate([f[-W:] for f in fields]), "px", n_px)
    hi = to_previous(jnp.concatenate([f[:W] for f in fields]), "px", n_px)
    los = [lo[k * W : (k + 1) * W] for k in range(len(fields))]
    his = [hi[k * W : (k + 1) * W] for k in range(len(fields))]

    def side(rows):
        return jnp.concatenate(
            [p[:, rows] for l, f, h in zip(los, fields, his) for p in (l, f, h)]
        ).reshape(len(fields) * XE * W, NZ)

    ylo = to_next(side(slice(CY - W, CY)), "py", n_py)
    yhi = to_previous(side(slice(0, W)), "py", n_py)
    return los, his, ylo, yhi


def gather(row, n):
    return lax.all_to_all(
        jnp.broadcast_to(row[:1], (n, LANES)), ("px", "py"), 0, 0, tiled=True
    )


def per_device(right_side, shift, coarse_inverse, *, n_px, n_py):
    n = n_px * n_py
    sizes = dict(n_px=n_px, n_py=n_py)
    where = jnp.stack([lax.axis_index("px"), lax.axis_index("py")]).astype(jnp.int32)
    columns = coarse_inverse.reshape(AGG, n, AGG).transpose(1, 0, 2).reshape(n, AGG * AGG)
    sums = jnp.sum(jnp.sum(right_side, axis=(0, 1)).reshape(AGG, SLAB), axis=1)
    g1 = gather(jnp.pad(sums / CELLS, (0, LANES - AGG))[None], n)
    (rlo, slo), (rhi, shi), ylo, yhi = halo((right_side, shift), n_px, n_py)
    rext, sext, iext, u, v, row = call(
        kernel_a, 11, [EXT, EXT, EXT, OWN, OWN, (8, LANES)],
        [EXT, EXT, (CY, NZ), (CY, NZ)], "first", **sizes,
    )(where, right_side, shift, rlo, rhi, slo, shi, ylo, yhi, columns, g1)
    g2 = gather(row, n)
    (vlo,), (vhi,), ylo, yhi = halo((v,), n_px, n_py)
    r1, un, vn, q, row, scal = call(
        kernel_b, 12, [OWN, OWN, OWN, OWN, (8, LANES), (8, LANES)],
        [EXT, EXT, EXT, EXT, (n, LANES), (16, LANES), (CY, NZ)], "second", **sizes,
    )(where, rext, sext, iext, v, vlo, vhi, ylo, yhi, columns, g1, g2)
    g3 = gather(row, n)
    return tuple(
        call(
            kernel_c, 10, [OWN, OWN], [(n, LANES), (16, LANES)], "third", **sizes
        )(where, shift, u, r1, un, vn, q, g2, g3, scal)
    )


def solution(mesh):
    n_px, n_py = mesh.shape["px"], mesh.shape["py"]
    placed = (P("px", "py", None), P("px", "py", None), P(("px", "py"), None))
    return jax.shard_map(
        functools.partial(per_device, n_px=n_px, n_py=n_py),
        mesh=mesh,
        in_specs=placed,
        out_specs=(P("px", "py", None), P("px", "py", None)),
        check_vma=False,
    )
```

time: 527 us -> 153 us (0.29)
  blocking collectives: 395 us -> 31.4 us
  Pallas kernels: 0 us -> 28.7 us
  other arithmetic: 28.1 us -> 1.95 us
  waiting for transfers between devices: 33.8 us -> 12.3 us
  local copies, waits for them, and re-layouts: 5.64 us -> 22 us
    psum x3 -> x0, blocking collectives: 235 us -> none  [the longest x2 157 us: inner_alignment(): return lax.psum(jnp.sum(first * second), ('px', 'py'))]
    unnamed x2 -> x0, blocking collectives: 160 us -> none
    ppermute x24 -> x8, starting transfers between devices: 57.5 us -> 23.7 us  [the longest x4 13 us: to_next(): return lax.ppermute(x, axis, [(i, i + 1) for i in range(n - 1)])]
    all_to_all x0 -> x1, blocking collectives: none -> 31.4 us  [gather(): lax.all_to_all(jnp.broadcast_to(row[:1], (n, LANES)), ('px', 'py'), 0, 0,...]
    all_to_all x0 -> x2, starting transfers between devices: none -> 30.9 us  [gather(): lax.all_to_all(jnp.broadcast_to(row[:1], (n, LANES)), ('px', 'py'), 0, 0,...]
    pallas_call x0 -> x3, Pallas kernels: none -> 28.7 us  [the longest x1 13.1 us: per_device(): call(kernel_b, 12, [OWN, OWN, OWN, OWN, (8, LANES), (8, LANES)], [EXT, EX...]
    ppermute x24 -> x8, waiting for transfers between devices: 33.8 us -> 12.3 us  [the longest x4 10.1 us: to_previous(): return lax.ppermute(x, axis, [(i + 1, i) for i in range(n - 1)])]
    reduce_sum x7 -> x2, other arithmetic: 9.33 us -> 0.23 us  [per_device(): sums = jnp.sum(jnp.sum(right_side, axis=(0, 1)).reshape(AGG, SLAB), axis=1)]
  transfers between devices with their start and end apart: 24 -> 10, of which waited for: 10 -> 6; matrix products, arithmetic and copies ran while one was open for 0% -> 8% of each run, Pallas kernels for 0% -> 0%
where the time goes in v1:
time: 153 us; the launch traced here: 152 us
  starting transfers between devices  54.6 us (36%)
  blocking collectives  31.4 us (21%)
  Pallas kernels  28.7 us (19%)
  local copies, waits for them, and re-layouts  22 us (14%)
  waiting for transfers between devices  12.3 us (8%)
  other arithmetic  1.95 us (1%)
    all_to_all x1, blocking collectives, gather(): lax.all_to_all(jnp.broadcast_to(row[:1], (n, LANES)), ('px', 'py'), 0, 0,...  31.4 us
    all_to_all x2, starting transfers between devices, gather(): lax.all_to_all(jnp.broadcast_to(row[:1], (n, LANES)), ('px', 'py'), 0, 0,...  30.9 us
    pallas_call x1, Pallas kernels, per_device(): call(kernel_b, 12, [OWN, OWN, OWN, OWN, (8, LANES), (8, LANES)], [EXT, EX...  13.1 us
    ppermute x4, starting transfers between devices, to_next(): return lax.ppermute(x, axis, [(i, i + 1) for i in range(n - 1)])  13 us
    pallas_call x1, Pallas kernels, per_device(): call(kernel_a, 11, [EXT, EXT, EXT, OWN, OWN, (8, LANES)], [EXT, EXT, (CY,...  12 us
    unnamed x35, local copies, waits for them, and re-layouts  11.7 us
    ppermute x4, starting transfers between devices, to_previous(): return lax.ppermute(x, axis, [(i + 1, i) for i in range(n - 1)])  10.7 us
    ppermute x4, waiting for transfers between devices, to_previous(): return lax.ppermute(x, axis, [(i + 1, i) for i in range(n - 1)])  10.1 us
  transfers between devices with their start and end apart: 10, of which 6 were waited for; matrix products, arithmetic and copies ran while one was open for 8% of the time, Pallas kernels for 0%

profile of v1, /device:TPU:1, one launch (start us, length us, event | category | flops | bytes accessed | tf_op | source)
XLA Modules:
  0.0 151.9 jit_solution(9319393277993735349)
XLA Ops:
  0.6 0.0 copy-start
  0.6 1.4 fusion.2
  2.0 0.8 pad_maximum_fusion
  2.8 4.9 %collective-permute-start = (f32[6,32,512]{2,1,0:T(8,128)}, f32[6,32,512]{2,1,0:T(8,128)}, u32[]{:S(2)}, u32[]{:S(2)}) collective-permute-start(f32[6,32,512]{2,1,0:T(8,128)} %pad_maximum_fusion), channel_id=1, source_target_pairs={{0,16},{16,32},{32,48},{48,64},{64,80},{80,96},{96,112},{112,128},... | collective-permute-start | bytes 1179656 | tf_op jit(solution)/shard_map/ppermute | solution.py:348
  7.7 0.0 copy-done
  7.7 0.1 reduce_sum.18
  7.9 0.1 reshape.47
  7.9 0.1 reduce_sum.19
  8.1 0.7 broadcast_in_dim.6
  8.8 13.4 %all-to-all-start = ((f32[256,1,128]{2,1,0:T(1,128)}), f32[256,1,128]{2,1,0:T(1,128)S(1)}, u32[]{:S(2)}, u32[]{:S(2)}) async-start(f32[256,1,128]{2,1,0:T(1,128)} %broadcast_in_dim.6), calls=%async_computation | async-start | bytes 262144 | tf_op jit(solution)/shard_map/all_to_all | solution.py:372
  22.2 0.8 pad_maximum_fusion.1
  22.9 4.0 %collective-permute-start.1 = (f32[6,32,512]{2,1,0:T(8,128)}, f32[6,32,512]{2,1,0:T(8,128)}, u32[]{:S(2)}, u32[]{:S(2)}) collective-permute-start(f32[6,32,512]{2,1,0:T(8,128)} %pad_maximum_fusion.1), channel_id=1, source_target_pairs={{16,0},{32,16},{48,32},{64,48},{80,64},{96,80},{112,96},{128,112},... | collective-permute-start | bytes 1179656 | tf_op jit(solution)/shard_map/ppermute | solution.py:352
  27.0 0.0 copy-done.14
  27.0 0.6 reshape.45
  27.6 0.3 copy.26
  27.9 0.1 copy.27.columns
  28.0 0.1 pad_add_fusion.where
  28.1 0.0 collective-permute-done
  28.1 0.8 constant_dynamic-update-slice_fusion.7
  28.9 0.1 slice_dynamic-update-slice_fusion.1
  29.0 3.6 %collective-permute-done.1 = f32[6,32,512]{2,1,0:T(8,128)} collective-permute-done((f32[6,32,512]{2,1,0:T(8,128)}, f32[6,32,512]{2,1,0:T(8,128)}, u32[]{:S(2)}, u32[]{:S(2)}) %collective-permute-start.1) | collective-permute-done | bytes 393248 | tf_op jit(solution)/shard_map/ppermute | solution.py:352
  32.5 0.8 constant_dynamic-update-slice_fusion.6
  33.4 0.8 constant_dynamic-update-slice_fusion.5
  34.2 0.1 slice_dynamic-update-slice_fusion
  34.3 0.8 constant_dynamic-update-slice_fusion.4
  35.2 0.1 reshape.44
  35.3 0.8 reshape.43
  36.1 3.3 %collective-permute-start.2 = (f32[132,512]{1,0:T(8,128)}, f32[132,512]{1,0:T(8,128)S(1)}, u32[]{:S(2)}, u32[]{:S(2)}) collective-permute-start(f32[132,512]{1,0:T(8,128)} %reshape.43), channel_id=1, source_target_pairs={{0,1},{1,2},{2,3},{3,4},{4,5},{5,6},{6,7},{7,8},{8,9},{9,10},{10,1... | collective-permute-start | bytes 811016 | tf_op jit(solution)/shard_map/ppermute | solution.py:348
  39.4 1.3 collective-permute-start.3
  40.7 1.8 %fusion.5 = (f32[3,32,512]{2,1,0:T(8,128)}, f32[3,32,512]{2,1,0:T(8,128)}) fusion(f32[6,32,512]{2,1,0:T(8,128)} %collective-permute-done), kind=kLoop, calls=%fused_computation.25 | loop fusion | bytes 786432 | tf_op jit(solution)/shard_map/slice | solution.py:358
  42.6 1.8 %fusion.4 = (f32[3,32,512]{2,1,0:T(8,128)}, f32[3,32,512]{2,1,0:T(8,128)}) fusion(f32[6,32,512]{2,1,0:T(8,128)} %collective-permute-done.1), kind=kLoop, calls=%fused_computation.24 | loop fusion | bytes 786432 | tf_op jit(solution)/shard_map/slice | solution.py:359
  44.4 0.0 all-to-all-done
  44.4 0.0 collective-permute-done.2.ylo
  44.4 0.7 copy-done.10
  45.1 1.6 %collective-permute-done.3.yhi = f32[132,512]{1,0:T(8,128)S(1)} collective-permute-done((f32[132,512]{1,0:T(8,128)S(1)}, f32[132,512]{1,0:T(8,128)S(1)}, u32[]{:S(2)}, u32[]{:S(2)}) %collective-permute-start.3) | collective-permute-done | bytes 270368 | tf_op jit(solution)/shard_map/ppermute | solution.py:352
  46.7 0.7 copy-done.12
  47.4 0.9 copy-done.6
  48.4 0.9 copy-done.7
  49.3 0.9 copy-done.8
  50.2 0.9 copy-done.9
  51.1 1.0 copy-done.11
  52.1 1.0 copy-done.13
  53.1 12.0 %first.1 = (f32[22,48,512]{2,1,0:T(8,128)}, f32[22,48,512]{2,1,0:T(8,128)}, f32[22,48,512]{2,1,0:T(8,128)}, f32[16,32,512]{2,1,0:T(8,128)S(1)}, f32[16,32,512]{2,1,0:T(8,128)S(1)}, /*index=5*/f32[8,128]{1,0:T(8,128)S(1)}) custom-call(s32[2]{0:T(128)S(1)} %pad_add_fusion.where, f32[16,32,512]{2,1,0:T(8,128)S(1)} %copy-done, f32[16,32,512]{2,1,0:T(8,128)S(1)} %copy-done.1, ...), custom_call_target="tpu_custom_call" | custom-call | tf_op jit(solution)/shard_map/first/pallas_call | solution.py:385
  65.1 1.0 copy-done.3
  66.0 0.8 broadcast_in_dim.7
  66.8 17.5 %all-to-all-start.1 = ((f32[256,1,128]{2,1,0:T(1,128)}), f32[256,1,128]{2,1,0:T(1,128)S(1)}, u32[]{:S(2)}, u32[]{:S(2)}) async-start(f32[256,1,128]{2,1,0:T(1,128)} %broadcast_in_dim.7), calls=%async_computation.1 | async-start | bytes 262144 | tf_op jit(solution)/shard_map/all_to_all | solution.py:372
  84.4 4.1 %collective-permute-start.5 = (f32[3,32,512]{2,1,0:T(8,128)S(1)}, f32[3,32,512]{2,1,0:T(8,128)S(1)}, u32[]{:S(2)}, u32[]{:S(2)}) collective-permute-start(f32[3,32,512]{2,1,0:T(8,128)S(1)} %get-tuple-element.28), channel_id=1, source_target_pairs={{16,0},{32,16},{48,32},{64,48},{80,64},{96,80},{112,96},{128,112},... | collective-permute-start | bytes 589832 | tf_op jit(solution)/shard_map/ppermute | solution.py:352
  88.5 1.9 %collective-permute-start.4 = (f32[3,32,512]{2,1,0:T(8,128)S(1)}, f32[3,32,512]{2,1,0:T(8,128)S(1)}, u32[]{:S(2)}, u32[]{:S(2)}) collective-permute-start(f32[3,32,512]{2,1,0:T(8,128)S(1)} %get-tuple-element.29), channel_id=1, source_target_pairs={{0,16},{16,32},{32,48},{48,64},{64,80},{80,96},{96,112},{112,128},... | collective-permute-start | bytes 589832 | tf_op jit(solution)/shard_map/ppermute | solution.py:348
  90.4 0.1 fusion
  90.5 1.4 collective-permute-done.5.vhi
  91.9 1.1 collective-permute-done.4.vlo
  93.1 0.1 reshape.49
  93.2 0.7 reshape.48
  93.9 2.9 %collective-permute-start.6 = (f32[66,512]{1,0:T(8,128)}, f32[66,512]{1,0:T(8,128)S(1)}, u32[]{:S(2)}, u32[]{:S(2)}) collective-permute-start(f32[66,512]{1,0:T(8,128)} %reshape.48), channel_id=1, source_target_pairs={{0,1},{1,2},{2,3},{3,4},{4,5},{5,6},{6,7},{7,8},{8,9},{9,10},{10,1... | collective-permute-start | bytes 405512 | tf_op jit(solution)/shard_map/ppermute | solution.py:348
  96.8 1.3 collective-permute-start.7
  98.1 0.0 all-to-all-done.1
  98.1 1.1 collective-permute-done.6.ylo
  99.2 3.5 %collective-permute-done.7.yhi = f32[66,512]{1,0:T(8,128)S(1)} collective-permute-done((f32[66,512]{1,0:T(8,128)S(1)}, f32[66,512]{1,0:T(8,128)S(1)}, u32[]{:S(2)}, u32[]{:S(2)}) %collective-permute-start.7) | collective-permute-done | bytes 135200 | tf_op jit(solution)/shard_map/ppermute | solution.py:352
  102.7 0.0 copy-done.2
  102.7 13.1 %second.1 = (f32[16,32,512]{2,1,0:T(8,128)S(1)}, f32[16,32,512]{2,1,0:T(8,128)S(1)}, f32[16,32,512]{2,1,0:T(8,128)S(1)}, f32[16,32,512]{2,1,0:T(8,128)S(1)}, f32[8,128]{1,0:T(8,128)S(1)}, /*index=5*/f32[8,128]{1,0:T(8,128)S(1)}) custom-call(s32[2]{0:T(128)S(1)} %pad_add_fusion.where, f32[22,48,512]{2,1,0:T(8,128)} %get-tuple-element.15.rext, ...), custom_call_target="tpu_custom_call" | custom-call | tf_op jit(solution)/shard_map/second/pallas_call | solution.py:391
  115.8 1.0 copy-done.5
  116.8 0.1 broadcast_in_dim.8
  116.9 31.4 %all_to_all.24 = f32[256,1,128]{2,1,0:T(1,128)S(1)} all-to-all(f32[256,1,128]{2,1,0:T(1,128)S(1)} %broadcast_in_dim.8), channel_id=1, replica_groups=mesh['px'=16,'py'=16] {'px','py'}, dimensions={0} | all-to-all | bytes 262144 | tf_op jit(solution)/shard_map/all_to_all | solution.py:372
  148.2 3.6 %third.1 = (f32[16,32,512]{2,1,0:T(8,128)}, f32[16,32,512]{2,1,0:T(8,128)}) custom-call(s32[2]{0:T(128)S(1)} %pad_add_fusion.where, f32[16,32,512]{2,1,0:T(8,128)S(1)} %copy-done.1, f32[16,32,512]{2,1,0:T(8,128)S(1)} %copy-done.4, f32[16,32,512]{2,1,0:T(8,128)S(1)} %get-tuple-element.20.r1, f32[16,32,512]{2,1,0:T(8,128)S(1)} %get-tuple-element.21.un, ...), custom_call_target="tpu_custom_call" | custom-call | tf_op jit(solution)/shard_map/third/pallas_call | solution.py:397
  (25 shorter events, 0.2 us)
Async XLA Ops:
  0.6 7.1 %copy-start = (f32[16,32,512]{2,1,0:T(8,128)S(1)}, f32[16,32,512]{2,1,0:T(8,128)}, u32[]{:S(2)}) copy-start(f32[16,32,512]{2,1,0:T(8,128)} %r.1) | copy-start | bytes 3145732
  0.6 26.4 %copy-start.14 = (f32[8,2048]{1,0:T(8,128)S(1)}, f32[8,2048]{1,0:T(8,128)}, u32[]{:S(2)}) copy-start(f32[8,2048]{1,0:T(8,128)} %param.5) | copy-start | bytes 196612
  2.8 25.3 %collective-permute-start = (f32[6,32,512]{2,1,0:T(8,128)}, f32[6,32,512]{2,1,0:T(8,128)}, u32[]{:S(2)}, u32[]{:S(2)}) collective-permute-start(f32[6,32,512]{2,1,0:T(8,128)} %pad_maximum_fusion), channel_id=1, source_target_pairs={{0,16},{16,32},{32,48},{48,64},{64,80},{80,96},{96,112},{112,128},... | collective-permute-start | bytes 1179656 | tf_op jit(solution)/shard_map/ppermute | solution.py:348
  8.8 25.5 %copy-start.1 = (f32[16,32,512]{2,1,0:T(8,128)S(1)}, f32[16,32,512]{2,1,0:T(8,128)}, u32[]{:S(2)}) copy-start(f32[16,32,512]{2,1,0:T(8,128)} %s.3) | copy-start | bytes 3145732
  8.8 35.6 %all-to-all-start = ((f32[256,1,128]{2,1,0:T(1,128)}), f32[256,1,128]{2,1,0:T(1,128)S(1)}, u32[]{:S(2)}, u32[]{:S(2)}) async-start(f32[256,1,128]{2,1,0:T(1,128)} %broadcast_in_dim.6), calls=%async_computation | async-start | bytes 262144 | tf_op jit(solution)/shard_map/all_to_all | solution.py:372
  22.9 9.6 %collective-permute-start.1 = (f32[6,32,512]{2,1,0:T(8,128)}, f32[6,32,512]{2,1,0:T(8,128)}, u32[]{:S(2)}, u32[]{:S(2)}) collective-permute-start(f32[6,32,512]{2,1,0:T(8,128)} %pad_maximum_fusion.1), channel_id=1, source_target_pairs={{16,0},{32,16},{48,32},{64,48},{80,64},{96,80},{112,96},{128,112},... | collective-permute-start | bytes 1179656 | tf_op jit(solution)/shard_map/ppermute | solution.py:352
  36.1 8.2 %collective-permute-start.2 = (f32[132,512]{1,0:T(8,128)}, f32[132,512]{1,0:T(8,128)S(1)}, u32[]{:S(2)}, u32[]{:S(2)}) collective-permute-start(f32[132,512]{1,0:T(8,128)} %reshape.43), channel_id=1, source_target_pairs={{0,1},{1,2},{2,3},{3,4},{4,5},{5,6},{6,7},{7,8},{8,9},{9,10},{10,1... | collective-permute-start | bytes 811016 | tf_op jit(solution)/shard_map/ppermute | solution.py:348
  39.4 7.3 %collective-permute-start.3 = (f32[132,512]{1,0:T(8,128)S(1)}, f32[132,512]{1,0:T(8,128)S(1)}, u32[]{:S(2)}, u32[]{:S(2)}) collective-permute-start(f32[132,512]{1,0:T(8,128)S(1)} %reshape.44), channel_id=1, source_target_pairs={{1,0},{2,1},{3,2},{4,3},{5,4},{6,5},{7,6},{8,7},{9,8},{10,9},{11,1... | collective-permute-start | bytes 811016 | tf_op jit(solution)/shard_map/ppermute | solution.py:352
  44.4 0.7 copy-start.10
  46.7 0.7 copy-start.12
  47.4 0.9 copy-start.6
  48.4 0.9 copy-start.7
  49.3 0.9 copy-start.8
  50.2 0.9 copy-start.9
  51.1 1.0 copy-start.11
  52.1 1.0 copy-start.13
  65.1 1.0 copy-start.3
  66.0 36.7 %copy-start.2 = (f32[16,32,512]{2,1,0:T(8,128)}, f32[16,32,512]{2,1,0:T(8,128)S(1)}, u32[]{:S(2)}) copy-start(f32[16,32,512]{2,1,0:T(8,128)S(1)} %get-tuple-element.18.v) | copy-start | bytes 3145732
  66.8 31.3 %all-to-all-start.1 = ((f32[256,1,128]{2,1,0:T(1,128)}), f32[256,1,128]{2,1,0:T(1,128)S(1)}, u32[]{:S(2)}, u32[]{:S(2)}) async-start(f32[256,1,128]{2,1,0:T(1,128)} %broadcast_in_dim.7), calls=%async_computation.1 | async-start | bytes 262144 | tf_op jit(solution)/shard_map/all_to_all | solution.py:372
  84.4 7.4 %collective-permute-start.5 = (f32[3,32,512]{2,1,0:T(8,128)S(1)}, f32[3,32,512]{2,1,0:T(8,128)S(1)}, u32[]{:S(2)}, u32[]{:S(2)}) collective-permute-start(f32[3,32,512]{2,1,0:T(8,128)S(1)} %get-tuple-element.28), channel_id=1, source_target_pairs={{16,0},{32,16},{48,32},{64,48},{80,64},{96,80},{112,96},{128,112},... | collective-permute-start | bytes 589832 | tf_op jit(solution)/shard_map/ppermute | solution.py:352
  88.5 4.5 %collective-permute-start.4 = (f32[3,32,512]{2,1,0:T(8,128)S(1)}, f32[3,32,512]{2,1,0:T(8,128)S(1)}, u32[]{:S(2)}, u32[]{:S(2)}) collective-permute-start(f32[3,32,512]{2,1,0:T(8,128)S(1)} %get-tuple-element.29), channel_id=1, source_target_pairs={{0,16},{16,32},{32,48},{48,64},{64,80},{80,96},{96,112},{112,128},... | collective-permute-start | bytes 589832 | tf_op jit(solution)/shard_map/ppermute | solution.py:348
  93.9 5.3 %collective-permute-start.6 = (f32[66,512]{1,0:T(8,128)}, f32[66,512]{1,0:T(8,128)S(1)}, u32[]{:S(2)}, u32[]{:S(2)}) collective-permute-start(f32[66,512]{1,0:T(8,128)} %reshape.48), channel_id=1, source_target_pairs={{0,1},{1,2},{2,3},{3,4},{4,5},{5,6},{6,7},{7,8},{8,9},{9,10},{10,1... | collective-permute-start | bytes 405512 | tf_op jit(solution)/shard_map/ppermute | solution.py:348
  96.8 5.9 %collective-permute-start.7 = (f32[66,512]{1,0:T(8,128)S(1)}, f32[66,512]{1,0:T(8,128)S(1)}, u32[]{:S(2)}, u32[]{:S(2)}) collective-permute-start(f32[66,512]{1,0:T(8,128)S(1)} %reshape.49), channel_id=1, source_target_pairs={{1,0},{2,1},{3,2},{4,3},{5,4},{6,5},{7,6},{8,7},{9,8},{10,9},{11,1... | collective-permute-start | bytes 405512 | tf_op jit(solution)/shard_map/ppermute | solution.py:352
  102.7 45.5 %copy-start.4 = (f32[16,32,512]{2,1,0:T(8,128)S(1)}, f32[16,32,512]{2,1,0:T(8,128)}, u32[]{:S(2)}) copy-start(f32[16,32,512]{2,1,0:T(8,128)} %copy-done.3) | copy-start | bytes 3145732
  115.8 1.0 copy-start.5

commit v2 on v0

v2 whole, which is shorter than its diff:
```python
import functools

import jax
import jax.numpy as jnp
from jax import lax
from jax.experimental import pallas as pl
from jax.experimental.pallas import tpu as pltpu
from jax.sharding import PartitionSpec as P

CX, CY, NZ = 16, 32, 512
AGG = 8
SLAB = NZ // AGG
CELLS = CX * CY * SLAB
H = 6
V = 3
T = 8
XE = CX + 2 * H
XV = CX + 2 * V
YE = CY + 2 * T
TILES = YE // T
LANES = 128
F32 = jnp.float32
HIGH = lax.Precision.HIGHEST
OWN = (CX, CY, NZ)
EXT = (XE, YE, NZ)
MID = (XV, YE, NZ)


def tile(t):
    return slice(t * T, (t + 1) * T)


def iota(shape, axis):
    return lax.broadcasted_iota(jnp.int32, shape, axis)


def chunks(row):
    return [row[:, k * LANES : (k + 1) * LANES] for k in range(NZ // LANES)]


def lane_sum(rows):
    lane = iota((rows.shape[0], LANES), 1)
    parts = chunks(rows)
    up = [pltpu.roll(p, 1, axis=1) for p in parts]
    down = [pltpu.roll(p, LANES - 1, axis=1) for p in parts]
    zero = jnp.zeros_like(parts[0])
    out = []
    for k, p in enumerate(parts):
        left = jnp.where(lane == 0, up[k - 1] if k else zero, up[k])
        right = jnp.where(
            lane == LANES - 1, down[k + 1] if k + 1 < len(parts) else zero, down[k]
        )
        out.append(left + p + right)
    return jnp.concatenate(out, axis=1)


def tile_boxes(xsum, tiles):
    row = iota((T, NZ), 0)
    have = {}

    def get(t):
        if t not in have:
            x = xsum(t)
            have[t] = (x, pltpu.roll(x, 1, axis=0), pltpu.roll(x, T - 1, axis=0))
        return have[t]

    for t in tiles:
        x, up, down = get(t)
        if t > 0:
            up = jnp.where(row == 0, get(t - 1)[1], up)
        if t < TILES - 1:
            down = jnp.where(row == T - 1, get(t + 1)[2], down)
        yield t, lane_sum(up + x + down)


def neighbours(ref, i, tiles):
    def xsum(t):
        return ref[i - 1, tile(t)] + ref[i, tile(t)] + ref[i + 1, tile(t)]

    for t, box in tile_boxes(xsum, tiles):
        mid = ref[i, tile(t)]
        yield t, box - mid, mid


def plane_box(plane):
    parts = [box for _, box in tile_boxes(lambda t: plane[tile(t)], range(TILES))]
    return jnp.concatenate(parts, axis=0)


def each(low, high, body):
    lax.fori_loop(low, high, lambda i, carry: (body(i), carry)[1], 0)


def total(x):
    return jnp.sum(x, keepdims=True)


def fold(rows):
    a, b, c, d = chunks(rows)
    return (a + b) + (c + d)


def exact_dot(a, b):
    return jnp.dot(a, b, precision=HIGH, preferred_element_type=F32)


def slab_sums(acc, offset):
    cell, lane = iota((NZ, LANES), 0), iota((NZ, LANES), 1)
    pick = jnp.where(cell // SLAB + offset == lane, 1.0, 0.0).astype(F32)
    return jnp.sum(exact_dot(acc, pick), axis=0, keepdims=True)


def spread(rows):
    lane, cell = iota((LANES, NZ), 0), iota((LANES, NZ), 1)
    return exact_dot(rows, jnp.where(cell // SLAB == lane, 1.0, 0.0).astype(F32))


def line_up(rows, offset, n_py):
    width = n_py * AGG
    src, dst = iota((LANES, width), 0), iota((LANES, width), 1)
    repeat = jnp.where((dst & (AGG - 1)) + offset == src, 1.0, 0.0).astype(F32)
    wide = exact_dot(rows, repeat)
    row, lane = iota(wide.shape, 0), iota(wide.shape, 1)
    wide = jnp.where((row & (n_py - 1)) == lane // AGG, wide, 0.0)
    return jnp.sum(wide.reshape(rows.shape[0] // n_py, n_py, width), axis=1)


def coarse_rows(inverse, vector):
    n, width = vector.shape
    acc = jnp.zeros((AGG, width), F32)
    for k in range(n):
        acc = acc + inverse[:, k * width : (k + 1) * width] * vector[k : k + 1]
    column = jnp.sum(acc, axis=1, keepdims=True)
    row, lane = iota((AGG, LANES), 0), iota((AGG, LANES), 1)
    return jnp.sum(jnp.where(row == lane, column, 0.0), axis=0, keepdims=True)


def coarse_operator(c, shift_sums):
    n, width = c.shape
    row, lane = iota(c.shape, 0), iota(c.shape, 1)
    slab = lane & (AGG - 1)
    t = (
        (3.0 * SLAB - 2.0) * c
        + jnp.where(slab == 0, 0.0, pltpu.roll(c, 1, axis=1))
        + jnp.where(slab == AGG - 1, 0.0, pltpu.roll(c, width - 1, axis=1))
    )
    t = (
        (3.0 * CY - 2.0) * t
        + jnp.where(lane < AGG, 0.0, pltpu.roll(t, AGG, axis=1))
        + jnp.where(lane >= width - AGG, 0.0, pltpu.roll(t, width - AGG, axis=1))
    )
    t = (
        (3.0 * CX - 2.0) * t
        + jnp.where(row == 0, 0.0, pltpu.roll(t, 1, axis=0))
        + jnp.where(row == n - 1, 0.0, pltpu.roll(t, n - 1, axis=0))
    )
    return (27.0 * CELLS + shift_sums) * c - t


def own_part(vector, where, ref):
    ref[...] = vector
    mine = ref[pl.ds(where[0], 1), :]
    lane = iota(mine.shape, 1)
    mine = jnp.where(lane // AGG == where[1], mine, 0.0)
    src, dst = iota((mine.shape[1], LANES), 0), iota((mine.shape[1], LANES), 1)
    pick = jnp.where((src & (AGG - 1)) == dst, 1.0, 0.0).astype(F32)
    return exact_dot(jnp.broadcast_to(mine, (T, mine.shape[1])), pick)[:1]


def coarse_planes(where, gathered, n_px, n_py, rows9):
    a, b = where[0], where[1]
    rows9[...] = jnp.zeros_like(rows9)
    for da in (-1, 0, 1):
        for db in (-1, 0, 1):
            aa, bb = a + da, b + db
            inside = (aa >= 0) & (aa < n_px) & (bb >= 0) & (bb < n_py)
            k = jnp.clip(aa, 0, n_px - 1) * n_py + jnp.clip(bb, 0, n_py - 1)
            at = (da + 1) * 3 + db + 1
            rows9[at : at + 1] = jnp.where(inside, gathered[pl.ds(k, 1), :], 0.0)
    fields = spread(rows9[...])
    y = iota((YE, NZ), 0)
    planes = []
    for da in range(3):
        lo, mid, hi = (fields[da * 3 + k : da * 3 + k + 1] for k in range(3))
        planes.append(jnp.where(y < T, lo, jnp.where(y < T + CY, mid, hi)))
    return planes, [plane_box(p) for p in planes]


def box_plane(boxes, x):
    lo, mid, hi = boxes
    if x <= -2:
        return 3.0 * lo
    if x == -1:
        return 2.0 * lo + mid
    if x == 0:
        return lo + 2.0 * mid
    if x < CX - 1:
        return 3.0 * mid
    if x == CX - 1:
        return 2.0 * mid + hi
    if x == CX:
        return mid + 2.0 * hi
    return 3.0 * hi


def kernel_pack_y(where, r, s, first, second, row):
    def copy(out, rows):
        out[0] = r[:, rows, :]
        out[1] = s[:, rows, :]

    @pl.when((where[1] & 1) == 0)
    def _():
        copy(first, slice(CY - T, CY))
        copy(second, slice(0, T))

    @pl.when((where[1] & 1) == 1)
    def _():
        copy(first, slice(0, T))
        copy(second, slice(CY - T, CY))

    def add(i, carry):
        ra, sa = carry
        for t in range(CY // T):
            ra = ra + r[i, tile(t)]
            sa = sa + s[i, tile(t)]
        return ra, sa

    zero = jnp.zeros((T, NZ), F32)
    ra, sa = lax.fori_loop(0, CX, add, (zero, zero))
    out = slab_sums(ra, 0) * (1.0 / CELLS) + slab_sums(sa, AGG)
    row[...] = jnp.broadcast_to(out, row.shape)


def kernel_pack_x(where, r, s, first, second, g, rown, sown, xfirst, xsecond, row, *, n_py):
    def sides(lo, hi):
        for k, (own, out) in enumerate(((r, rown), (s, sown))):
            out[:, :T] = lo[k]
            out[:, T : T + CY] = own[...]
            out[:, T + CY :] = hi[k]

    pl.when((where[1] & 1) == 0)(lambda: sides(second, first))
    pl.when((where[1] & 1) == 1)(lambda: sides(first, second))

    def faces(lo, hi):
        for k, own in enumerate((rown, sown)):
            lo[k] = own[:H]
            hi[k] = own[CX - H :]

    pl.when((where[0] & 1) == 0)(lambda: faces(xsecond, xfirst))
    pl.when((where[0] & 1) == 1)(lambda: faces(xfirst, xsecond))
    rows = g[...]
    for k in range(2):
        one = line_up(rows, k * AGG, n_py)
        row[:, k : k + 1, :] = jnp.broadcast_to(one[None], (row.shape[0], 1, row.shape[2]))


def smooth_last(rref, iref, zref, yref, n):
    def sweep(src, dst, i):
        for t, box, _ in neighbours(src, i, range(TILES)):
            dst[i, tile(t)] = (rref[i, tile(t)] + box) * iref[i, tile(t)]

    each(1, n - 1, lambda i: sweep(zref, yref, i))
    each(2, n - 2, lambda i: sweep(yref, zref, i))


def kernel_a(where, rown, sown, first, second, inverse, g1,
             rmid, smid, imid, v, u, row, rext, iext, zref, yref, *, n_px, n_py):
    a, b = where[0], where[1]
    y = iota((T, NZ), 0)

    def put(i, plane_of, inside):
        for t in range(TILES):
            rr, ss = plane_of(t)
            keep = inside
            if t == 0:
                keep = inside & (b > 0)
            if t == TILES - 1:
                keep = inside & (b < n_py - 1)
            inv = jnp.where(keep, 1.0 / (26.0 + ss), 0.0)
            rext[i, tile(t)] = rr
            iext[i, tile(t)] = inv
            zref[i, tile(t)] = rr * inv

    def mids(i, rr, ss):
        rmid[i - (H - V)] = rr
        smid[i - (H - V)] = ss

    def own(k):
        put(k + H, lambda t: (rown[k, tile(t)], sown[k, tile(t)]), a >= 0)
        mids(k + H, rown[k], sown[k])

    each(0, CX, own)

    def sides(lo, hi):
        each(0, H, lambda k: put(k, lambda t: (lo[0, k, tile(t)], lo[1, k, tile(t)]), a > 0))
        each(
            0, H,
            lambda k: put(
                k + H + CX, lambda t: (hi[0, k, tile(t)], hi[1, k, tile(t)]), a < n_px - 1
            ),
        )
        each(H - V, H, lambda k: mids(k, lo[0, k], lo[1, k]))
        each(0, V, lambda k: mids(k + H + CX, hi[0, k], hi[1, k]))

    pl.when((a & 1) == 0)(lambda: sides(second, first))
    pl.when((a & 1) == 1)(lambda: sides(first, second))
    smooth_last(rext, iext, zref, yref, XE)

    def apply(i, tiles):
        j = i - (H - V)
        for t, box, mid in neighbours(zref, i, tiles):
            v[j, tile(t)] = (26.0 + smid[j, tile(t)]) * mid - box
        imid[j] = iext[i]

    each(H - V, H, lambda i: apply(i, range(TILES)))
    each(H + CX, H + CX + V, lambda i: apply(i, range(TILES)))

    def apply_own(i, carry):
        ru, uv, av = carry
        j = i - (H - V)
        for t, box, mid in neighbours(zref, i, range(TILES)):
            vv = (26.0 + smid[j, tile(t)]) * mid - box
            v[j, tile(t)] = vv
            if 1 <= t < TILES - 1:
                u[i - H, tile(t - 1)] = mid
                ru = ru + fold(rext[i, tile(t)] * mid)
                uv = uv + fold(mid * vv)
                av = av + vv
        imid[j] = iext[i]
        return ru, uv, av

    zero = jnp.zeros((T, LANES), F32)
    ru, uv, av = lax.fori_loop(H, H + CX, apply_own, (zero, zero, jnp.zeros((T, NZ), F32)))
    m = g1[:, 0, :]
    lane = iota((1, LANES), 1)
    out = coarse_rows(inverse, m) + slab_sums(av, AGG) * (1.0 / CELLS)
    out = out + jnp.where(lane == 24, total(ru), 0.0) + jnp.where(lane == 25, total(uv), 0.0)
    row[...] = jnp.broadcast_to(out, row.shape)


def kernel_b(where, rmid, smid, imid, v, inverse, g1, g2,
             r1o, uo, vo, qo, row, scal, rref, qref, zref, yref, rows9, cref, *, n_px, n_py):
    g = g2[...]
    m, shifts = g1[:, 0, :], g1[:, 1, :]
    c = line_up(g, 0, n_py)
    w = line_up(g, AGG, n_py)
    lane = iota(g.shape, 1)
    tc = coarse_operator(c, shifts)
    rz = total(jnp.where(lane == 24, g, 0.0)) + CELLS * total(m * c)
    curv = total(jnp.where(lane == 25, g, 0.0)) + total(c * (2.0 * CELLS * w + tc))
    alpha = rz / curv
    e = w + tc * (1.0 / CELLS)
    mnew = m - alpha * e
    cnew = coarse_rows(inverse, mnew)
    planes, boxes = coarse_planes(where, g2, n_px, n_py, rows9)

    def image(i, pc, bc):
        for t in range(TILES):
            at = tile(t)
            q = v[i, at] + (27.0 + smid[i, at]) * pc[at] - bc[at]
            rr = rmid[i, at] - alpha * q
            qref[i, at] = q
            rref[i, at] = rr
            zref[i, at] = rr * imid[i, at]

    for i in (0, 1, 2, 3, XV - 4, XV - 3, XV - 2, XV - 1):
        block = 0 if i < V else 1 if i < V + CX else 2
        image(i, planes[block], box_plane(boxes, i - V))
    inner = 3.0 * boxes[1]
    each(V + 1, V + CX - 1, lambda i: image(i, planes[1], inner))
    smooth_last(rref, imid, zref, yref, XV)

    def apply(i, carry):
        ru, uv, uq, av = carry
        for t, box, uu in neighbours(zref, i, range(1, TILES - 1)):
            at, to = tile(t), tile(t - 1)
            vv = (26.0 + smid[i, at]) * uu - box
            rr, qq = rref[i, at], qref[i, at]
            uo[i - V, to] = uu
            vo[i - V, to] = vv
            r1o[i - V, to] = rr
            qo[i - V, to] = qq
            ru = ru + fold(rr * uu)
            uv = uv + fold(uu * vv)
            uq = uq + fold(uu * qq)
            av = av + vv
        return ru, uv, uq, av

    zero = jnp.zeros((T, LANES), F32)
    ru, uv, uq, av = lax.fori_loop(
        V, V + CX, apply, (zero, zero, zero, jnp.zeros((T, NZ), F32))
    )
    e_own = own_part(e, where, cref)
    m_own = own_part(mnew, where, cref)
    lane = iota((1, LANES), 1)
    out = cnew + slab_sums(av, AGG) * (1.0 / CELLS)
    out = out + jnp.where(lane == 24, total(ru) + CELLS * total(m_own * cnew), 0.0)
    out = out + jnp.where(lane == 25, total(uv), 0.0)
    out = out + jnp.where(lane == 26, total(uq) + CELLS * total(e_own * cnew), 0.0)
    row[...] = jnp.broadcast_to(out, row.shape)
    at = iota((8, LANES), 0)
    scal[...] = jnp.where(at == 0, rz, jnp.where(at == 1, curv, alpha))


def kernel_c(where, s, u, r1, un, vn, q, g1, g2, g3, scal, x, r2, rows9, *, n_px, n_py):
    g = g3[...]
    c = line_up(g, 0, n_py)
    w = line_up(g, AGG, n_py)
    lane = iota(g.shape, 1)
    tc = coarse_operator(c, g1[:, 1, :])
    rz, curv, alpha = scal[0:1, 0:1], scal[1:2, 0:1], scal[2:3, 0:1]
    rz1 = total(jnp.where(lane == 24, g, 0.0))
    zaz = total(jnp.where(lane == 25, g, 0.0)) + total(c * (2.0 * CELLS * w + tc))
    zq = total(jnp.where(lane == 26, g, 0.0))
    beta = rz1 / rz
    alpha2 = rz1 / (zaz + 2.0 * beta * zq + beta * beta * curv)
    first = alpha + alpha2 * beta
    planes, boxes = coarse_planes(where, g3, n_px, n_py, rows9)
    me = where[0] * n_py + where[1]
    c_old = spread(jnp.broadcast_to(g2[pl.ds(me, 1), :], (T, LANES)))
    rows = slice(T, T + CY)
    pc = planes[1][rows]
    base = first * c_old[0:1] + alpha2 * pc

    def finish(i, bc):
        for t in range(CY // T):
            at = tile(t)
            x[i, at] = first * u[i, at] + alpha2 * un[i, at] + base[at]
            image = vn[i, at] + (27.0 + s[i, at]) * pc[at] - bc[at] + beta * q[i, at]
            r2[i, at] = r1[i, at] - alpha2 * image

    for i in (0, CX - 1):
        finish(i, box_plane(boxes, i)[rows])
    inner = 3.0 * boxes[1][rows]
    each(1, CX - 1, lambda i: finish(i, inner))


VMEM = pl.BlockSpec(memory_space=pltpu.VMEM)
SMEM = pl.BlockSpec(memory_space=pltpu.SMEM)


def call(body, args, outs, scratch, name, **sizes):
    return pl.pallas_call(
        functools.partial(body, **sizes) if sizes else body,
        in_specs=[SMEM] + [VMEM] * (len(args) - 1),
        out_specs=[VMEM] * len(outs),
        out_shape=[jax.ShapeDtypeStruct(o, F32) for o in outs],
        scratch_shapes=[pltpu.VMEM(x, F32) for x in scratch],
        compiler_params=pltpu.CompilerParams(vmem_limit_bytes=32 * 1024 * 1024),
        name=name,
    )(*args)


def swap(x, axis, n, odd):
    pairs = [(i, i + 1) for i in range(odd, n - 1, 2)]
    return lax.ppermute(x, axis, pairs + [(j, i) for i, j in pairs])


def all_rows(x, axes):
    return lax.all_to_all(x, axes, 0, 0, tiled=True)


def per_device(right_side, shift, coarse_inverse, *, n_px, n_py):
    n = n_px * n_py
    width = n_py * AGG
    sizes = dict(n_px=n_px, n_py=n_py)
    where = jnp.stack([lax.axis_index("px"), lax.axis_index("py")]).astype(jnp.int32)
    face = (2, CX, T, NZ)
    first, second, row = call(
        kernel_pack_y, (where, right_side, shift), [face, face, (n_py, LANES)], [], "pack_y"
    )
    first = swap(first, "py", n_py, 0)
    second = swap(second, "py", n_py, 1)
    g = all_rows(row, "py")
    face = (2, H, YE, NZ)
    own = (CX, YE, NZ)
    rown, sown, first, second, row = call(
        kernel_pack_x, (where, right_side, shift, first, second, g),
        [own, own, face, face, (n_px, 2, width)], [], "pack_x", n_py=n_py,
    )
    first = swap(first, "px", n_px, 0)
    second = swap(second, "px", n_px, 1)
    g1 = all_rows(row, "px")
    rmid, smid, imid, v, u, row = call(
        kernel_a, (where, rown, sown, first, second, coarse_inverse, g1),
        [MID, MID, MID, MID, OWN, (n, LANES)], [EXT, EXT, EXT, EXT], "first", **sizes,
    )
    g2 = all_rows(row, ("px", "py"))
    r1, un, vn, q, row, scal = call(
        kernel_b, (where, rmid, smid, imid, v, coarse_inverse, g1, g2),
        [OWN, OWN, OWN, OWN, (n, LANES), (8, LANES)],
        [MID, MID, MID, MID, (16, LANES), (n_px, width)], "second", **sizes,
    )
    g3 = all_rows(row, ("px", "py"))
    return tuple(
        call(
            kernel_c, (where, shift, u, r1, un, vn, q, g1, g2, g3, scal),
            [OWN, OWN], [(16, LANES)], "third", **sizes,
        )
    )


def solution(mesh):
    placed = (P("px", "py", None), P("px", "py", None), P(("px", "py"), None))
    return jax.shard_map(
        functools.partial(per_device, n_px=mesh.shape["px"], n_py=mesh.shape["py"]),
        mesh=mesh,
        in_specs=placed,
        out_specs=(P("px", "py", None), P("px", "py", None)),
        check_vma=False,
    )
```

time: 527 us -> 114 us (0.22)
  blocking collectives: 395 us -> 76.1 us
  starting transfers between devices: 57.5 us -> 8.5 us
  waiting for transfers between devices: 33.8 us -> 0.01 us
  other arithmetic: 28.1 us -> 0.08 us
  Pallas kernels: 0 us -> 25.9 us
    psum x3 -> x0, blocking collectives: 235 us -> none  [the longest x2 157 us: inner_alignment(): return lax.psum(jnp.sum(first * second), ('px', 'py'))]
    unnamed x2 -> x0, blocking collectives: 160 us -> none
    all_to_all x0 -> x4, blocking collectives: none -> 76.1 us  [all_rows(): return lax.all_to_all(x, axes, 0, 0, tiled=True)]
    ppermute x24 -> x4, starting transfers between devices: 57.5 us -> 8.5 us  [swap(): return lax.ppermute(x, axis, pairs + [(j, i) for i, j in pairs])]
    ppermute x24 -> x4, waiting for transfers between devices: 33.8 us -> 0.01 us  [swap(): return lax.ppermute(x, axis, pairs + [(j, i) for i, j in pairs])]
    pallas_call x0 -> x5, Pallas kernels: none -> 25.9 us  [call(): pl.pallas_call(functools.partial(body, **sizes) if sizes else body, in_sp...]
    reduce_sum x7 -> x0, other arithmetic: 9.33 us -> none  [the longest x2 4.65 us: inner_curvature(): return lax.psum(jnp.sum(first * second), ('px', 'py'))]
    concatenate x6 -> x0, other arithmetic: 6.24 us -> none  [extended(): jnp.concatenate([lax.ppermute(tail, axis, [(i, (i + 1) % count) for i in...]
  transfers between devices with their start and end apart: 24 -> 4, of which waited for: 10 -> 0; matrix products, arithmetic and copies ran while one was open for 0% -> 0% of each run, Pallas kernels for 0% -> 0%
where the time goes in v2:
time: 114 us
  blocking collectives  76.1 us (67%)
  Pallas kernels  25.9 us (23%)
  starting transfers between devices  8.5 us (7%)
  local copies, waits for them, and re-layouts  2.46 us (2%)
    all_to_all x4, blocking collectives, all_rows(): return lax.all_to_all(x, axes, 0, 0, tiled=True)  76.1 us
    pallas_call x5, Pallas kernels, call(): pl.pallas_call(functools.partial(body, **sizes) if sizes else body, in_sp...  25.9 us
    ppermute x4, starting transfers between devices, swap(): return lax.ppermute(x, axis, pairs + [(j, i) for i, j in pairs])  8.5 us
    unnamed x8, local copies, waits for them, and re-layouts  2.46 us
  transfers between devices with their start and end apart: 4, of which 0 were waited for; matrix products, arithmetic and copies ran while one was open for 0% of the time, Pallas kernels for 0%

profile of v2, /device:TPU:1, one launch (start us, length us, event | category | flops | bytes accessed | tf_op | source)
XLA Modules:
  0.0 113.8 jit_solution(7870332860411299996)
XLA Ops:
  0.6 0.1 pad_add_fusion.where
  0.7 0.0 copy-start
  0.7 1.2 %copy-done = f32[16,32,512]{2,1,0:T(8,128)S(1)} copy-done((f32[16,32,512]{2,1,0:T(8,128)S(1)}, f32[16,32,512]{2,1,0:T(8,128)}, u32[]{:S(2)}) %copy-start) | copy-done | bytes 1048600
  1.9 0.0 copy-start.2
  1.9 1.2 %copy-done.2 = f32[16,32,512]{2,1,0:T(8,128)S(1)} copy-done((f32[16,32,512]{2,1,0:T(8,128)S(1)}, f32[16,32,512]{2,1,0:T(8,128)}, u32[]{:S(2)}) %copy-start.2) | copy-done | bytes 1048600
  3.2 1.1 pack_y.1
  4.3 2.1 %collective-permute-start = (f32[2,16,8,512]{3,2,1,0:T(8,128)S(1)}, f32[2,16,8,512]{3,2,1,0:T(8,128)S(1)}, u32[]{:S(2)}, u32[]{:S(2)}) collective-permute-start(f32[2,16,8,512]{3,2,1,0:T(8,128)S(1)} %get-tuple-element.22), channel_id=1, source_target_pairs={{0,1},{2,3},{4,5},{6,7},{8,9},{10,11},{12,13},{14,15},{1,0},{3,2},... | collective-permute-start | bytes 1572872 | tf_op jit(solution)/shard_map/ppermute | solution.py:456
  6.4 0.7 collective-permute-start.1
  7.1 18.0 %all_to_all.38 = f32[16,1,128]{2,1,0:T(1,128)S(1)} all-to-all(f32[16,1,128]{2,1,0:T(1,128)S(1)} %bitcast.20), channel_id=1, replica_groups=mesh['px'=16,'py'=16] {'py'}, dimensions={0} | all-to-all | bytes 16384 | tf_op jit(solution)/shard_map/all_to_all | solution.py:460
  25.1 0.0 collective-permute-done.first
  25.1 0.0 collective-permute-done.1.second
  25.1 0.0 copy-start.3
  25.1 1.1 pack_x.1
  26.2 2.2 %collective-permute-start.2 = (f32[2,6,48,512]{3,2,1,0:T(8,128)S(1)}, f32[2,6,48,512]{3,2,1,0:T(8,128)S(1)}, u32[]{:S(2)}, u32[]{:S(2)}) collective-permute-start(f32[2,6,48,512]{3,2,1,0:T(8,128)S(1)} %get-tuple-element.27), channel_id=1, source_target_pairs={{0,16},{32,48},{64,80},{96,112},{128,144},{160,176},{192,208},{224... | collective-permute-start | bytes 3538952 | tf_op jit(solution)/shard_map/ppermute | solution.py:456
  28.4 3.4 %collective-permute-start.3 = (f32[2,6,48,512]{3,2,1,0:T(8,128)S(1)}, f32[2,6,48,512]{3,2,1,0:T(8,128)S(1)}, u32[]{:S(2)}, u32[]{:S(2)}) collective-permute-start(f32[2,6,48,512]{3,2,1,0:T(8,128)S(1)} %get-tuple-element.28), channel_id=1, source_target_pairs={{16,32},{48,64},{80,96},{112,128},{144,160},{176,192},{208,224},{3... | collective-permute-start | bytes 3538952 | tf_op jit(solution)/shard_map/ppermute | solution.py:456
  31.9 19.8 %all_to_all.39.g1 = f32[16,2,128]{2,1,0:T(2,128)S(1)} all-to-all(f32[16,2,128]{2,1,0:T(2,128)S(1)} %get-tuple-element.29), channel_id=1, replica_groups=mesh['px'=16,'py'=16] {'px'}, dimensions={0} | all-to-all | bytes 32768 | tf_op jit(solution)/shard_map/all_to_all | solution.py:460
  51.7 0.0 collective-permute-done.2.first
  51.7 0.0 collective-permute-done.3.second
  51.7 0.0 copy-done.3
  51.7 11.2 %first.1 = (f32[22,48,512]{2,1,0:T(8,128)S(1)}, f32[22,48,512]{2,1,0:T(8,128)S(1)}, f32[22,48,512]{2,1,0:T(8,128)S(1)}, f32[22,48,512]{2,1,0:T(8,128)S(1)}, f32[...) custom-call(s32[2]{0:T(128)S(1)} %pad_add_fusion.where, f32[16,48,512]{2,1,0:T(8,128)S(1)} %get-tuple-element.25.rown, ...), custom_call_target="tpu_custom_call" | custom-call | tf_op jit(solution)/shard_map/first/pallas_call | solution.py:443
  62.8 19.9 %all_to_all.40 = f32[256,1,128]{2,1,0:T(1,128)S(1)} all-to-all(f32[256,1,128]{2,1,0:T(1,128)S(1)} %bitcast.17), channel_id=1, replica_groups=mesh['px'=16,'py'=16] {'px','py'}, dimensions={0} | all-to-all | bytes 262144 | tf_op jit(solution)/shard_map/all_to_all | solution.py:460
  82.7 0.0 copy-start.1
  82.8 9.4 %second.1 = (f32[16,32,512]{2,1,0:T(8,128)S(1)}, f32[16,32,512]{2,1,0:T(8,128)S(1)}, f32[16,32,512]{2,1,0:T(8,128)S(1)}, f32[16,32,512]{2,1,0:T(8,128)S(1)}, f32...) custom-call(s32[2]{0:T(128)S(1)} %pad_add_fusion.where, f32[22,48,512]{2,1,0:T(8,128)S(1)} %get-tuple-element.31.rmid, ...), custom_call_target="tpu_custom_call" | custom-call | tf_op jit(solution)/shard_map/second/pallas_call | solution.py:443
  92.1 18.4 %all_to_all.41 = f32[256,1,128]{2,1,0:T(1,128)S(1)} all-to-all(f32[256,1,128]{2,1,0:T(1,128)S(1)} %bitcast.18), channel_id=1, replica_groups=mesh['px'=16,'py'=16] {'px','py'}, dimensions={0} | all-to-all | bytes 262144 | tf_op jit(solution)/shard_map/all_to_all | solution.py:460
  110.6 0.0 copy-done.1
  110.6 3.2 %third.1 = (f32[16,32,512]{2,1,0:T(8,128)}, f32[16,32,512]{2,1,0:T(8,128)}) custom-call(s32[2]{0:T(128)S(1)} %pad_add_fusion.where, f32[16,32,512]{2,1,0:T(8,128)S(1)} %copy-done.1, f32[16,32,512]{2,1,0:T(8,128)S(1)} %get-tuple-element.30.u, f32[16,32,512]{2,1,0:T(8,128)S(1)} %get-tuple-element.36.r1, f32[16,32,512]{2,1,0:T(8,128)S(1)} %get-tuple-element.37.un, ...), custom_call_target="tpu_custom_call" | custom-call | tf_op jit(solution)/shard_map/third/pallas_call | solution.py:443
Async XLA Ops:
  0.7 1.2 %copy-start = (f32[16,32,512]{2,1,0:T(8,128)S(1)}, f32[16,32,512]{2,1,0:T(8,128)}, u32[]{:S(2)}) copy-start(f32[16,32,512]{2,1,0:T(8,128)} %s.5) | copy-start | bytes 3145732
  1.9 1.2 %copy-start.2 = (f32[16,32,512]{2,1,0:T(8,128)S(1)}, f32[16,32,512]{2,1,0:T(8,128)}, u32[]{:S(2)}) copy-start(f32[16,32,512]{2,1,0:T(8,128)} %r.3) | copy-start | bytes 3145732
  4.3 20.8 %collective-permute-start = (f32[2,16,8,512]{3,2,1,0:T(8,128)S(1)}, f32[2,16,8,512]{3,2,1,0:T(8,128)S(1)}, u32[]{:S(2)}, u32[]{:S(2)}) collective-permute-start(f32[2,16,8,512]{3,2,1,0:T(8,128)S(1)} %get-tuple-element.22), channel_id=1, source_target_pairs={{0,1},{2,3},{4,5},{6,7},{8,9},{10,11},{12,13},{14,15},{1,0},{3,2},... | collective-permute-start | bytes 1572872 | tf_op jit(solution)/shard_map/ppermute | solution.py:456
  6.4 18.7 %collective-permute-start.1 = (f32[2,16,8,512]{3,2,1,0:T(8,128)S(1)}, f32[2,16,8,512]{3,2,1,0:T(8,128)S(1)}, u32[]{:S(2)}, u32[]{:S(2)}) collective-permute-start(f32[2,16,8,512]{3,2,1,0:T(8,128)S(1)} %get-tuple-element.23), channel_id=1, source_target_pairs={{1,2},{3,4},{5,6},{7,8},{9,10},{11,12},{13,14},{2,1},{4,3},{6,5},{... | collective-permute-start | bytes 1572872 | tf_op jit(solution)/shard_map/ppermute | solution.py:456
  25.1 26.6 %copy-start.3 = (f32[8,2048]{1,0:T(8,128)S(1)}, f32[8,2048]{1,0:T(8,128)}, u32[]{:S(2)}) copy-start(f32[8,2048]{1,0:T(8,128)} %inverse.3) | copy-start | bytes 196612
  26.2 25.5 %collective-permute-start.2 = (f32[2,6,48,512]{3,2,1,0:T(8,128)S(1)}, f32[2,6,48,512]{3,2,1,0:T(8,128)S(1)}, u32[]{:S(2)}, u32[]{:S(2)}) collective-permute-start(f32[2,6,48,512]{3,2,1,0:T(8,128)S(1)} %get-tuple-element.27), channel_id=1, source_target_pairs={{0,16},{32,48},{64,80},{96,112},{128,144},{160,176},{192,208},{224... | collective-permute-start | bytes 3538952 | tf_op jit(solution)/shard_map/ppermute | solution.py:456
  28.4 23.2 %collective-permute-start.3 = (f32[2,6,48,512]{3,2,1,0:T(8,128)S(1)}, f32[2,6,48,512]{3,2,1,0:T(8,128)S(1)}, u32[]{:S(2)}, u32[]{:S(2)}) collective-permute-start(f32[2,6,48,512]{3,2,1,0:T(8,128)S(1)} %get-tuple-element.28), channel_id=1, source_target_pairs={{16,32},{48,64},{80,96},{112,128},{144,160},{176,192},{208,224},{3... | collective-permute-start | bytes 3538952 | tf_op jit(solution)/shard_map/ppermute | solution.py:456
  82.7 27.8 %copy-start.1 = (f32[16,32,512]{2,1,0:T(8,128)S(1)}, f32[16,32,512]{2,1,0:T(8,128)}, u32[]{:S(2)}) copy-start(f32[16,32,512]{2,1,0:T(8,128)} %s.5) | copy-start | bytes 3145732

commit v3 on v2

--- a/solution.py
+++ b/solution.py
@@ -19,6 +19,8 @@
 YE = CY + 2 * T
 TILES = YE // T
 LANES = 128
+UNROLL = 8
+PARTS = 4
 F32 = jnp.float32
 HIGH = lax.Precision.HIGHEST
 OWN = (CX, CY, NZ)
@@ -87,8 +89,12 @@
     return jnp.concatenate(parts, axis=0)
 
 
-def each(low, high, body):
-    lax.fori_loop(low, high, lambda i, carry: (body(i), carry)[1], 0)
+def each(low, high, body, unroll=UNROLL):
+    def step(i, carry):
+        body(i)
+        return carry
+
+    lax.fori_loop(low, high, step, 0, unroll=unroll)
 
 
 def total(x):
@@ -203,134 +209,159 @@
     return 3.0 * hi
 
 
-def kernel_pack_y(where, r, s, first, second, row):
-    def copy(out, rows):
-        out[0] = r[:, rows, :]
-        out[1] = s[:, rows, :]
-
-    @pl.when((where[1] & 1) == 0)
-    def _():
-        copy(first, slice(CY - T, CY))
-        copy(second, slice(0, T))
-
-    @pl.when((where[1] & 1) == 1)
-    def _():
-        copy(first, slice(0, T))
-        copy(second, slice(CY - T, CY))
-
-    def add(i, carry):
-        ra, sa = carry
-        for t in range(CY // T):
-            ra = ra + r[i, tile(t)]
-            sa = sa + s[i, tile(t)]
-        return ra, sa
-
-    zero = jnp.zeros((T, NZ), F32)
-    ra, sa = lax.fori_loop(0, CX, add, (zero, zero))
-    out = slab_sums(ra, 0) * (1.0 / CELLS) + slab_sums(sa, AGG)
+class Field:
+    def __init__(self, own, halo, width):
+        self.own, self.halo, self.width = own, halo, width
+
+    def __call__(self, i, t):
+        outer = (self.halo.shape[0] - 2 * self.width) // 2
+        if isinstance(i, int) and i < self.width:
+            return self.halo[i + outer, tile(t)]
+        if isinstance(i, int) and i >= self.width + CX:
+            return self.halo[i + outer - CX, tile(t)]
+        return self.own[i - self.width, tile(t)]
+
+
+def over(low, high, width, body):
+    for i in range(low, width):
+        body(i)
+    each(width, width + CX, body)
+    for i in range(width + CX, high):
+        body(i)
+
+
+def kernel_pack_y(where, r_in, s_in, r, s, first, second, row, sems):
+    size = CX // PARTS
+    copies = [
+        [
+            pltpu.make_async_copy(
+                src.at[pl.ds(k * size, size)], dst.at[pl.ds(k * size, size)], sems.at[f, k]
+            )
+            for k in range(PARTS)
+        ]
+        for f, (src, dst) in enumerate(((r_in, r), (s_in, s)))
+    ]
+    for group in copies:
+        for copy in group:
+            copy.start()
+    even = (where[1] & 1) == 0
+    sums = []
+    for f, own in enumerate((r, s)):
+        acc = jnp.zeros((T, NZ), F32)
+        for k in range(PARTS):
+            copies[f][k].wait()
+            for i in range(k * size, (k + 1) * size):
+                lo, hi = own[i, tile(0)], own[i, tile(CY // T - 1)]
+                first[f, i] = jnp.where(even, hi, lo)
+                second[f, i] = jnp.where(even, lo, hi)
+                for t in range(CY // T):
+                    acc = acc + own[i, tile(t)]
+        sums.append(acc)
+    out = slab_sums(sums[0], 0) * (1.0 / CELLS) + slab_sums(sums[1], AGG)
     row[...] = jnp.broadcast_to(out, row.shape)
 
 
 def kernel_pack_x(where, r, s, first, second, g, rown, sown, xfirst, xsecond, row, *, n_py):
-    def sides(lo, hi):
+    even = (where[1] & 1) == 0
+    for i in range(CX):
         for k, (own, out) in enumerate(((r, rown), (s, sown))):
-            out[:, :T] = lo[k]
-            out[:, T : T + CY] = own[...]
-            out[:, T + CY :] = hi[k]
-
-    pl.when((where[1] & 1) == 0)(lambda: sides(second, first))
-    pl.when((where[1] & 1) == 1)(lambda: sides(first, second))
-
-    def faces(lo, hi):
-        for k, own in enumerate((rown, sown)):
-            lo[k] = own[:H]
-            hi[k] = own[CX - H :]
-
-    pl.when((where[0] & 1) == 0)(lambda: faces(xsecond, xfirst))
-    pl.when((where[0] & 1) == 1)(lambda: faces(xfirst, xsecond))
+            out[i, tile(0)] = jnp.where(even, second[k, i], first[k, i])
+            out[i, tile(TILES - 1)] = jnp.where(even, first[k, i], second[k, i])
+            for t in range(CY // T):
+                out[i, tile(t + 1)] = own[i, tile(t)]
+    even = (where[0] & 1) == 0
+
+    def put(at, t, lo, hi):
+        xfirst[at, tile(t)] = jnp.where(even, hi, lo)
+        xsecond[at, tile(t)] = jnp.where(even, lo, hi)
+
+    for t in range(TILES):
+        for k in range(H - 1):
+            put(k, t, rown[k, tile(t)], rown[CX - 1 - k, tile(t)])
+            put(H - 1 + k, t, sown[k, tile(t)], sown[CX - 1 - k, tile(t)])
+        lo, hi = (
+            rown[i, tile(t)] / (26.0 + sown[i, tile(t)]) for i in (H - 1, CX - H)
+        )
+        put(2 * H - 2, t, lo, hi)
     rows = g[...]
     for k in range(2):
         one = line_up(rows, k * AGG, n_py)
         row[:, k : k + 1, :] = jnp.broadcast_to(one[None], (row.shape[0], 1, row.shape[2]))
 
 
-def smooth_last(rref, iref, zref, yref, n):
-    def sweep(src, dst, i):
-        for t, box, _ in neighbours(src, i, range(TILES)):
-            dst[i, tile(t)] = (rref[i, tile(t)] + box) * iref[i, tile(t)]
-
-    each(1, n - 1, lambda i: sweep(zref, yref, i))
-    each(2, n - 2, lambda i: sweep(yref, zref, i))
+def smooth_last(r, iref, zref, yref, n, width):
+    def sweep(src, dst):
+        def body(i):
+            for t, box, _ in neighbours(src, i, range(TILES)):
+                dst[i, tile(t)] = (r(i, t) + box) * iref[i, tile(t)]
+
+        return body
+
+    over(1, n - 1, width, sweep(zref, yref))
+    over(2, n - 2, width, sweep(yref, zref))
 
 
 def kernel_a(where, rown, sown, first, second, inverse, g1,
-             rmid, smid, imid, v, u, row, rext, iext, zref, yref, *, n_px, n_py):
+             rhalo, shalo, iext, v, zref, row, yref, *, n_px, n_py):
     a, b = where[0], where[1]
-    y = iota((T, NZ), 0)
-
-    def put(i, plane_of, inside):
+    even = (a & 1) == 0
+
+    def invert(i, t, ss, inside):
+        keep = inside
+        if t == 0:
+            keep = inside & (b > 0)
+        if t == TILES - 1:
+            keep = inside & (b < n_py - 1)
+        inv = jnp.where(keep, 1.0 / (26.0 + ss), 0.0)
+        iext[i, tile(t)] = inv
+        return inv
+
+    def own(i):
         for t in range(TILES):
-            rr, ss = plane_of(t)
-            keep = inside
-            if t == 0:
-                keep = inside & (b > 0)
-            if t == TILES - 1:
-                keep = inside & (b < n_py - 1)
-            inv = jnp.where(keep, 1.0 / (26.0 + ss), 0.0)
-            rext[i, tile(t)] = rr
-            iext[i, tile(t)] = inv
-            zref[i, tile(t)] = rr * inv
-
-    def mids(i, rr, ss):
-        rmid[i - (H - V)] = rr
-        smid[i - (H - V)] = ss
-
-    def own(k):
-        put(k + H, lambda t: (rown[k, tile(t)], sown[k, tile(t)]), a >= 0)
-        mids(k + H, rown[k], sown[k])
-
-    each(0, CX, own)
-
-    def sides(lo, hi):
-        each(0, H, lambda k: put(k, lambda t: (lo[0, k, tile(t)], lo[1, k, tile(t)]), a > 0))
-        each(
-            0, H,
-            lambda k: put(
-                k + H + CX, lambda t: (hi[0, k, tile(t)], hi[1, k, tile(t)]), a < n_px - 1
-            ),
-        )
-        each(H - V, H, lambda k: mids(k, lo[0, k], lo[1, k]))
-        each(0, V, lambda k: mids(k + H + CX, hi[0, k], hi[1, k]))
-
-    pl.when((a & 1) == 0)(lambda: sides(second, first))
-    pl.when((a & 1) == 1)(lambda: sides(first, second))
-    smooth_last(rext, iext, zref, yref, XE)
-
-    def apply(i, tiles):
-        j = i - (H - V)
-        for t, box, mid in neighbours(zref, i, tiles):
-            v[j, tile(t)] = (26.0 + smid[j, tile(t)]) * mid - box
-        imid[j] = iext[i]
-
-    each(H - V, H, lambda i: apply(i, range(TILES)))
-    each(H + CX, H + CX + V, lambda i: apply(i, range(TILES)))
+            zref[i, tile(t)] = rown[i - H, tile(t)] * invert(i, t, sown[i - H, tile(t)], a >= 0)
+
+    each(H, H + CX, own)
+    for t in range(TILES):
+        at = tile(t)
+
+        def got(k):
+            x, y = first[k, at], second[k, at]
+            return jnp.where(even, y, x), jnp.where(even, x, y)
+
+        for k in range(H - 1):
+            for i, rr, ss, inside in zip(
+                (H - 1 - k, H + CX + k), got(k), got(H - 1 + k), (a > 0, a < n_px - 1)
+            ):
+                at_halo = i if i < H else i - CX
+                rhalo[at_halo, at] = rr
+                shalo[at_halo, at] = ss
+                zref[i, at] = rr * invert(i, t, ss, inside)
+        zref[0, at], zref[XE - 1, at] = got(2 * H - 2)
+    r, s = Field(rown, rhalo, H), Field(sown, shalo, H)
+    smooth_last(r, iext, zref, yref, XE, H)
+
+    def apply(i):
+        for t, box, mid in neighbours(zref, i, range(TILES)):
+            v[i - (H - V), tile(t)] = (26.0 + s(i, t)) * mid - box
+
+    for i in (*range(H - V, H), *range(H + CX, H + CX + V)):
+        apply(i)
 
     def apply_own(i, carry):
         ru, uv, av = carry
-        j = i - (H - V)
         for t, box, mid in neighbours(zref, i, range(TILES)):
-            vv = (26.0 + smid[j, tile(t)]) * mid - box
-            v[j, tile(t)] = vv
+            vv = (26.0 + s(i, t)) * mid - box
+            v[i - (H - V), tile(t)] = vv
             if 1 <= t < TILES - 1:
-                u[i - H, tile(t - 1)] = mid
-                ru = ru + fold(rext[i, tile(t)] * mid)
+                ru = ru + fold(r(i, t) * mid)
                 uv = uv + fold(mid * vv)
                 av = av + vv
-        imid[j] = iext[i]
         return ru, uv, av
 
     zero = jnp.zeros((T, LANES), F32)
-    ru, uv, av = lax.fori_loop(H, H + CX, apply_own, (zero, zero, jnp.zeros((T, NZ), F32)))
+    ru, uv, av = lax.fori_loop(
+        H, H + CX, apply_own, (zero, zero, jnp.zeros((T, NZ), F32)), unroll=UNROLL
+    )
     m = g1[:, 0, :]
     lane = iota((1, LANES), 1)
     out = coarse_rows(inverse, m) + slab_sums(av, AGG) * (1.0 / CELLS)
@@ -338,8 +369,8 @@
     row[...] = jnp.broadcast_to(out, row.shape)
 
 
-def kernel_b(where, rmid, smid, imid, v, inverse, g1, g2,
-             r1o, uo, vo, qo, row, scal, rref, qref, zref, yref, rows9, cref, *, n_px, n_py):
+def kernel_b(where, rown, sown, rhalo, shalo, iext, v, inverse, g1, g2,
+             rref, qref, zref, vo, row, scal, iref, yref, rows9, cref, *, n_px, n_py):
     g = g2[...]
     m, shifts = g1[:, 0, :], g1[:, 1, :]
     c = line_up(g, 0, n_py)
@@ -353,42 +384,41 @@
     mnew = m - alpha * e
     cnew = coarse_rows(inverse, mnew)
     planes, boxes = coarse_planes(where, g2, n_px, n_py, rows9)
+    r, s = Field(rown, rhalo, V), Field(sown, shalo, V)
 
     def image(i, pc, bc):
         for t in range(TILES):
             at = tile(t)
-            q = v[i, at] + (27.0 + smid[i, at]) * pc[at] - bc[at]
-            rr = rmid[i, at] - alpha * q
+            q = v[i, at] + (27.0 + s(i, t)) * pc[at] - bc[at]
+            rr = r(i, t) - alpha * q
+            inv = iext[i + (H - V), at]
             qref[i, at] = q
             rref[i, at] = rr
-            zref[i, at] = rr * imid[i, at]
+            zref[i, at] = rr * inv
+            iref[i, at] = inv
 
     for i in (0, 1, 2, 3, XV - 4, XV - 3, XV - 2, XV - 1):
         block = 0 if i < V else 1 if i < V + CX else 2
         image(i, planes[block], box_plane(boxes, i - V))
     inner = 3.0 * boxes[1]
-    each(V + 1, V + CX - 1, lambda i: image(i, planes[1], inner))
-    smooth_last(rref, imid, zref, yref, XV)
+    each(V + 1, V + CX - 1, lambda i: image(i, planes[1], inner), unroll=2)
+    smooth_last(lambda i, t: rref[i, tile(t)], iref, zref, yref, XV, V)
 
     def apply(i, carry):
         ru, uv, uq, av = carry
         for t, box, uu in neighbours(zref, i, range(1, TILES - 1)):
-            at, to = tile(t), tile(t - 1)
-            vv = (26.0 + smid[i, at]) * uu - box
-            rr, qq = rref[i, at], qref[i, at]
-            uo[i - V, to] = uu
-            vo[i - V, to] = vv
-            r1o[i - V, to] = rr
-            qo[i - V, to] = qq
-            ru = ru + fold(rr * uu)
+            at = tile(t)
+            vv = (26.0 + s(i, t)) * uu - box
+            vo[i - V, tile(t - 1)] = vv
+            ru = ru + fold(rref[i, at] * uu)
             uv = uv + fold(uu * vv)
-            uq = uq + fold(uu * qq)
+            uq = uq + fold(uu * qref[i, at])
             av = av + vv
         return ru, uv, uq, av
 
     zero = jnp.zeros((T, LANES), F32)
     ru, uv, uq, av = lax.fori_loop(
-        V, V + CX, apply, (zero, zero, zero, jnp.zeros((T, NZ), F32))
+        V, V + CX, apply, (zero, zero, zero, jnp.zeros((T, NZ), F32)), unroll=UNROLL
     )
     e_own = own_part(e, where, cref)
     m_own = own_part(mnew, where, cref)
@@ -402,7 +432,8 @@
     scal[...] = jnp.where(at == 0, rz, jnp.where(at == 1, curv, alpha))
 
 
-def kernel_c(where, s, u, r1, un, vn, q, g1, g2, g3, scal, x, r2, rows9, *, n_px, n_py):
+def kernel_c(where, sown, u, r1, un, vn, q, g1, g2, g3, scal, x_out, r_out,
+             x, r2, rows9, sems, *, n_px, n_py):
     g = g3[...]
     c = line_up(g, 0, n_py)
     w = line_up(g, AGG, n_py)
@@ -418,34 +449,41 @@
     planes, boxes = coarse_planes(where, g3, n_px, n_py, rows9)
     me = where[0] * n_py + where[1]
     c_old = spread(jnp.broadcast_to(g2[pl.ds(me, 1), :], (T, LANES)))
-    rows = slice(T, T + CY)
-    pc = planes[1][rows]
-    base = first * c_old[0:1] + alpha2 * pc
-
-    def finish(i, bc):
+    pc = planes[1][T : 2 * T]
+    base = first * c_old + alpha2 * pc
+    size = CX // PARTS
+    copies = []
+    for i in range(CX):
+        bc = box_plane(boxes, i)
         for t in range(CY // T):
-            at = tile(t)
-            x[i, at] = first * u[i, at] + alpha2 * un[i, at] + base[at]
-            image = vn[i, at] + (27.0 + s[i, at]) * pc[at] - bc[at] + beta * q[i, at]
-            r2[i, at] = r1[i, at] - alpha2 * image
-
-    for i in (0, CX - 1):
-        finish(i, box_plane(boxes, i)[rows])
-    inner = 3.0 * boxes[1][rows]
-    each(1, CX - 1, lambda i: finish(i, inner))
+            to, at = tile(t), tile(t + 1)
+            x[i, to] = first * u[i + H, at] + alpha2 * un[i + V, at] + base
+            image = vn[i, to] + (27.0 + sown[i, at]) * pc - bc[at] + beta * q[i + V, at]
+            r2[i, to] = r1[i + V, at] - alpha2 * image
+        if (i + 1) % size == 0:
+            k = i // size
+            for f, (src, dst) in enumerate(((x, x_out), (r2, r_out))):
+                part = pl.ds(k * size, size)
+                copies.append(
+                    pltpu.make_async_copy(src.at[part], dst.at[part], sems.at[f, k])
+                )
+                copies[-1].start()
+    for copy in copies:
+        copy.wait()
 
 
 VMEM = pl.BlockSpec(memory_space=pltpu.VMEM)
 SMEM = pl.BlockSpec(memory_space=pltpu.SMEM)
-
-
-def call(body, args, outs, scratch, name, **sizes):
+ANY = pl.BlockSpec(memory_space=pl.ANY)
+
+
+def call(body, args, outs, scratch, name, in_specs=None, out_specs=None, **sizes):
     return pl.pallas_call(
         functools.partial(body, **sizes) if sizes else body,
-        in_specs=[SMEM] + [VMEM] * (len(args) - 1),
-        out_specs=[VMEM] * len(outs),
+        in_specs=in_specs or [SMEM] + [VMEM] * (len(args) - 1),
+        out_specs=out_specs or [VMEM] * len(outs),
         out_shape=[jax.ShapeDtypeStruct(o, F32) for o in outs],
-        scratch_shapes=[pltpu.VMEM(x, F32) for x in scratch],
+        scratch_shapes=[pltpu.VMEM(x, F32) if isinstance(x, tuple) else x for x in scratch],
         compiler_params=pltpu.CompilerParams(vmem_limit_bytes=32 * 1024 * 1024),
         name=name,
     )(*args)
@@ -464,38 +502,42 @@
     n = n_px * n_py
     width = n_py * AGG
     sizes = dict(n_px=n_px, n_py=n_py)
+    copies = pltpu.SemaphoreType.DMA((2, PARTS))
     where = jnp.stack([lax.axis_index("px"), lax.axis_index("py")]).astype(jnp.int32)
     face = (2, CX, T, NZ)
-    first, second, row = call(
-        kernel_pack_y, (where, right_side, shift), [face, face, (n_py, LANES)], [], "pack_y"
+    r, s, first, second, row = call(
+        kernel_pack_y, (where, right_side, shift), [OWN, OWN, face, face, (n_py, LANES)],
+        [copies], "pack_y", in_specs=[SMEM, ANY, ANY],
     )
     first = swap(first, "py", n_py, 0)
     second = swap(second, "py", n_py, 1)
     g = all_rows(row, "py")
-    face = (2, H, YE, NZ)
+    face = (2 * H - 1, YE, NZ)
     own = (CX, YE, NZ)
     rown, sown, first, second, row = call(
-        kernel_pack_x, (where, right_side, shift, first, second, g),
+        kernel_pack_x, (where, r, s, first, second, g),
         [own, own, face, face, (n_px, 2, width)], [], "pack_x", n_py=n_py,
     )
     first = swap(first, "px", n_px, 0)
     second = swap(second, "px", n_px, 1)
     g1 = all_rows(row, "px")
-    rmid, smid, imid, v, u, row = call(
+    halo = (2 * H, YE, NZ)
+    rhalo, shalo, iext, v, u, row = call(
         kernel_a, (where, rown, sown, first, second, coarse_inverse, g1),
-        [MID, MID, MID, MID, OWN, (n, LANES)], [EXT, EXT, EXT, EXT], "first", **sizes,
+        [halo, halo, EXT, MID, EXT, (n, LANES)], [EXT], "first", **sizes,
     )
     g2 = all_rows(row, ("px", "py"))
-    r1, un, vn, q, row, scal = call(
-        kernel_b, (where, rmid, smid, imid, v, coarse_inverse, g1, g2),
-        [OWN, OWN, OWN, OWN, (n, LANES), (8, LANES)],
-        [MID, MID, MID, MID, (16, LANES), (n_px, width)], "second", **sizes,
+    r1, q, un, vn, row, scal = call(
+        kernel_b, (where, rown, sown, rhalo, shalo, iext, v, coarse_inverse, g1, g2),
+        [MID, MID, MID, OWN, (n, LANES), (8, LANES)],
+        [MID, MID, (16, LANES), (n_px, width)], "second", **sizes,
     )
     g3 = all_rows(row, ("px", "py"))
     return tuple(
         call(
-            kernel_c, (where, shift, u, r1, un, vn, q, g1, g2, g3, scal),
-            [OWN, OWN], [(16, LANES)], "third", **sizes,
+            kernel_c, (where, sown, u, r1, un, vn, q, g1, g2, g3, scal),
+            [OWN, OWN], [OWN, OWN, (16, LANES), copies], "third",
+            out_specs=[ANY, ANY], **sizes,
         )
     )
 

time: 114 us -> 105 us (0.921)
  Pallas kernels: 25.9 us -> 17.4 us
    pallas_call x5, Pallas kernels: 25.9 us -> 17.4 us  [call(): pl.pallas_call(functools.partial(body, **sizes) if sizes else body, in_sp...]
    unnamed x8 -> x6, local copies, waits for them, and re-layouts: 2.46 us -> 2.45 us
where the time goes in v3:
time: 105 us
  blocking collectives  75.2 us (72%)
  Pallas kernels  17.4 us (17%)
  starting transfers between devices  8.5 us (8%)
  local copies, waits for them, and re-layouts  2.45 us (2%)
    all_to_all x4, blocking collectives, all_rows(): return lax.all_to_all(x, axes, 0, 0, tiled=True)  75.2 us
    pallas_call x5, Pallas kernels, call(): pl.pallas_call(functools.partial(body, **sizes) if sizes else body, in_sp...  17.4 us
    ppermute x4, starting transfers between devices, swap(): return lax.ppermute(x, axis, pairs + [(j, i) for i, j in pairs])  8.5 us
    unnamed x6, local copies, waits for them, and re-layouts  2.45 us
  transfers between devices with their start and end apart: 4, of which 0 were waited for; matrix products, arithmetic and copies ran while one was open for 0% of the time, Pallas kernels for 0%

profile of v3, /device:TPU:1, one launch (start us, length us, event | category | flops | bytes accessed | tf_op | source)
XLA Modules:
  0.0 104.6 jit_solution(6049217262813355611)
XLA Ops:
  0.6 0.1 pad_add_fusion.where
  0.7 0.0 copy-start
  0.7 1.2 %copy-done = f32[16,32,512]{2,1,0:T(8,128)S(1)} copy-done((f32[16,32,512]{2,1,0:T(8,128)S(1)}, f32[16,32,512]{2,1,0:T(8,128)}, u32[]{:S(2)}) %copy-start) | copy-done | bytes 1048600
  1.9 0.0 copy-start.1
  1.9 1.2 %copy-done.1 = f32[16,32,512]{2,1,0:T(8,128)S(1)} copy-done((f32[16,32,512]{2,1,0:T(8,128)S(1)}, f32[16,32,512]{2,1,0:T(8,128)}, u32[]{:S(2)}) %copy-start.1) | copy-done | bytes 1048600
  3.2 1.3 %pack_y.1 = (f32[16,32,512]{2,1,0:T(8,128)S(1)}, f32[16,32,512]{2,1,0:T(8,128)S(1)}, f32[2,16,8,512]{3,2,1,0:T(8,128)S(1)}, f32[2,16,8,512]{3,2,1,0:T(8,128)S(1)}, f32[16,128]{1,0:T(8,128)S(1)}) custom-call(s32[2]{0:T(128)S(1)} %pad_add_fusion.where, f32[16,32,512]{2,1,0:T(8,128)S(1)} %copy-done, f32[16,32,512]{2,1,0:T(8,128)S(1)} %copy-done.1), custom_call_target="tpu_custom_call" | custom-call | tf_op jit(solution)/shard_map/pack_y/pallas_call | solution.py:481
  4.5 2.1 %collective-permute-start = (f32[2,16,8,512]{3,2,1,0:T(8,128)S(1)}, f32[2,16,8,512]{3,2,1,0:T(8,128)S(1)}, u32[]{:S(2)}, u32[]{:S(2)}) collective-permute-start(f32[2,16,8,512]{3,2,1,0:T(8,128)S(1)} %get-tuple-element.26), channel_id=1, source_target_pairs={{0,1},{2,3},{4,5},{6,7},{8,9},{10,11},{12,13},{14,15},{1,0},{3,2},... | collective-permute-start | bytes 1572872 | tf_op jit(solution)/shard_map/ppermute | solution.py:494
  6.6 0.7 collective-permute-start.1
  7.3 18.0 %all_to_all.38 = f32[16,1,128]{2,1,0:T(1,128)S(1)} all-to-all(f32[16,1,128]{2,1,0:T(1,128)S(1)} %bitcast.20), channel_id=1, replica_groups=mesh['px'=16,'py'=16] {'py'}, dimensions={0} | all-to-all | bytes 16384 | tf_op jit(solution)/shard_map/all_to_all | solution.py:498
  25.3 0.0 collective-permute-done.first
  25.3 0.0 collective-permute-done.1.second
  25.3 0.0 copy-start.2
  25.3 1.0 pack_x.1
  26.3 2.2 %collective-permute-start.2 = (f32[11,48,512]{2,1,0:T(8,128)S(1)}, f32[11,48,512]{2,1,0:T(8,128)S(1)}, u32[]{:S(2)}, u32[]{:S(2)}) collective-permute-start(f32[11,48,512]{2,1,0:T(8,128)S(1)} %get-tuple-element.31), channel_id=1, source_target_pairs={{0,16},{32,48},{64,80},{96,112},{128,144},{160,176},{192,208},{224... | collective-permute-start | bytes 3244040 | tf_op jit(solution)/shard_map/ppermute | solution.py:494
  28.6 3.4 %collective-permute-start.3 = (f32[11,48,512]{2,1,0:T(8,128)S(1)}, f32[11,48,512]{2,1,0:T(8,128)S(1)}, u32[]{:S(2)}, u32[]{:S(2)}) collective-permute-start(f32[11,48,512]{2,1,0:T(8,128)S(1)} %get-tuple-element.32), channel_id=1, source_target_pairs={{16,32},{48,64},{80,96},{112,128},{144,160},{176,192},{208,224},{3... | collective-permute-start | bytes 3244040 | tf_op jit(solution)/shard_map/ppermute | solution.py:494
  32.0 18.7 %all_to_all.39.g1 = f32[16,2,128]{2,1,0:T(2,128)S(1)} all-to-all(f32[16,2,128]{2,1,0:T(2,128)S(1)} %get-tuple-element.33), channel_id=1, replica_groups=mesh['px'=16,'py'=16] {'px'}, dimensions={0} | all-to-all | bytes 32768 | tf_op jit(solution)/shard_map/all_to_all | solution.py:498
  50.8 0.0 collective-permute-done.2.first
  50.8 0.0 collective-permute-done.3.second
  50.8 0.0 copy-done.2
  50.8 6.2 %first.1 = (f32[12,48,512]{2,1,0:T(8,128)S(1)}, f32[12,48,512]{2,1,0:T(8,128)S(1)}, f32[28,48,512]{2,1,0:T(8,128)S(1)}, f32[22,48,512]{2,1,0:T(8,128)S(1)}, f32[...) custom-call(s32[2]{0:T(128)S(1)} %pad_add_fusion.where, f32[16,48,512]{2,1,0:T(8,128)S(1)} %get-tuple-element.30.rown, ...), custom_call_target="tpu_custom_call" | custom-call | tf_op jit(solution)/shard_map/first/pallas_call | solution.py:481
  57.0 19.9 %all_to_all.40 = f32[256,1,128]{2,1,0:T(1,128)S(1)} all-to-all(f32[256,1,128]{2,1,0:T(1,128)S(1)} %bitcast.18), channel_id=1, replica_groups=mesh['px'=16,'py'=16] {'px','py'}, dimensions={0} | all-to-all | bytes 262144 | tf_op jit(solution)/shard_map/all_to_all | solution.py:498
  76.9 6.0 %second.1 = (f32[22,48,512]{2,1,0:T(8,128)S(1)}, f32[22,48,512]{2,1,0:T(8,128)S(1)}, f32[22,48,512]{2,1,0:T(8,128)S(1)}, f32[16,32,512]{2,1,0:T(8,128)S(1)}, f32...) custom-call(s32[2]{0:T(128)S(1)} %pad_add_fusion.where, f32[16,48,512]{2,1,0:T(8,128)S(1)} %get-tuple-element.30.rown, ...), custom_call_target="tpu_custom_call" | custom-call | tf_op jit(solution)/shard_map/second/pallas_call | solution.py:481
  82.9 18.6 %all_to_all.41 = f32[256,1,128]{2,1,0:T(1,128)S(1)} all-to-all(f32[256,1,128]{2,1,0:T(1,128)S(1)} %bitcast.17), channel_id=1, replica_groups=mesh['px'=16,'py'=16] {'px','py'}, dimensions={0} | all-to-all | bytes 262144 | tf_op jit(solution)/shard_map/all_to_all | solution.py:498
  101.5 2.9 %third.1 = (f32[16,32,512]{2,1,0:T(8,128)}, f32[16,32,512]{2,1,0:T(8,128)}) custom-call(s32[2]{0:T(128)S(1)} %pad_add_fusion.where, f32[16,48,512]{2,1,0:T(8,128)S(1)} %get-tuple-element.29.sown, f32[28,48,512]{2,1,0:T(8,128)S(1)} %get-tuple-element.34.u, f32[22,48,512]{2,1,0:T(8,128)S(1)} %get-tuple-element.40.r1, f32[22,48,512]{2,1,0:T(8,128)S(1)} %get-tuple-element.41.un, ...), custom_call_target="tpu_custom_call" | custom-call | tf_op jit(solution)/shard_map/third/pallas_call | solution.py:481
Async XLA Ops:
  0.7 1.2 %copy-start = (f32[16,32,512]{2,1,0:T(8,128)S(1)}, f32[16,32,512]{2,1,0:T(8,128)}, u32[]{:S(2)}) copy-start(f32[16,32,512]{2,1,0:T(8,128)} %r_in.1) | copy-start | bytes 3145732
  1.9 1.2 %copy-start.1 = (f32[16,32,512]{2,1,0:T(8,128)S(1)}, f32[16,32,512]{2,1,0:T(8,128)}, u32[]{:S(2)}) copy-start(f32[16,32,512]{2,1,0:T(8,128)} %s_in.1) | copy-start | bytes 3145732
  4.5 20.8 %collective-permute-start = (f32[2,16,8,512]{3,2,1,0:T(8,128)S(1)}, f32[2,16,8,512]{3,2,1,0:T(8,128)S(1)}, u32[]{:S(2)}, u32[]{:S(2)}) collective-permute-start(f32[2,16,8,512]{3,2,1,0:T(8,128)S(1)} %get-tuple-element.26), channel_id=1, source_target_pairs={{0,1},{2,3},{4,5},{6,7},{8,9},{10,11},{12,13},{14,15},{1,0},{3,2},... | collective-permute-start | bytes 1572872 | tf_op jit(solution)/shard_map/ppermute | solution.py:494
  6.6 18.7 %collective-permute-start.1 = (f32[2,16,8,512]{3,2,1,0:T(8,128)S(1)}, f32[2,16,8,512]{3,2,1,0:T(8,128)S(1)}, u32[]{:S(2)}, u32[]{:S(2)}) collective-permute-start(f32[2,16,8,512]{3,2,1,0:T(8,128)S(1)} %get-tuple-element.27), channel_id=1, source_target_pairs={{1,2},{3,4},{5,6},{7,8},{9,10},{11,12},{13,14},{2,1},{4,3},{6,5},{... | collective-permute-start | bytes 1572872 | tf_op jit(solution)/shard_map/ppermute | solution.py:494
  25.3 25.5 %copy-start.2 = (f32[8,2048]{1,0:T(8,128)S(1)}, f32[8,2048]{1,0:T(8,128)}, u32[]{:S(2)}) copy-start(f32[8,2048]{1,0:T(8,128)} %inverse.3) | copy-start | bytes 196612
  26.3 24.4 %collective-permute-start.2 = (f32[11,48,512]{2,1,0:T(8,128)S(1)}, f32[11,48,512]{2,1,0:T(8,128)S(1)}, u32[]{:S(2)}, u32[]{:S(2)}) collective-permute-start(f32[11,48,512]{2,1,0:T(8,128)S(1)} %get-tuple-element.31), channel_id=1, source_target_pairs={{0,16},{32,48},{64,80},{96,112},{128,144},{160,176},{192,208},{224... | collective-permute-start | bytes 3244040 | tf_op jit(solution)/shard_map/ppermute | solution.py:494
  28.6 22.2 %collective-permute-start.3 = (f32[11,48,512]{2,1,0:T(8,128)S(1)}, f32[11,48,512]{2,1,0:T(8,128)S(1)}, u32[]{:S(2)}, u32[]{:S(2)}) collective-permute-start(f32[11,48,512]{2,1,0:T(8,128)S(1)} %get-tuple-element.32), channel_id=1, source_target_pairs={{16,32},{48,64},{80,96},{112,128},{144,160},{176,192},{208,224},{3... | collective-permute-start | bytes 3244040 | tf_op jit(solution)/shard_map/ppermute | solution.py:494

commit v4 on v3

--- a/solution.py
+++ b/solution.py
@@ -11,11 +11,10 @@
 AGG = 8
 SLAB = NZ // AGG
 CELLS = CX * CY * SLAB
-H = 6
-V = 3
+H = 3
 T = 8
+HY = 6
 XE = CX + 2 * H
-XV = CX + 2 * V
 YE = CY + 2 * T
 TILES = YE // T
 LANES = 128
@@ -25,7 +24,7 @@
 HIGH = lax.Precision.HIGHEST
 OWN = (CX, CY, NZ)
 EXT = (XE, YE, NZ)
-MID = (XV, YE, NZ)
+TALL = (CX, YE, NZ)
 
 
 def tile(t):
@@ -210,24 +209,48 @@
 
 
 class Field:
-    def __init__(self, own, halo, width):
-        self.own, self.halo, self.width = own, halo, width
+    def __init__(self, own, halo):
+        self.own, self.halo = own, halo
 
     def __call__(self, i, t):
-        outer = (self.halo.shape[0] - 2 * self.width) // 2
-        if isinstance(i, int) and i < self.width:
-            return self.halo[i + outer, tile(t)]
-        if isinstance(i, int) and i >= self.width + CX:
-            return self.halo[i + outer - CX, tile(t)]
-        return self.own[i - self.width, tile(t)]
-
-
-def over(low, high, width, body):
-    for i in range(low, width):
+        if isinstance(i, int) and i < H:
+            return self.halo[i, tile(t)]
+        if isinstance(i, int) and i >= H + CX:
+            return self.halo[i - CX, tile(t)]
+        return self.own[i - H, tile(t)]
+
+
+def over(low, high, body):
+    for i in range(low, H):
         body(i)
-    each(width, width + CX, body)
-    for i in range(width + CX, high):
+    each(H, H + CX, body)
+    for i in range(H + CX, high):
         body(i)
+
+
+def shifted(rows, k):
+    return pltpu.roll(rows, k % T, axis=0) if k % T else rows
+
+
+def squeeze(pieces, o):
+    row = iota((T, NZ), 0)
+    a, b, c, d = pieces
+    return (
+        jnp.where(row < 6, shifted(a, -o), shifted(b, 6 - o)),
+        jnp.where(row < 4, shifted(b, -o - 2), shifted(c, 4 - o)),
+        jnp.where(row < 2, shifted(c, -o - 4), shifted(d, 2 - o)),
+    )
+
+
+def unsqueeze(tiles, o):
+    row = iota((T, NZ), 0)
+    a, b, c = tiles
+    return (
+        shifted(a, o),
+        jnp.where(row < o + 2, shifted(a, o - 6), shifted(b, o + 2)),
+        jnp.where(row < o + 4, shifted(b, o - 4), shifted(c, o + 4)),
+        shifted(c, o - 2),
+    )
 
 
 def kernel_pack_y(where, r_in, s_in, r, s, first, second, row, sems):
@@ -250,10 +273,14 @@
         acc = jnp.zeros((T, NZ), F32)
         for k in range(PARTS):
             copies[f][k].wait()
-            for i in range(k * size, (k + 1) * size):
-                lo, hi = own[i, tile(0)], own[i, tile(CY // T - 1)]
-                first[f, i] = jnp.where(even, hi, lo)
-                second[f, i] = jnp.where(even, lo, hi)
+            planes = range(k * size, (k + 1) * size)
+            los = squeeze([own[i, tile(0)] for i in planes], 0)
+            his = squeeze([own[i, tile(CY // T - 1)] for i in planes], T - HY)
+            for j, (lo, hi) in enumerate(zip(los, his)):
+                at = tile((f * PARTS + k) * 3 + j)
+                first[at] = jnp.where(even, hi, lo)
+                second[at] = jnp.where(even, lo, hi)
+            for i in planes:
                 for t in range(CY // T):
                     acc = acc + own[i, tile(t)]
         sums.append(acc)
@@ -263,33 +290,31 @@
 
 def kernel_pack_x(where, r, s, first, second, g, rown, sown, xfirst, xsecond, row, *, n_py):
     even = (where[1] & 1) == 0
-    for i in range(CX):
-        for k, (own, out) in enumerate(((r, rown), (s, sown))):
-            out[i, tile(0)] = jnp.where(even, second[k, i], first[k, i])
-            out[i, tile(TILES - 1)] = jnp.where(even, first[k, i], second[k, i])
-            for t in range(CY // T):
-                out[i, tile(t + 1)] = own[i, tile(t)]
+    for f, (own, out) in enumerate(((r, rown), (s, sown))):
+        for k in range(PARTS):
+            ats = [tile((f * PARTS + k) * 3 + j) for j in range(3)]
+            los = unsqueeze([jnp.where(even, second[at], first[at]) for at in ats], T - HY)
+            his = unsqueeze([jnp.where(even, first[at], second[at]) for at in ats], 0)
+            for j, (lo, hi) in enumerate(zip(los, his)):
+                i = k * (CX // PARTS) + j
+                out[i, tile(0)] = lo
+                out[i, tile(TILES - 1)] = hi
+                for t in range(CY // T):
+                    out[i, tile(t + 1)] = own[i, tile(t)]
     even = (where[0] & 1) == 0
-
-    def put(at, t, lo, hi):
-        xfirst[at, tile(t)] = jnp.where(even, hi, lo)
-        xsecond[at, tile(t)] = jnp.where(even, lo, hi)
-
-    for t in range(TILES):
-        for k in range(H - 1):
-            put(k, t, rown[k, tile(t)], rown[CX - 1 - k, tile(t)])
-            put(H - 1 + k, t, sown[k, tile(t)], sown[CX - 1 - k, tile(t)])
-        lo, hi = (
-            rown[i, tile(t)] / (26.0 + sown[i, tile(t)]) for i in (H - 1, CX - H)
-        )
-        put(2 * H - 2, t, lo, hi)
+    for k in range(H):
+        for at, own in ((k, rown), (H + k, sown)):
+            for t in range(TILES):
+                lo, hi = own[k, tile(t)], own[CX - 1 - k, tile(t)]
+                xfirst[at, tile(t)] = jnp.where(even, hi, lo)
+                xsecond[at, tile(t)] = jnp.where(even, lo, hi)
     rows = g[...]
     for k in range(2):
         one = line_up(rows, k * AGG, n_py)
         row[:, k : k + 1, :] = jnp.broadcast_to(one[None], (row.shape[0], 1, row.shape[2]))
 
 
-def smooth_last(r, iref, zref, yref, n, width):
+def smooth_last(r, iref, zref, yref):
     def sweep(src, dst):
         def body(i):
             for t, box, _ in neighbours(src, i, range(TILES)):
@@ -297,61 +322,54 @@
 
         return body
 
-    over(1, n - 1, width, sweep(zref, yref))
-    over(2, n - 2, width, sweep(yref, zref))
+    over(1, XE - 1, sweep(zref, yref))
+    over(2, XE - 2, sweep(yref, zref))
 
 
 def kernel_a(where, rown, sown, first, second, inverse, g1,
-             rhalo, shalo, iext, v, zref, row, yref, *, n_px, n_py):
+             rhalo, shalo, iext, v, zref, vfirst, vsecond, row, yref, *, n_px, n_py):
     a, b = where[0], where[1]
     even = (a & 1) == 0
-
-    def invert(i, t, ss, inside):
+    y = iota((T, NZ), 0)
+
+    def start(i, t, rr, ss, inside):
         keep = inside
         if t == 0:
-            keep = inside & (b > 0)
+            keep = inside & (b > 0) & (y >= T - HY)
         if t == TILES - 1:
-            keep = inside & (b < n_py - 1)
+            keep = inside & (b < n_py - 1) & (y < HY)
         inv = jnp.where(keep, 1.0 / (26.0 + ss), 0.0)
         iext[i, tile(t)] = inv
-        return inv
+        zref[i, tile(t)] = rr * inv
 
     def own(i):
         for t in range(TILES):
-            zref[i, tile(t)] = rown[i - H, tile(t)] * invert(i, t, sown[i - H, tile(t)], a >= 0)
+            start(i, t, rown[i - H, tile(t)], sown[i - H, tile(t)], a >= 0)
 
     each(H, H + CX, own)
     for t in range(TILES):
         at = tile(t)
 
         def got(k):
-            x, y = first[k, at], second[k, at]
-            return jnp.where(even, y, x), jnp.where(even, x, y)
-
-        for k in range(H - 1):
+            x, z = first[k, at], second[k, at]
+            return jnp.where(even, z, x), jnp.where(even, x, z)
+
+        for k in range(H):
             for i, rr, ss, inside in zip(
-                (H - 1 - k, H + CX + k), got(k), got(H - 1 + k), (a > 0, a < n_px - 1)
+                (H - 1 - k, H + CX + k), got(k), got(H + k), (a > 0, a < n_px - 1)
             ):
                 at_halo = i if i < H else i - CX
                 rhalo[at_halo, at] = rr
                 shalo[at_halo, at] = ss
-                zref[i, at] = rr * invert(i, t, ss, inside)
-        zref[0, at], zref[XE - 1, at] = got(2 * H - 2)
-    r, s = Field(rown, rhalo, H), Field(sown, shalo, H)
-    smooth_last(r, iext, zref, yref, XE, H)
-
-    def apply(i):
-        for t, box, mid in neighbours(zref, i, range(TILES)):
-            v[i - (H - V), tile(t)] = (26.0 + s(i, t)) * mid - box
-
-    for i in (*range(H - V, H), *range(H + CX, H + CX + V)):
-        apply(i)
-
-    def apply_own(i, carry):
+                start(i, t, rr, ss, inside)
+    r, s = Field(rown, rhalo), Field(sown, shalo)
+    smooth_last(r, iext, zref, yref)
+
+    def apply(i, carry):
         ru, uv, av = carry
         for t, box, mid in neighbours(zref, i, range(TILES)):
             vv = (26.0 + s(i, t)) * mid - box
-            v[i - (H - V), tile(t)] = vv
+            v[i - H, tile(t)] = vv
             if 1 <= t < TILES - 1:
                 ru = ru + fold(r(i, t) * mid)
                 uv = uv + fold(mid * vv)
@@ -360,8 +378,13 @@
 
     zero = jnp.zeros((T, LANES), F32)
     ru, uv, av = lax.fori_loop(
-        H, H + CX, apply_own, (zero, zero, jnp.zeros((T, NZ), F32)), unroll=UNROLL
-    )
+        H, H + CX, apply, (zero, zero, jnp.zeros((T, NZ), F32)), unroll=UNROLL
+    )
+    for k in range(H):
+        for t in range(TILES):
+            lo, hi = v[k, tile(t)], v[CX - 1 - k, tile(t)]
+            vfirst[k, tile(t)] = jnp.where(even, hi, lo)
+            vsecond[k, tile(t)] = jnp.where(even, lo, hi)
     m = g1[:, 0, :]
     lane = iota((1, LANES), 1)
     out = coarse_rows(inverse, m) + slab_sums(av, AGG) * (1.0 / CELLS)
@@ -369,8 +392,8 @@
     row[...] = jnp.broadcast_to(out, row.shape)
 
 
-def kernel_b(where, rown, sown, rhalo, shalo, iext, v, inverse, g1, g2,
-             rref, qref, zref, vo, row, scal, iref, yref, rows9, cref, *, n_px, n_py):
+def kernel_b(where, rown, sown, rhalo, shalo, iext, vown, vfirst, vsecond, inverse, g1, g2,
+             rref, qref, zref, vo, row, scal, yref, rows9, cref, *, n_px, n_py):
     g = g2[...]
     m, shifts = g1[:, 0, :], g1[:, 1, :]
     c = line_up(g, 0, n_py)
@@ -384,32 +407,38 @@
     mnew = m - alpha * e
     cnew = coarse_rows(inverse, mnew)
     planes, boxes = coarse_planes(where, g2, n_px, n_py, rows9)
-    r, s = Field(rown, rhalo, V), Field(sown, shalo, V)
+    r, s = Field(rown, rhalo), Field(sown, shalo)
+    even = (where[0] & 1) == 0
+
+    def v(i, t):
+        if isinstance(i, int) and not H <= i < H + CX:
+            k = H - 1 - i if i < H else i - H - CX
+            x, z = vfirst[k, tile(t)], vsecond[k, tile(t)]
+            return jnp.where(even, z, x) if i < H else jnp.where(even, x, z)
+        return vown[i - H, tile(t)]
 
     def image(i, pc, bc):
         for t in range(TILES):
             at = tile(t)
-            q = v[i, at] + (27.0 + s(i, t)) * pc[at] - bc[at]
+            q = v(i, t) + (27.0 + s(i, t)) * pc[at] - bc[at]
             rr = r(i, t) - alpha * q
-            inv = iext[i + (H - V), at]
             qref[i, at] = q
             rref[i, at] = rr
-            zref[i, at] = rr * inv
-            iref[i, at] = inv
-
-    for i in (0, 1, 2, 3, XV - 4, XV - 3, XV - 2, XV - 1):
-        block = 0 if i < V else 1 if i < V + CX else 2
-        image(i, planes[block], box_plane(boxes, i - V))
+            zref[i, at] = rr * iext[i, at]
+
+    for i in (*range(H + 1), *range(H + CX - 1, XE)):
+        block = 0 if i < H else 1 if i < H + CX else 2
+        image(i, planes[block], box_plane(boxes, i - H))
     inner = 3.0 * boxes[1]
-    each(V + 1, V + CX - 1, lambda i: image(i, planes[1], inner), unroll=2)
-    smooth_last(lambda i, t: rref[i, tile(t)], iref, zref, yref, XV, V)
+    each(H + 1, H + CX - 1, lambda i: image(i, planes[1], inner), unroll=2)
+    smooth_last(lambda i, t: rref[i, tile(t)], iext, zref, yref)
 
     def apply(i, carry):
         ru, uv, uq, av = carry
         for t, box, uu in neighbours(zref, i, range(1, TILES - 1)):
             at = tile(t)
             vv = (26.0 + s(i, t)) * uu - box
-            vo[i - V, tile(t - 1)] = vv
+            vo[i - H, tile(t - 1)] = vv
             ru = ru + fold(rref[i, at] * uu)
             uv = uv + fold(uu * vv)
             uq = uq + fold(uu * qref[i, at])
@@ -418,7 +447,7 @@
 
     zero = jnp.zeros((T, LANES), F32)
     ru, uv, uq, av = lax.fori_loop(
-        V, V + CX, apply, (zero, zero, zero, jnp.zeros((T, NZ), F32)), unroll=UNROLL
+        H, H + CX, apply, (zero, zero, zero, jnp.zeros((T, NZ), F32)), unroll=UNROLL
     )
     e_own = own_part(e, where, cref)
     m_own = own_part(mnew, where, cref)
@@ -457,9 +486,9 @@
         bc = box_plane(boxes, i)
         for t in range(CY // T):
             to, at = tile(t), tile(t + 1)
-            x[i, to] = first * u[i + H, at] + alpha2 * un[i + V, at] + base
-            image = vn[i, to] + (27.0 + sown[i, at]) * pc - bc[at] + beta * q[i + V, at]
-            r2[i, to] = r1[i + V, at] - alpha2 * image
+            x[i, to] = first * u[i + H, at] + alpha2 * un[i + H, at] + base
+            image = vn[i, to] + (27.0 + sown[i, at]) * pc - bc[at] + beta * q[i + H, at]
+            r2[i, to] = r1[i + H, at] - alpha2 * image
         if (i + 1) % size == 0:
             k = i // size
             for f, (src, dst) in enumerate(((x, x_out), (r2, r_out))):
@@ -474,7 +503,7 @@
 
 VMEM = pl.BlockSpec(memory_space=pltpu.VMEM)
 SMEM = pl.BlockSpec(memory_space=pltpu.SMEM)
-ANY = pl.BlockSpec(memory_space=pl.ANY)
+HBM = pl.BlockSpec(memory_space=pltpu.HBM)
 
 
 def call(body, args, outs, scratch, name, in_specs=None, out_specs=None, **sizes):
@@ -504,40 +533,44 @@
     sizes = dict(n_px=n_px, n_py=n_py)
     copies = pltpu.SemaphoreType.DMA((2, PARTS))
     where = jnp.stack([lax.axis_index("px"), lax.axis_index("py")]).astype(jnp.int32)
-    face = (2, CX, T, NZ)
+    inputs = [pltpu.with_memory_space_constraint(f, pltpu.HBM) for f in (right_side, shift)]
+    face = (2 * CX * HY, NZ)
     r, s, first, second, row = call(
-        kernel_pack_y, (where, right_side, shift), [OWN, OWN, face, face, (n_py, LANES)],
-        [copies], "pack_y", in_specs=[SMEM, ANY, ANY],
+        kernel_pack_y, (where, *inputs), [OWN, OWN, face, face, (n_py, LANES)],
+        [copies], "pack_y", in_specs=[SMEM, HBM, HBM],
     )
     first = swap(first, "py", n_py, 0)
     second = swap(second, "py", n_py, 1)
     g = all_rows(row, "py")
-    face = (2 * H - 1, YE, NZ)
-    own = (CX, YE, NZ)
+    face = (2 * H, YE, NZ)
     rown, sown, first, second, row = call(
         kernel_pack_x, (where, r, s, first, second, g),
-        [own, own, face, face, (n_px, 2, width)], [], "pack_x", n_py=n_py,
+        [TALL, TALL, face, face, (n_px, 2, width)], [], "pack_x", n_py=n_py,
     )
     first = swap(first, "px", n_px, 0)
     second = swap(second, "px", n_px, 1)
     g1 = all_rows(row, "px")
     halo = (2 * H, YE, NZ)
-    rhalo, shalo, iext, v, u, row = call(
+    face = (H, YE, NZ)
+    rhalo, shalo, iext, v, u, first, second, row = call(
         kernel_a, (where, rown, sown, first, second, coarse_inverse, g1),
-        [halo, halo, EXT, MID, EXT, (n, LANES)], [EXT], "first", **sizes,
-    )
+        [halo, halo, EXT, TALL, EXT, face, face, (n, LANES)], [EXT], "first", **sizes,
+    )
+    first = swap(first, "px", n_px, 0)
+    second = swap(second, "px", n_px, 1)
     g2 = all_rows(row, ("px", "py"))
     r1, q, un, vn, row, scal = call(
-        kernel_b, (where, rown, sown, rhalo, shalo, iext, v, coarse_inverse, g1, g2),
-        [MID, MID, MID, OWN, (n, LANES), (8, LANES)],
-        [MID, MID, (16, LANES), (n_px, width)], "second", **sizes,
+        kernel_b,
+        (where, rown, sown, rhalo, shalo, iext, v, first, second, coarse_inverse, g1, g2),
+        [EXT, EXT, EXT, OWN, (n, LANES), (8, LANES)],
+        [EXT, (16, LANES), (n_px, width)], "second", **sizes,
     )
     g3 = all_rows(row, ("px", "py"))
     return tuple(
         call(
             kernel_c, (where, sown, u, r1, un, vn, q, g1, g2, g3, scal),
             [OWN, OWN], [OWN, OWN, (16, LANES), copies], "third",
-            out_specs=[ANY, ANY], **sizes,
+            out_specs=[HBM, HBM], **sizes,
         )
     )
 

time: 105 us -> 98.9 us (0.942)
  blocking collectives: 75.2 us -> 68.9 us
  starting transfers between devices: 8.5 us -> 11.4 us
  local copies, waits for them, and re-layouts: 2.45 us -> 0.01 us
    all_to_all x4, blocking collectives: 75.2 us -> 68.9 us  [all_rows(): return lax.all_to_all(x, axes, 0, 0, tiled=True)]
    ppermute x4 -> x6, starting transfers between devices: 8.5 us -> 11.4 us  [swap(): return lax.ppermute(x, axis, pairs + [(j, i) for i, j in pairs])]
    unnamed x6 -> x2, local copies, waits for them, and re-layouts: 2.45 us -> 0.01 us
  transfers between devices with their start and end apart: 4 -> 6, of which waited for: 0 -> 0; matrix products, arithmetic and copies ran while one was open for 0% -> 0% of each run, Pallas kernels for 0% -> 0%
where the time goes in v4:
time: 98.9 us; the launch traced here: 98.6 us
  blocking collectives  68.9 us (70%)
  Pallas kernels  17.6 us (18%)
  starting transfers between devices  11.4 us (12%)
    all_to_all x4, blocking collectives, all_rows(): return lax.all_to_all(x, axes, 0, 0, tiled=True)  68.9 us
    pallas_call x5, Pallas kernels, call(): pl.pallas_call(functools.partial(body, **sizes) if sizes else body, in_sp...  17.6 us
    ppermute x6, starting transfers between devices, swap(): return lax.ppermute(x, axis, pairs + [(j, i) for i, j in pairs])  11.4 us
  transfers between devices with their start and end apart: 6, of which 0 were waited for; matrix products, arithmetic and copies ran while one was open for 0% of the time, Pallas kernels for 0%

profile of v4, /device:TPU:1, one launch (start us, length us, event | category | flops | bytes accessed | tf_op | source)
XLA Modules:
  0.0 98.6 jit_solution(3122616024385124771)
XLA Ops:
  0.6 0.1 pad_add_fusion.where
  0.7 0.0 copy-start
  0.7 2.5 %pack_y.1 = (f32[16,32,512]{2,1,0:T(8,128)S(1)}, f32[16,32,512]{2,1,0:T(8,128)S(1)}, f32[192,512]{1,0:T(8,128)S(1)}, f32[192,512]{1,0:T(8,128)S(1)}, f32[16,128]{1,0:T(8,128)S(1)}) custom-call(s32[2]{0:T(128)S(1)} %pad_add_fusion.where, f32[16,32,512]{2,1,0:T(8,128)} %r_in.1, f32[16,32,512]{2,1,0:T(8,128)} %s_in.1), custom_call_target="tpu_custom_call" | custom-call | tf_op jit(solution)/shard_map/pack_y/pallas_call | solution.py:510
  3.2 2.1 %collective-permute-start = (f32[192,512]{1,0:T(8,128)S(1)}, f32[192,512]{1,0:T(8,128)S(1)}, u32[]{:S(2)}, u32[]{:S(2)}) collective-permute-start(f32[192,512]{1,0:T(8,128)S(1)} %get-tuple-element.28), channel_id=1, source_target_pairs={{0,1},{2,3},{4,5},{6,7},{8,9},{10,11},{12,13},{14,15},{1,0},{3,2},... | collective-permute-start | bytes 1179656 | tf_op jit(solution)/shard_map/ppermute | solution.py:523
  5.4 0.7 collective-permute-start.1
  6.0 15.2 %all_to_all.38 = f32[16,1,128]{2,1,0:T(1,128)S(1)} all-to-all(f32[16,1,128]{2,1,0:T(1,128)S(1)} %bitcast.20), channel_id=1, replica_groups=mesh['px'=16,'py'=16] {'py'}, dimensions={0} | all-to-all | bytes 16384 | tf_op jit(solution)/shard_map/all_to_all | solution.py:527
  21.2 0.0 collective-permute-done.first
  21.2 0.0 collective-permute-done.1.second
  21.2 1.0 pack_x.1
  22.2 2.4 %collective-permute-start.2 = (f32[6,48,512]{2,1,0:T(8,128)S(1)}, f32[6,48,512]{2,1,0:T(8,128)S(1)}, u32[]{:S(2)}, u32[]{:S(2)}) collective-permute-start(f32[6,48,512]{2,1,0:T(8,128)S(1)} %get-tuple-element.33), channel_id=1, source_target_pairs={{0,16},{32,48},{64,80},{96,112},{128,144},{160,176},{192,208},{224... | collective-permute-start | bytes 1769480 | tf_op jit(solution)/shard_map/ppermute | solution.py:523
  24.6 3.4 %collective-permute-start.3 = (f32[6,48,512]{2,1,0:T(8,128)S(1)}, f32[6,48,512]{2,1,0:T(8,128)S(1)}, u32[]{:S(2)}, u32[]{:S(2)}) collective-permute-start(f32[6,48,512]{2,1,0:T(8,128)S(1)} %get-tuple-element.34), channel_id=1, source_target_pairs={{16,32},{48,64},{80,96},{112,128},{144,160},{176,192},{208,224},{3... | collective-permute-start | bytes 1769480 | tf_op jit(solution)/shard_map/ppermute | solution.py:523
  28.1 14.8 %all_to_all.39.g1 = f32[16,2,128]{2,1,0:T(2,128)S(1)} all-to-all(f32[16,2,128]{2,1,0:T(2,128)S(1)} %get-tuple-element.35), channel_id=1, replica_groups=mesh['px'=16,'py'=16] {'px'}, dimensions={0} | all-to-all | bytes 32768 | tf_op jit(solution)/shard_map/all_to_all | solution.py:527
  42.9 0.0 collective-permute-done.2.first
  42.9 0.0 collective-permute-done.3.second
  42.9 0.0 copy-done
  42.9 5.1 %first.1 = (f32[6,48,512]{2,1,0:T(8,128)S(1)}, f32[6,48,512]{2,1,0:T(8,128)S(1)}, f32[22,48,512]{2,1,0:T(8,128)S(1)}, f32[16,48,512]{2,1,0:T(8,128)S(1)}, f32[22...) custom-call(s32[2]{0:T(128)S(1)} %pad_add_fusion.where, ...), custom_call_target="tpu_custom_call" | custom-call | tf_op jit(solution)/shard_map/first/pallas_call | solution.py:510
  48.0 0.5 collective-permute-start.4
  48.5 2.2 %collective-permute-start.5 = (f32[3,48,512]{2,1,0:T(8,128)S(1)}, f32[3,48,512]{2,1,0:T(8,128)S(1)}, u32[]{:S(2)}, u32[]{:S(2)}) collective-permute-start(f32[3,48,512]{2,1,0:T(8,128)S(1)} %get-tuple-element.42), channel_id=1, source_target_pairs={{16,32},{48,64},{80,96},{112,128},{144,160},{176,192},{208,224},{3... | collective-permute-start | bytes 884744 | tf_op jit(solution)/shard_map/ppermute | solution.py:523
  50.7 20.5 %all_to_all.40 = f32[256,1,128]{2,1,0:T(1,128)S(1)} all-to-all(f32[256,1,128]{2,1,0:T(1,128)S(1)} %bitcast.17), channel_id=1, replica_groups=mesh['px'=16,'py'=16] {'px','py'}, dimensions={0} | all-to-all | bytes 262144 | tf_op jit(solution)/shard_map/all_to_all | solution.py:527
  71.2 0.0 collective-permute-done.4.vfirst
  71.2 0.0 collective-permute-done.5.vsecond
  71.2 6.1 %second.1 = (f32[22,48,512]{2,1,0:T(8,128)S(1)}, f32[22,48,512]{2,1,0:T(8,128)S(1)}, f32[22,48,512]{2,1,0:T(8,128)S(1)}, f32[16,32,512]{2,1,0:T(8,128)S(1)}, f32...) custom-call(s32[2]{0:T(128)S(1)} %pad_add_fusion.where, f32[16,48,512]{2,1,0:T(8,128)S(1)} %get-tuple-element.32.rown, ...), custom_call_target="tpu_custom_call" | custom-call | tf_op jit(solution)/shard_map/second/pallas_call | solution.py:510
  77.3 18.4 %all_to_all.41 = f32[256,1,128]{2,1,0:T(1,128)S(1)} all-to-all(f32[256,1,128]{2,1,0:T(1,128)S(1)} %bitcast.18), channel_id=1, replica_groups=mesh['px'=16,'py'=16] {'px','py'}, dimensions={0} | all-to-all | bytes 262144 | tf_op jit(solution)/shard_map/all_to_all | solution.py:527
  95.8 2.9 %third.1 = (f32[16,32,512]{2,1,0:T(8,128)}, f32[16,32,512]{2,1,0:T(8,128)}) custom-call(s32[2]{0:T(128)S(1)} %pad_add_fusion.where, f32[16,48,512]{2,1,0:T(8,128)S(1)} %get-tuple-element.31.sown, f32[22,48,512]{2,1,0:T(8,128)S(1)} %get-tuple-element.36.u, f32[22,48,512]{2,1,0:T(8,128)S(1)} %get-tuple-element.44.r1, f32[22,48,512]{2,1,0:T(8,128)S(1)} %get-tuple-element.45.un, ...), custom_call_target="tpu_custom_call" | custom-call | tf_op jit(solution)/shard_map/third/pallas_call | solution.py:510
Async XLA Ops:
  0.7 42.2 %copy-start = (f32[8,2048]{1,0:T(8,128)S(1)}, f32[8,2048]{1,0:T(8,128)}, u32[]{:S(2)}) copy-start(f32[8,2048]{1,0:T(8,128)} %inverse.3) | copy-start | bytes 196612
  3.2 18.0 %collective-permute-start = (f32[192,512]{1,0:T(8,128)S(1)}, f32[192,512]{1,0:T(8,128)S(1)}, u32[]{:S(2)}, u32[]{:S(2)}) collective-permute-start(f32[192,512]{1,0:T(8,128)S(1)} %get-tuple-element.28), channel_id=1, source_target_pairs={{0,1},{2,3},{4,5},{6,7},{8,9},{10,11},{12,13},{14,15},{1,0},{3,2},... | collective-permute-start | bytes 1179656 | tf_op jit(solution)/shard_map/ppermute | solution.py:523
  5.4 15.9 %collective-permute-start.1 = (f32[192,512]{1,0:T(8,128)S(1)}, f32[192,512]{1,0:T(8,128)S(1)}, u32[]{:S(2)}, u32[]{:S(2)}) collective-permute-start(f32[192,512]{1,0:T(8,128)S(1)} %get-tuple-element.29), channel_id=1, source_target_pairs={{1,2},{3,4},{5,6},{7,8},{9,10},{11,12},{13,14},{2,1},{4,3},{6,5},{... | collective-permute-start | bytes 1179656 | tf_op jit(solution)/shard_map/ppermute | solution.py:523
  22.2 20.7 %collective-permute-start.2 = (f32[6,48,512]{2,1,0:T(8,128)S(1)}, f32[6,48,512]{2,1,0:T(8,128)S(1)}, u32[]{:S(2)}, u32[]{:S(2)}) collective-permute-start(f32[6,48,512]{2,1,0:T(8,128)S(1)} %get-tuple-element.33), channel_id=1, source_target_pairs={{0,16},{32,48},{64,80},{96,112},{128,144},{160,176},{192,208},{224... | collective-permute-start | bytes 1769480 | tf_op jit(solution)/shard_map/ppermute | solution.py:523
  24.6 18.3 %collective-permute-start.3 = (f32[6,48,512]{2,1,0:T(8,128)S(1)}, f32[6,48,512]{2,1,0:T(8,128)S(1)}, u32[]{:S(2)}, u32[]{:S(2)}) collective-permute-start(f32[6,48,512]{2,1,0:T(8,128)S(1)} %get-tuple-element.34), channel_id=1, source_target_pairs={{16,32},{48,64},{80,96},{112,128},{144,160},{176,192},{208,224},{3... | collective-permute-start | bytes 1769480 | tf_op jit(solution)/shard_map/ppermute | solution.py:523
  48.0 23.2 %collective-permute-start.4 = (f32[3,48,512]{2,1,0:T(8,128)S(1)}, f32[3,48,512]{2,1,0:T(8,128)S(1)}, u32[]{:S(2)}, u32[]{:S(2)}) collective-permute-start(f32[3,48,512]{2,1,0:T(8,128)S(1)} %get-tuple-element.41), channel_id=1, source_target_pairs={{0,16},{32,48},{64,80},{96,112},{128,144},{160,176},{192,208},{224... | collective-permute-start | bytes 884744 | tf_op jit(solution)/shard_map/ppermute | solution.py:523
  48.5 22.7 %collective-permute-start.5 = (f32[3,48,512]{2,1,0:T(8,128)S(1)}, f32[3,48,512]{2,1,0:T(8,128)S(1)}, u32[]{:S(2)}, u32[]{:S(2)}) collective-permute-start(f32[3,48,512]{2,1,0:T(8,128)S(1)} %get-tuple-element.42), channel_id=1, source_target_pairs={{16,32},{48,64},{80,96},{112,128},{144,160},{176,192},{208,224},{3... | collective-permute-start | bytes 884744 | tf_op jit(solution)/shard_map/ppermute | solution.py:523

commit v5 on v4

--- a/solution.py
+++ b/solution.py
@@ -253,39 +253,41 @@
     )
 
 
-def kernel_pack_y(where, r_in, s_in, r, s, first, second, row, sems):
+def kernel_pack_y(where, r_in, s_in, r, first, second, row, slo, shi, sems):
     size = CX // PARTS
-    copies = [
-        [
-            pltpu.make_async_copy(
-                src.at[pl.ds(k * size, size)], dst.at[pl.ds(k * size, size)], sems.at[f, k]
-            )
-            for k in range(PARTS)
-        ]
-        for f, (src, dst) in enumerate(((r_in, r), (s_in, s)))
+    parts = [pl.ds(k * size, size) for k in range(PARTS)]
+    r_copies = [
+        pltpu.make_async_copy(r_in.at[p], r.at[p], sems.at[0, k]) for k, p in enumerate(parts)
     ]
-    for group in copies:
-        for copy in group:
-            copy.start()
+    s_copies = [
+        pltpu.make_async_copy(s_in.at[:, pl.ds(y, T)], out, sems.at[1, k])
+        for k, (y, out) in enumerate(((0, slo), (CY - T, shi)))
+    ]
+    for copy in (*r_copies, *s_copies):
+        copy.start()
     even = (where[1] & 1) == 0
-    sums = []
-    for f, own in enumerate((r, s)):
-        acc = jnp.zeros((T, NZ), F32)
-        for k in range(PARTS):
-            copies[f][k].wait()
-            planes = range(k * size, (k + 1) * size)
-            los = squeeze([own[i, tile(0)] for i in planes], 0)
-            his = squeeze([own[i, tile(CY // T - 1)] for i in planes], T - HY)
-            for j, (lo, hi) in enumerate(zip(los, his)):
-                at = tile((f * PARTS + k) * 3 + j)
-                first[at] = jnp.where(even, hi, lo)
-                second[at] = jnp.where(even, lo, hi)
-            for i in planes:
-                for t in range(CY // T):
-                    acc = acc + own[i, tile(t)]
-        sums.append(acc)
-    out = slab_sums(sums[0], 0) * (1.0 / CELLS) + slab_sums(sums[1], AGG)
-    row[...] = jnp.broadcast_to(out, row.shape)
+
+    def pack(f, k, lo_of, hi_of):
+        planes = range(k * size, (k + 1) * size)
+        los = squeeze([lo_of(i) for i in planes], 0)
+        his = squeeze([hi_of(i) for i in planes], T - HY)
+        for j, (lo, hi) in enumerate(zip(los, his)):
+            at = tile((f * PARTS + k) * 3 + j)
+            first[at] = jnp.where(even, hi, lo)
+            second[at] = jnp.where(even, lo, hi)
+
+    acc = jnp.zeros((T, NZ), F32)
+    for k in range(PARTS):
+        r_copies[k].wait()
+        pack(0, k, lambda i: r[i, tile(0)], lambda i: r[i, tile(CY // T - 1)])
+        for i in range(k * size, (k + 1) * size):
+            for t in range(CY // T):
+                acc = acc + r[i, tile(t)]
+    for copy in s_copies:
+        copy.wait()
+    for k in range(PARTS):
+        pack(1, k, lambda i: slo[i], lambda i: shi[i])
+    row[...] = jnp.broadcast_to(slab_sums(acc, 0) * (1.0 / CELLS), row.shape)
 
 
 def kernel_pack_x(where, r, s, first, second, g, rown, sown, xfirst, xsecond, row, *, n_py):
@@ -308,10 +310,7 @@
                 lo, hi = own[k, tile(t)], own[CX - 1 - k, tile(t)]
                 xfirst[at, tile(t)] = jnp.where(even, hi, lo)
                 xsecond[at, tile(t)] = jnp.where(even, lo, hi)
-    rows = g[...]
-    for k in range(2):
-        one = line_up(rows, k * AGG, n_py)
-        row[:, k : k + 1, :] = jnp.broadcast_to(one[None], (row.shape[0], 1, row.shape[2]))
+    row[...] = jnp.broadcast_to(line_up(g[...], 0, n_py), row.shape)
 
 
 def smooth_last(r, iref, zref, yref):
@@ -366,40 +365,42 @@
     smooth_last(r, iext, zref, yref)
 
     def apply(i, carry):
-        ru, uv, av = carry
+        ru, uv, av, sa = carry
         for t, box, mid in neighbours(zref, i, range(TILES)):
-            vv = (26.0 + s(i, t)) * mid - box
+            ss = s(i, t)
+            vv = (26.0 + ss) * mid - box
             v[i - H, tile(t)] = vv
             if 1 <= t < TILES - 1:
                 ru = ru + fold(r(i, t) * mid)
                 uv = uv + fold(mid * vv)
                 av = av + vv
-        return ru, uv, av
+                sa = sa + ss
+        return ru, uv, av, sa
 
     zero = jnp.zeros((T, LANES), F32)
-    ru, uv, av = lax.fori_loop(
-        H, H + CX, apply, (zero, zero, jnp.zeros((T, NZ), F32)), unroll=UNROLL
-    )
+    wide = jnp.zeros((T, NZ), F32)
+    ru, uv, av, sa = lax.fori_loop(H, H + CX, apply, (zero, zero, wide, wide), unroll=UNROLL)
     for k in range(H):
         for t in range(TILES):
             lo, hi = v[k, tile(t)], v[CX - 1 - k, tile(t)]
             vfirst[k, tile(t)] = jnp.where(even, hi, lo)
             vsecond[k, tile(t)] = jnp.where(even, lo, hi)
-    m = g1[:, 0, :]
     lane = iota((1, LANES), 1)
-    out = coarse_rows(inverse, m) + slab_sums(av, AGG) * (1.0 / CELLS)
+    out = coarse_rows(inverse, g1[...]) + slab_sums(av, AGG) * (1.0 / CELLS)
+    out = out + slab_sums(sa, 2 * AGG)
     out = out + jnp.where(lane == 24, total(ru), 0.0) + jnp.where(lane == 25, total(uv), 0.0)
     row[...] = jnp.broadcast_to(out, row.shape)
 
 
 def kernel_b(where, rown, sown, rhalo, shalo, iext, vown, vfirst, vsecond, inverse, g1, g2,
-             rref, qref, zref, vo, row, scal, yref, rows9, cref, *, n_px, n_py):
+             rref, qref, zref, vo, row, scal, shifts, yref, rows9, cref, *, n_px, n_py):
     g = g2[...]
-    m, shifts = g1[:, 0, :], g1[:, 1, :]
+    m = g1[...]
     c = line_up(g, 0, n_py)
+    shifts[...] = line_up(g, 2 * AGG, n_py)
     w = line_up(g, AGG, n_py)
     lane = iota(g.shape, 1)
-    tc = coarse_operator(c, shifts)
+    tc = coarse_operator(c, shifts[...])
     rz = total(jnp.where(lane == 24, g, 0.0)) + CELLS * total(m * c)
     curv = total(jnp.where(lane == 25, g, 0.0)) + total(c * (2.0 * CELLS * w + tc))
     alpha = rz / curv
@@ -461,13 +462,13 @@
     scal[...] = jnp.where(at == 0, rz, jnp.where(at == 1, curv, alpha))
 
 
-def kernel_c(where, sown, u, r1, un, vn, q, g1, g2, g3, scal, x_out, r_out,
+def kernel_c(where, sown, u, r1, un, vn, q, shifts, g2, g3, scal, x_out, r_out,
              x, r2, rows9, sems, *, n_px, n_py):
     g = g3[...]
     c = line_up(g, 0, n_py)
     w = line_up(g, AGG, n_py)
     lane = iota(g.shape, 1)
-    tc = coarse_operator(c, g1[:, 1, :])
+    tc = coarse_operator(c, shifts[...])
     rz, curv, alpha = scal[0:1, 0:1], scal[1:2, 0:1], scal[2:3, 0:1]
     rz1 = total(jnp.where(lane == 24, g, 0.0))
     zaz = total(jnp.where(lane == 25, g, 0.0)) + total(c * (2.0 * CELLS * w + tc))
@@ -519,7 +520,7 @@
 
 
 def swap(x, axis, n, odd):
-    pairs = [(i, i + 1) for i in range(odd, n - 1, 2)]
+    pairs = [(i, (i + 1) % n) for i in range(odd, n, 2)]
     return lax.ppermute(x, axis, pairs + [(j, i) for i, j in pairs])
 
 
@@ -535,17 +536,17 @@
     where = jnp.stack([lax.axis_index("px"), lax.axis_index("py")]).astype(jnp.int32)
     inputs = [pltpu.with_memory_space_constraint(f, pltpu.HBM) for f in (right_side, shift)]
     face = (2 * CX * HY, NZ)
-    r, s, first, second, row = call(
-        kernel_pack_y, (where, *inputs), [OWN, OWN, face, face, (n_py, LANES)],
-        [copies], "pack_y", in_specs=[SMEM, HBM, HBM],
+    r, first, second, row = call(
+        kernel_pack_y, (where, *inputs), [OWN, face, face, (n_py, LANES)],
+        [(CX, T, NZ), (CX, T, NZ), copies], "pack_y", in_specs=[SMEM, HBM, HBM],
     )
     first = swap(first, "py", n_py, 0)
     second = swap(second, "py", n_py, 1)
     g = all_rows(row, "py")
     face = (2 * H, YE, NZ)
     rown, sown, first, second, row = call(
-        kernel_pack_x, (where, r, s, first, second, g),
-        [TALL, TALL, face, face, (n_px, 2, width)], [], "pack_x", n_py=n_py,
+        kernel_pack_x, (where, r, shift, first, second, g),
+        [TALL, TALL, face, face, (n_px, width)], [], "pack_x", n_py=n_py,
     )
     first = swap(first, "px", n_px, 0)
     second = swap(second, "px", n_px, 1)
@@ -559,16 +560,16 @@
     first = swap(first, "px", n_px, 0)
     second = swap(second, "px", n_px, 1)
     g2 = all_rows(row, ("px", "py"))
-    r1, q, un, vn, row, scal = call(
+    r1, q, un, vn, row, scal, shifts = call(
         kernel_b,
         (where, rown, sown, rhalo, shalo, iext, v, first, second, coarse_inverse, g1, g2),
-        [EXT, EXT, EXT, OWN, (n, LANES), (8, LANES)],
+        [EXT, EXT, EXT, OWN, (n, LANES), (8, LANES), (n_px, width)],
         [EXT, (16, LANES), (n_px, width)], "second", **sizes,
     )
     g3 = all_rows(row, ("px", "py"))
     return tuple(
         call(
-            kernel_c, (where, sown, u, r1, un, vn, q, g1, g2, g3, scal),
+            kernel_c, (where, sown, u, r1, un, vn, q, shifts, g2, g3, scal),
             [OWN, OWN], [OWN, OWN, (16, LANES), copies], "third",
             out_specs=[HBM, HBM], **sizes,
         )

time: 98.9 us -> 94.3 us (0.953)
  blocking collectives: 68.9 us -> 64.4 us
    all_to_all x4, blocking collectives: 68.9 us -> 64.4 us  [all_rows(): return lax.all_to_all(x, axes, 0, 0, tiled=True)]
where the time goes in v5:
time: 94.3 us; the launch traced here: 94.1 us
  blocking collectives  64.4 us (68%)
  Pallas kernels  17.3 us (18%)
  starting transfers between devices  11.4 us (12%)
    all_to_all x4, blocking collectives, all_rows(): return lax.all_to_all(x, axes, 0, 0, tiled=True)  64.4 us
    pallas_call x5, Pallas kernels, call(): pl.pallas_call(functools.partial(body, **sizes) if sizes else body, in_sp...  17.3 us
    ppermute x6, starting transfers between devices, swap(): return lax.ppermute(x, axis, pairs + [(j, i) for i, j in pairs])  11.4 us
  transfers between devices with their start and end apart: 6, of which 0 were waited for; matrix products, arithmetic and copies ran while one was open for 0% of the time, Pallas kernels for 0%

profile of v5, /device:TPU:1, one launch (start us, length us, event | category | flops | bytes accessed | tf_op | source)
XLA Modules:
  0.0 94.1 jit_solution(10327071366813515557)
XLA Ops:
  0.6 0.0 copy-start
  0.6 0.1 pad_add_fusion.where
  0.7 0.0 copy-start.1
  0.7 2.2 %pack_y.1 = (f32[16,32,512]{2,1,0:T(8,128)S(1)}, f32[192,512]{1,0:T(8,128)S(1)}, f32[192,512]{1,0:T(8,128)S(1)}, f32[16,128]{1,0:T(8,128)S(1)}) custom-call(s32[2]{0:T(128)S(1)} %pad_add_fusion.where, f32[16,32,512]{2,1,0:T(8,128)} %r_in.1, f32[16,32,512]{2,1,0:T(8,128)} %s.1), custom_call_target="tpu_custom_call" | custom-call | tf_op jit(solution)/shard_map/pack_y/pallas_call | solution.py:511
  3.0 2.1 %collective-permute-start = (f32[192,512]{1,0:T(8,128)S(1)}, f32[192,512]{1,0:T(8,128)S(1)}, u32[]{:S(2)}, u32[]{:S(2)}) collective-permute-start(f32[192,512]{1,0:T(8,128)S(1)} %get-tuple-element.27), channel_id=1, source_target_pairs={{0,1},{2,3},{4,5},{6,7},{8,9},{10,11},{12,13},{14,15},{1,0},{3,2},... | collective-permute-start | bytes 1179656 | tf_op jit(solution)/shard_map/ppermute | solution.py:524
  5.1 4.3 %collective-permute-start.1 = (f32[192,512]{1,0:T(8,128)S(1)}, f32[192,512]{1,0:T(8,128)S(1)}, u32[]{:S(2)}, u32[]{:S(2)}) collective-permute-start(f32[192,512]{1,0:T(8,128)S(1)} %get-tuple-element.28), channel_id=1, source_target_pairs={{1,2},{3,4},{5,6},{7,8},{9,10},{11,12},{13,14},{15,0},{2,1},{4,3},... | collective-permute-start | bytes 1179656 | tf_op jit(solution)/shard_map/ppermute | solution.py:524
  9.3 9.7 %all_to_all.44 = f32[16,1,128]{2,1,0:T(1,128)S(1)} all-to-all(f32[16,1,128]{2,1,0:T(1,128)S(1)} %bitcast.27), channel_id=1, replica_groups=mesh['px'=16,'py'=16] {'py'}, dimensions={0} | all-to-all | bytes 16384 | tf_op jit(solution)/shard_map/all_to_all | solution.py:528
  19.1 0.0 collective-permute-done.first
  19.1 0.0 collective-permute-done.1.second
  19.1 0.0 copy-done
  19.1 0.8 pack_x.1
  19.9 2.4 %collective-permute-start.2 = (f32[6,48,512]{2,1,0:T(8,128)S(1)}, f32[6,48,512]{2,1,0:T(8,128)S(1)}, u32[]{:S(2)}, u32[]{:S(2)}) collective-permute-start(f32[6,48,512]{2,1,0:T(8,128)S(1)} %get-tuple-element.32), channel_id=1, source_target_pairs={{0,16},{32,48},{64,80},{96,112},{128,144},{160,176},{192,208},{224... | collective-permute-start | bytes 1769480 | tf_op jit(solution)/shard_map/ppermute | solution.py:524
  22.3 1.6 %collective-permute-start.3 = (f32[6,48,512]{2,1,0:T(8,128)S(1)}, f32[6,48,512]{2,1,0:T(8,128)S(1)}, u32[]{:S(2)}, u32[]{:S(2)}) collective-permute-start(f32[6,48,512]{2,1,0:T(8,128)S(1)} %get-tuple-element.33), channel_id=1, source_target_pairs={{16,32},{48,64},{80,96},{112,128},{144,160},{176,192},{208,224},{2... | collective-permute-start | bytes 1769480 | tf_op jit(solution)/shard_map/ppermute | solution.py:524
  23.9 14.5 %all_to_all.45 = f32[16,1,128]{2,1,0:T(1,128)S(1)} all-to-all(f32[16,1,128]{2,1,0:T(1,128)S(1)} %bitcast.26), channel_id=1, replica_groups=mesh['px'=16,'py'=16] {'px'}, dimensions={0} | all-to-all | bytes 16384 | tf_op jit(solution)/shard_map/all_to_all | solution.py:528
  38.4 0.0 collective-permute-done.2.first
  38.4 0.0 collective-permute-done.3.second
  38.4 0.0 copy-done.1
  38.4 5.3 %first.1 = (f32[6,48,512]{2,1,0:T(8,128)S(1)}, f32[6,48,512]{2,1,0:T(8,128)S(1)}, f32[22,48,512]{2,1,0:T(8,128)S(1)}, f32[16,48,512]{2,1,0:T(8,128)S(1)}, f32[22...) custom-call(s32[2]{0:T(128)S(1)} %pad_add_fusion.where, ...), custom_call_target="tpu_custom_call" | custom-call | tf_op jit(solution)/shard_map/first/pallas_call | solution.py:511
  43.7 0.7 collective-permute-start.4
  44.4 0.3 collective-permute-start.5
  44.7 21.6 %all_to_all.46 = f32[256,1,128]{2,1,0:T(1,128)S(1)} all-to-all(f32[256,1,128]{2,1,0:T(1,128)S(1)} %bitcast.21), channel_id=1, replica_groups=mesh['px'=16,'py'=16] {'px','py'}, dimensions={0} | all-to-all | bytes 262144 | tf_op jit(solution)/shard_map/all_to_all | solution.py:528
  66.3 0.0 collective-permute-done.4.vfirst
  66.3 0.0 collective-permute-done.5.vsecond
  66.3 6.1 %second.1 = (f32[22,48,512]{2,1,0:T(8,128)S(1)}, f32[22,48,512]{2,1,0:T(8,128)S(1)}, f32[22,48,512]{2,1,0:T(8,128)S(1)}, f32[16,32,512]{2,1,0:T(8,128)S(1)}, f32...) custom-call(s32[2]{0:T(128)S(1)} %pad_add_fusion.where, ...), custom_call_target="tpu_custom_call" | custom-call | tf_op jit(solution)/shard_map/second/pallas_call | solution.py:511
  72.4 18.6 %all_to_all.47 = f32[256,1,128]{2,1,0:T(1,128)S(1)} all-to-all(f32[256,1,128]{2,1,0:T(1,128)S(1)} %bitcast.22), channel_id=1, replica_groups=mesh['px'=16,'py'=16] {'px','py'}, dimensions={0} | all-to-all | bytes 262144 | tf_op jit(solution)/shard_map/all_to_all | solution.py:528
  91.0 2.9 %third.1 = (f32[16,32,512]{2,1,0:T(8,128)}, f32[16,32,512]{2,1,0:T(8,128)}) custom-call(s32[2]{0:T(128)S(1)} %pad_add_fusion.where, f32[16,48,512]{2,1,0:T(8,128)S(1)} %get-tuple-element.30.sown, f32[22,48,512]{2,1,0:T(8,128)S(1)} %get-tuple-element.35.u, f32[22,48,512]{2,1,0:T(8,128)S(1)} %get-tuple-element.43.r1, f32[22,48,512]{2,1,0:T(8,128)S(1)} %get-tuple-element.44.un, ...), custom_call_target="tpu_custom_call" | custom-call | tf_op jit(solution)/shard_map/third/pallas_call | solution.py:511
Async XLA Ops:
  0.6 18.4 %copy-start = (f32[16,32,512]{2,1,0:T(8,128)S(1)}, f32[16,32,512]{2,1,0:T(8,128)}, u32[]{:S(2)}) copy-start(f32[16,32,512]{2,1,0:T(8,128)} %s.1) | copy-start | bytes 3145732
  0.7 37.7 %copy-start.1 = (f32[8,2048]{1,0:T(8,128)S(1)}, f32[8,2048]{1,0:T(8,128)}, u32[]{:S(2)}) copy-start(f32[8,2048]{1,0:T(8,128)} %inverse.3) | copy-start | bytes 196612
  3.0 16.1 %collective-permute-start = (f32[192,512]{1,0:T(8,128)S(1)}, f32[192,512]{1,0:T(8,128)S(1)}, u32[]{:S(2)}, u32[]{:S(2)}) collective-permute-start(f32[192,512]{1,0:T(8,128)S(1)} %get-tuple-element.27), channel_id=1, source_target_pairs={{0,1},{2,3},{4,5},{6,7},{8,9},{10,11},{12,13},{14,15},{1,0},{3,2},... | collective-permute-start | bytes 1179656 | tf_op jit(solution)/shard_map/ppermute | solution.py:524
  5.1 14.0 %collective-permute-start.1 = (f32[192,512]{1,0:T(8,128)S(1)}, f32[192,512]{1,0:T(8,128)S(1)}, u32[]{:S(2)}, u32[]{:S(2)}) collective-permute-start(f32[192,512]{1,0:T(8,128)S(1)} %get-tuple-element.28), channel_id=1, source_target_pairs={{1,2},{3,4},{5,6},{7,8},{9,10},{11,12},{13,14},{15,0},{2,1},{4,3},... | collective-permute-start | bytes 1179656 | tf_op jit(solution)/shard_map/ppermute | solution.py:524
  19.9 18.5 %collective-permute-start.2 = (f32[6,48,512]{2,1,0:T(8,128)S(1)}, f32[6,48,512]{2,1,0:T(8,128)S(1)}, u32[]{:S(2)}, u32[]{:S(2)}) collective-permute-start(f32[6,48,512]{2,1,0:T(8,128)S(1)} %get-tuple-element.32), channel_id=1, source_target_pairs={{0,16},{32,48},{64,80},{96,112},{128,144},{160,176},{192,208},{224... | collective-permute-start | bytes 1769480 | tf_op jit(solution)/shard_map/ppermute | solution.py:524
  22.3 16.1 %collective-permute-start.3 = (f32[6,48,512]{2,1,0:T(8,128)S(1)}, f32[6,48,512]{2,1,0:T(8,128)S(1)}, u32[]{:S(2)}, u32[]{:S(2)}) collective-permute-start(f32[6,48,512]{2,1,0:T(8,128)S(1)} %get-tuple-element.33), channel_id=1, source_target_pairs={{16,32},{48,64},{80,96},{112,128},{144,160},{176,192},{208,224},{2... | collective-permute-start | bytes 1769480 | tf_op jit(solution)/shard_map/ppermute | solution.py:524
  43.7 22.6 %collective-permute-start.4 = (f32[3,48,512]{2,1,0:T(8,128)S(1)}, f32[3,48,512]{2,1,0:T(8,128)S(1)}, u32[]{:S(2)}, u32[]{:S(2)}) collective-permute-start(f32[3,48,512]{2,1,0:T(8,128)S(1)} %get-tuple-element.40), channel_id=1, source_target_pairs={{0,16},{32,48},{64,80},{96,112},{128,144},{160,176},{192,208},{224... | collective-permute-start | bytes 884744 | tf_op jit(solution)/shard_map/ppermute | solution.py:524
  44.4 21.9 %collective-permute-start.5 = (f32[3,48,512]{2,1,0:T(8,128)S(1)}, f32[3,48,512]{2,1,0:T(8,128)S(1)}, u32[]{:S(2)}, u32[]{:S(2)}) collective-permute-start(f32[3,48,512]{2,1,0:T(8,128)S(1)} %get-tuple-element.41), channel_id=1, source_target_pairs={{16,32},{48,64},{80,96},{112,128},{144,160},{176,192},{208,224},{2... | collective-permute-start | bytes 884744 | tf_op jit(solution)/shard_map/ppermute | solution.py:524

commit v6 on v5

--- a/solution.py
+++ b/solution.py
@@ -21,7 +21,6 @@
 UNROLL = 8
 PARTS = 4
 F32 = jnp.float32
-HIGH = lax.Precision.HIGHEST
 OWN = (CX, CY, NZ)
 EXT = (XE, YE, NZ)
 TALL = (CX, YE, NZ)
@@ -105,29 +104,35 @@
     return (a + b) + (c + d)
 
 
-def exact_dot(a, b):
-    return jnp.dot(a, b, precision=HIGH, preferred_element_type=F32)
-
-
 def slab_sums(acc, offset):
-    cell, lane = iota((NZ, LANES), 0), iota((NZ, LANES), 1)
-    pick = jnp.where(cell // SLAB + offset == lane, 1.0, 0.0).astype(F32)
-    return jnp.sum(exact_dot(acc, pick), axis=0, keepdims=True)
+    lane = iota((T, LANES), 1)
+    out = jnp.zeros((T, LANES), F32)
+    for k, part in enumerate(chunks(acc)):
+        for h, half in enumerate((lane < SLAB, lane >= SLAB)):
+            one = jnp.sum(jnp.where(half, part, 0.0), axis=1, keepdims=True)
+            out = jnp.where(lane == offset + 2 * k + h, one, out)
+    return jnp.sum(out, axis=0, keepdims=True)
 
 
 def spread(rows):
-    lane, cell = iota((LANES, NZ), 0), iota((LANES, NZ), 1)
-    return exact_dot(rows, jnp.where(cell // SLAB == lane, 1.0, 0.0).astype(F32))
+    low = iota((rows.shape[0], LANES), 1) < SLAB
+    return jnp.concatenate(
+        [jnp.where(low, rows[:, j : j + 1], rows[:, j + 1 : j + 2]) for j in range(0, AGG, 2)],
+        axis=1,
+    )
 
 
 def line_up(rows, offset, n_py):
-    width = n_py * AGG
-    src, dst = iota((LANES, width), 0), iota((LANES, width), 1)
-    repeat = jnp.where((dst & (AGG - 1)) + offset == src, 1.0, 0.0).astype(F32)
-    wide = exact_dot(rows, repeat)
-    row, lane = iota(wide.shape, 0), iota(wide.shape, 1)
-    wide = jnp.where((row & (n_py - 1)) == lane // AGG, wide, 0.0)
-    return jnp.sum(wide.reshape(rows.shape[0] // n_py, n_py, width), axis=1)
+    lane = iota(rows.shape, 1)
+    rows = jnp.where((lane >= offset) & (lane < offset + AGG), rows, 0.0)
+    if offset:
+        rows = pltpu.roll(rows, LANES - offset, axis=1)
+    out = []
+    for k in range(rows.shape[0] // n_py):
+        part = rows[k * n_py : (k + 1) * n_py]
+        part = pltpu.roll(part, 0, axis=1, stride=AGG, stride_axis=0)
+        out.append(jnp.sum(part, axis=0, keepdims=True)[:, : n_py * AGG])
+    return jnp.concatenate(out, axis=0)
 
 
 def coarse_rows(inverse, vector):
@@ -160,16 +165,6 @@
         + jnp.where(row == n - 1, 0.0, pltpu.roll(t, n - 1, axis=0))
     )
     return (27.0 * CELLS + shift_sums) * c - t
-
-
-def own_part(vector, where, ref):
-    ref[...] = vector
-    mine = ref[pl.ds(where[0], 1), :]
-    lane = iota(mine.shape, 1)
-    mine = jnp.where(lane // AGG == where[1], mine, 0.0)
-    src, dst = iota((mine.shape[1], LANES), 0), iota((mine.shape[1], LANES), 1)
-    pick = jnp.where((src & (AGG - 1)) == dst, 1.0, 0.0).astype(F32)
-    return exact_dot(jnp.broadcast_to(mine, (T, mine.shape[1])), pick)[:1]
 
 
 def coarse_planes(where, gathered, n_px, n_py, rows9):
@@ -393,19 +388,20 @@
 
 
 def kernel_b(where, rown, sown, rhalo, shalo, iext, vown, vfirst, vsecond, inverse, g1, g2,
-             rref, qref, zref, vo, row, scal, shifts, yref, rows9, cref, *, n_px, n_py):
+             rref, qref, zref, vo, row, scal, coarse, yref, rows9, *, n_px, n_py):
     g = g2[...]
     m = g1[...]
     c = line_up(g, 0, n_py)
-    shifts[...] = line_up(g, 2 * AGG, n_py)
+    shifts = line_up(g, 2 * AGG, n_py)
     w = line_up(g, AGG, n_py)
     lane = iota(g.shape, 1)
-    tc = coarse_operator(c, shifts[...])
+    tc = coarse_operator(c, shifts)
     rz = total(jnp.where(lane == 24, g, 0.0)) + CELLS * total(m * c)
     curv = total(jnp.where(lane == 25, g, 0.0)) + total(c * (2.0 * CELLS * w + tc))
     alpha = rz / curv
     e = w + tc * (1.0 / CELLS)
     mnew = m - alpha * e
+    coarse[0], coarse[1], coarse[2] = shifts, mnew, e
     cnew = coarse_rows(inverse, mnew)
     planes, boxes = coarse_planes(where, g2, n_px, n_py, rows9)
     r, s = Field(rown, rhalo), Field(sown, shalo)
@@ -450,29 +446,26 @@
     ru, uv, uq, av = lax.fori_loop(
         H, H + CX, apply, (zero, zero, zero, jnp.zeros((T, NZ), F32)), unroll=UNROLL
     )
-    e_own = own_part(e, where, cref)
-    m_own = own_part(mnew, where, cref)
     lane = iota((1, LANES), 1)
     out = cnew + slab_sums(av, AGG) * (1.0 / CELLS)
-    out = out + jnp.where(lane == 24, total(ru) + CELLS * total(m_own * cnew), 0.0)
-    out = out + jnp.where(lane == 25, total(uv), 0.0)
-    out = out + jnp.where(lane == 26, total(uq) + CELLS * total(e_own * cnew), 0.0)
+    for k, part in ((24, ru), (25, uv), (26, uq)):
+        out = out + jnp.where(lane == k, total(part), 0.0)
     row[...] = jnp.broadcast_to(out, row.shape)
     at = iota((8, LANES), 0)
     scal[...] = jnp.where(at == 0, rz, jnp.where(at == 1, curv, alpha))
 
 
-def kernel_c(where, sown, u, r1, un, vn, q, shifts, g2, g3, scal, x_out, r_out,
+def kernel_c(where, sown, u, r1, un, vn, q, coarse, g2, g3, scal, x_out, r_out,
              x, r2, rows9, sems, *, n_px, n_py):
     g = g3[...]
     c = line_up(g, 0, n_py)
     w = line_up(g, AGG, n_py)
     lane = iota(g.shape, 1)
-    tc = coarse_operator(c, shifts[...])
+    tc = coarse_operator(c, coarse[0])
     rz, curv, alpha = scal[0:1, 0:1], scal[1:2, 0:1], scal[2:3, 0:1]
-    rz1 = total(jnp.where(lane == 24, g, 0.0))
+    rz1 = total(jnp.where(lane == 24, g, 0.0)) + CELLS * total(c * coarse[1])
     zaz = total(jnp.where(lane == 25, g, 0.0)) + total(c * (2.0 * CELLS * w + tc))
-    zq = total(jnp.where(lane == 26, g, 0.0))
+    zq = total(jnp.where(lane == 26, g, 0.0)) + CELLS * total(c * coarse[2])
     beta = rz1 / rz
     alpha2 = rz1 / (zaz + 2.0 * beta * zq + beta * beta * curv)
     first = alpha + alpha2 * beta
@@ -560,16 +553,16 @@
     first = swap(first, "px", n_px, 0)
     second = swap(second, "px", n_px, 1)
     g2 = all_rows(row, ("px", "py"))
-    r1, q, un, vn, row, scal, shifts = call(
+    r1, q, un, vn, row, scal, coarse = call(
         kernel_b,
         (where, rown, sown, rhalo, shalo, iext, v, first, second, coarse_inverse, g1, g2),
-        [EXT, EXT, EXT, OWN, (n, LANES), (8, LANES), (n_px, width)],
-        [EXT, (16, LANES), (n_px, width)], "second", **sizes,
+        [EXT, EXT, EXT, OWN, (n, LANES), (8, LANES), (3, n_px, width)],
+        [EXT, (16, LANES)], "second", **sizes,
     )
     g3 = all_rows(row, ("px", "py"))
     return tuple(
         call(
-            kernel_c, (where, sown, u, r1, un, vn, q, shifts, g2, g3, scal),
+            kernel_c, (where, sown, u, r1, un, vn, q, coarse, g2, g3, scal),
             [OWN, OWN], [OWN, OWN, (16, LANES), copies], "third",
             out_specs=[HBM, HBM], **sizes,
         )

time: 94.3 us -> 92.8 us (0.984)
  Pallas kernels: 17.3 us -> 16.2 us
    pallas_call x5, Pallas kernels: 17.3 us -> 16.2 us  [call(): pl.pallas_call(functools.partial(body, **sizes) if sizes else body, in_sp...]
where the time goes in v6:
time: 92.8 us; the launch traced here: 92.6 us
  blocking collectives  64.2 us (69%)
  Pallas kernels  16.2 us (17%)
  starting transfers between devices  11.4 us (12%)
    all_to_all x4, blocking collectives, all_rows(): return lax.all_to_all(x, axes, 0, 0, tiled=True)  64.2 us
    pallas_call x5, Pallas kernels, call(): pl.pallas_call(functools.partial(body, **sizes) if sizes else body, in_sp...  16.2 us
    ppermute x6, starting transfers between devices, swap(): return lax.ppermute(x, axis, pairs + [(j, i) for i, j in pairs])  11.4 us
  transfers between devices with their start and end apart: 6, of which 0 were waited for; matrix products, arithmetic and copies ran while one was open for 0% of the time, Pallas kernels for 0%

profile of v6, /device:TPU:1, one launch (start us, length us, event | category | flops | bytes accessed | tf_op | source)
XLA Modules:
  0.0 92.6 jit_solution(7020226680545124227)
XLA Ops:
  0.6 0.0 copy-start
  0.6 0.1 pad_add_fusion.where
  0.7 0.0 copy-start.1
  0.7 2.0 %pack_y.1 = (f32[16,32,512]{2,1,0:T(8,128)S(1)}, f32[192,512]{1,0:T(8,128)S(1)}, f32[192,512]{1,0:T(8,128)S(1)}, f32[16,128]{1,0:T(8,128)S(1)}) custom-call(s32[2]{0:T(128)S(1)} %pad_add_fusion.where, f32[16,32,512]{2,1,0:T(8,128)} %r_in.1, f32[16,32,512]{2,1,0:T(8,128)} %s.1), custom_call_target="tpu_custom_call" | custom-call | tf_op jit(solution)/shard_map/pack_y/pallas_call | solution.py:504
  2.8 2.1 %collective-permute-start = (f32[192,512]{1,0:T(8,128)S(1)}, f32[192,512]{1,0:T(8,128)S(1)}, u32[]{:S(2)}, u32[]{:S(2)}) collective-permute-start(f32[192,512]{1,0:T(8,128)S(1)} %get-tuple-element.27), channel_id=1, source_target_pairs={{0,1},{2,3},{4,5},{6,7},{8,9},{10,11},{12,13},{14,15},{1,0},{3,2},... | collective-permute-start | bytes 1179656 | tf_op jit(solution)/shard_map/ppermute | solution.py:517
  4.9 4.3 %collective-permute-start.1 = (f32[192,512]{1,0:T(8,128)S(1)}, f32[192,512]{1,0:T(8,128)S(1)}, u32[]{:S(2)}, u32[]{:S(2)}) collective-permute-start(f32[192,512]{1,0:T(8,128)S(1)} %get-tuple-element.28), channel_id=1, source_target_pairs={{1,2},{3,4},{5,6},{7,8},{9,10},{11,12},{13,14},{15,0},{2,1},{4,3},... | collective-permute-start | bytes 1179656 | tf_op jit(solution)/shard_map/ppermute | solution.py:517
  9.2 9.7 %all_to_all.44 = f32[16,1,128]{2,1,0:T(1,128)S(1)} all-to-all(f32[16,1,128]{2,1,0:T(1,128)S(1)} %bitcast.27), channel_id=1, replica_groups=mesh['px'=16,'py'=16] {'py'}, dimensions={0} | all-to-all | bytes 16384 | tf_op jit(solution)/shard_map/all_to_all | solution.py:521
  18.9 0.0 collective-permute-done.first
  18.9 0.0 collective-permute-done.1.second
  18.9 0.0 copy-done
  18.9 0.8 pack_x.1
  19.7 2.4 %collective-permute-start.2 = (f32[6,48,512]{2,1,0:T(8,128)S(1)}, f32[6,48,512]{2,1,0:T(8,128)S(1)}, u32[]{:S(2)}, u32[]{:S(2)}) collective-permute-start(f32[6,48,512]{2,1,0:T(8,128)S(1)} %get-tuple-element.32), channel_id=1, source_target_pairs={{0,16},{32,48},{64,80},{96,112},{128,144},{160,176},{192,208},{224... | collective-permute-start | bytes 1769480 | tf_op jit(solution)/shard_map/ppermute | solution.py:517
  22.1 1.6 %collective-permute-start.3 = (f32[6,48,512]{2,1,0:T(8,128)S(1)}, f32[6,48,512]{2,1,0:T(8,128)S(1)}, u32[]{:S(2)}, u32[]{:S(2)}) collective-permute-start(f32[6,48,512]{2,1,0:T(8,128)S(1)} %get-tuple-element.33), channel_id=1, source_target_pairs={{16,32},{48,64},{80,96},{112,128},{144,160},{176,192},{208,224},{2... | collective-permute-start | bytes 1769480 | tf_op jit(solution)/shard_map/ppermute | solution.py:517
  23.7 14.5 %all_to_all.45 = f32[16,1,128]{2,1,0:T(1,128)S(1)} all-to-all(f32[16,1,128]{2,1,0:T(1,128)S(1)} %bitcast.26), channel_id=1, replica_groups=mesh['px'=16,'py'=16] {'px'}, dimensions={0} | all-to-all | bytes 16384 | tf_op jit(solution)/shard_map/all_to_all | solution.py:521
  38.2 0.0 collective-permute-done.2.first
  38.2 0.0 collective-permute-done.3.second
  38.2 0.0 copy-done.1
  38.2 5.0 %first.1 = (f32[6,48,512]{2,1,0:T(8,128)S(1)}, f32[6,48,512]{2,1,0:T(8,128)S(1)}, f32[22,48,512]{2,1,0:T(8,128)S(1)}, f32[16,48,512]{2,1,0:T(8,128)S(1)}, f32[22...) custom-call(s32[2]{0:T(128)S(1)} %pad_add_fusion.where, ...), custom_call_target="tpu_custom_call" | custom-call | tf_op jit(solution)/shard_map/first/pallas_call | solution.py:504
  43.2 0.7 collective-permute-start.4
  44.0 0.3 collective-permute-start.5
  44.2 21.6 %all_to_all.46 = f32[256,1,128]{2,1,0:T(1,128)S(1)} all-to-all(f32[256,1,128]{2,1,0:T(1,128)S(1)} %bitcast.21), channel_id=1, replica_groups=mesh['px'=16,'py'=16] {'px','py'}, dimensions={0} | all-to-all | bytes 262144 | tf_op jit(solution)/shard_map/all_to_all | solution.py:521
  65.8 0.0 collective-permute-done.4.vfirst
  65.8 0.0 collective-permute-done.5.vsecond
  65.8 5.7 %second.1 = (f32[22,48,512]{2,1,0:T(8,128)S(1)}, f32[22,48,512]{2,1,0:T(8,128)S(1)}, f32[22,48,512]{2,1,0:T(8,128)S(1)}, f32[16,32,512]{2,1,0:T(8,128)S(1)}, f32...) custom-call(s32[2]{0:T(128)S(1)} %pad_add_fusion.where, ...), custom_call_target="tpu_custom_call" | custom-call | tf_op jit(solution)/shard_map/second/pallas_call | solution.py:504
  71.5 18.4 %all_to_all.47 = f32[256,1,128]{2,1,0:T(1,128)S(1)} all-to-all(f32[256,1,128]{2,1,0:T(1,128)S(1)} %bitcast.22), channel_id=1, replica_groups=mesh['px'=16,'py'=16] {'px','py'}, dimensions={0} | all-to-all | bytes 262144 | tf_op jit(solution)/shard_map/all_to_all | solution.py:521
  89.9 2.6 %third.1 = (f32[16,32,512]{2,1,0:T(8,128)}, f32[16,32,512]{2,1,0:T(8,128)}) custom-call(s32[2]{0:T(128)S(1)} %pad_add_fusion.where, f32[16,48,512]{2,1,0:T(8,128)S(1)} %get-tuple-element.30.sown, f32[22,48,512]{2,1,0:T(8,128)S(1)} %get-tuple-element.35.u, f32[22,48,512]{2,1,0:T(8,128)S(1)} %get-tuple-element.43.r1, f32[22,48,512]{2,1,0:T(8,128)S(1)} %get-tuple-element.44.un, ...), custom_call_target="tpu_custom_call" | custom-call | tf_op jit(solution)/shard_map/third/pallas_call | solution.py:504
Async XLA Ops:
  0.6 18.3 %copy-start = (f32[16,32,512]{2,1,0:T(8,128)S(1)}, f32[16,32,512]{2,1,0:T(8,128)}, u32[]{:S(2)}) copy-start(f32[16,32,512]{2,1,0:T(8,128)} %s.1) | copy-start | bytes 3145732
  0.7 37.5 %copy-start.1 = (f32[8,2048]{1,0:T(8,128)S(1)}, f32[8,2048]{1,0:T(8,128)}, u32[]{:S(2)}) copy-start(f32[8,2048]{1,0:T(8,128)} %inverse.3) | copy-start | bytes 196612
  2.8 16.1 %collective-permute-start = (f32[192,512]{1,0:T(8,128)S(1)}, f32[192,512]{1,0:T(8,128)S(1)}, u32[]{:S(2)}, u32[]{:S(2)}) collective-permute-start(f32[192,512]{1,0:T(8,128)S(1)} %get-tuple-element.27), channel_id=1, source_target_pairs={{0,1},{2,3},{4,5},{6,7},{8,9},{10,11},{12,13},{14,15},{1,0},{3,2},... | collective-permute-start | bytes 1179656 | tf_op jit(solution)/shard_map/ppermute | solution.py:517
  4.9 14.0 %collective-permute-start.1 = (f32[192,512]{1,0:T(8,128)S(1)}, f32[192,512]{1,0:T(8,128)S(1)}, u32[]{:S(2)}, u32[]{:S(2)}) collective-permute-start(f32[192,512]{1,0:T(8,128)S(1)} %get-tuple-element.28), channel_id=1, source_target_pairs={{1,2},{3,4},{5,6},{7,8},{9,10},{11,12},{13,14},{15,0},{2,1},{4,3},... | collective-permute-start | bytes 1179656 | tf_op jit(solution)/shard_map/ppermute | solution.py:517
  19.7 18.5 %collective-permute-start.2 = (f32[6,48,512]{2,1,0:T(8,128)S(1)}, f32[6,48,512]{2,1,0:T(8,128)S(1)}, u32[]{:S(2)}, u32[]{:S(2)}) collective-permute-start(f32[6,48,512]{2,1,0:T(8,128)S(1)} %get-tuple-element.32), channel_id=1, source_target_pairs={{0,16},{32,48},{64,80},{96,112},{128,144},{160,176},{192,208},{224... | collective-permute-start | bytes 1769480 | tf_op jit(solution)/shard_map/ppermute | solution.py:517
  22.1 16.1 %collective-permute-start.3 = (f32[6,48,512]{2,1,0:T(8,128)S(1)}, f32[6,48,512]{2,1,0:T(8,128)S(1)}, u32[]{:S(2)}, u32[]{:S(2)}) collective-permute-start(f32[6,48,512]{2,1,0:T(8,128)S(1)} %get-tuple-element.33), channel_id=1, source_target_pairs={{16,32},{48,64},{80,96},{112,128},{144,160},{176,192},{208,224},{2... | collective-permute-start | bytes 1769480 | tf_op jit(solution)/shard_map/ppermute | solution.py:517
  43.2 22.6 %collective-permute-start.4 = (f32[3,48,512]{2,1,0:T(8,128)S(1)}, f32[3,48,512]{2,1,0:T(8,128)S(1)}, u32[]{:S(2)}, u32[]{:S(2)}) collective-permute-start(f32[3,48,512]{2,1,0:T(8,128)S(1)} %get-tuple-element.40), channel_id=1, source_target_pairs={{0,16},{32,48},{64,80},{96,112},{128,144},{160,176},{192,208},{224... | collective-permute-start | bytes 884744 | tf_op jit(solution)/shard_map/ppermute | solution.py:517
  44.0 21.9 %collective-permute-start.5 = (f32[3,48,512]{2,1,0:T(8,128)S(1)}, f32[3,48,512]{2,1,0:T(8,128)S(1)}, u32[]{:S(2)}, u32[]{:S(2)}) collective-permute-start(f32[3,48,512]{2,1,0:T(8,128)S(1)} %get-tuple-element.41), channel_id=1, source_target_pairs={{16,32},{48,64},{80,96},{112,128},{144,160},{176,192},{208,224},{2... | collective-permute-start | bytes 884744 | tf_op jit(solution)/shard_map/ppermute | solution.py:517

commit v7 on v6

--- a/solution.py
+++ b/solution.py
@@ -18,7 +18,7 @@
 YE = CY + 2 * T
 TILES = YE // T
 LANES = 128
-UNROLL = 8
+UNROLL = 16
 PARTS = 4
 F32 = jnp.float32
 OWN = (CX, CY, NZ)
@@ -427,7 +427,7 @@
         block = 0 if i < H else 1 if i < H + CX else 2
         image(i, planes[block], box_plane(boxes, i - H))
     inner = 3.0 * boxes[1]
-    each(H + 1, H + CX - 1, lambda i: image(i, planes[1], inner), unroll=2)
+    each(H + 1, H + CX - 1, lambda i: image(i, planes[1], inner), unroll=7)
     smooth_last(lambda i, t: rref[i, tile(t)], iext, zref, yref)
 
     def apply(i, carry):
@@ -541,8 +541,8 @@
         kernel_pack_x, (where, r, shift, first, second, g),
         [TALL, TALL, face, face, (n_px, width)], [], "pack_x", n_py=n_py,
     )
+    second = swap(second, "px", n_px, 1)
     first = swap(first, "px", n_px, 0)
-    second = swap(second, "px", n_px, 1)
     g1 = all_rows(row, "px")
     halo = (2 * H, YE, NZ)
     face = (H, YE, NZ)
@@ -550,8 +550,8 @@
         kernel_a, (where, rown, sown, first, second, coarse_inverse, g1),
         [halo, halo, EXT, TALL, EXT, face, face, (n, LANES)], [EXT], "first", **sizes,
     )
+    second = swap(second, "px", n_px, 1)
     first = swap(first, "px", n_px, 0)
-    second = swap(second, "px", n_px, 1)
     g2 = all_rows(row, ("px", "py"))
     r1, q, un, vn, row, scal, coarse = call(
         kernel_b,

time: 92.8 us -> 92.4 us (level)
  no operation moved by 1% of the time
where the time goes in v7:
time: 92.4 us; the launch traced here: 92.2 us
  blocking collectives  64.2 us (69%)
  Pallas kernels  15.7 us (17%)
  starting transfers between devices  11.4 us (12%)
    all_to_all x4, blocking collectives, all_rows(): return lax.all_to_all(x, axes, 0, 0, tiled=True)  64.2 us
    pallas_call x5, Pallas kernels, call(): pl.pallas_call(functools.partial(body, **sizes) if sizes else body, in_sp...  15.7 us
    ppermute x6, starting transfers between devices, swap(): return lax.ppermute(x, axis, pairs + [(j, i) for i, j in pairs])  11.4 us
  transfers between devices with their start and end apart: 6, of which 0 were waited for; matrix products, arithmetic and copies ran while one was open for 0% of the time, Pallas kernels for 0%

profile of v7, /device:TPU:1, one launch (start us, length us, event | category | flops | bytes accessed | tf_op | source)
XLA Modules:
  0.0 92.2 jit_solution(7509941461195706921)
XLA Ops:
  0.6 0.0 copy-start
  0.6 0.1 pad_add_fusion.where
  0.7 0.0 copy-start.1
  0.7 2.0 %pack_y.1 = (f32[16,32,512]{2,1,0:T(8,128)S(1)}, f32[192,512]{1,0:T(8,128)S(1)}, f32[192,512]{1,0:T(8,128)S(1)}, f32[16,128]{1,0:T(8,128)S(1)}) custom-call(s32[2]{0:T(128)S(1)} %pad_add_fusion.where, f32[16,32,512]{2,1,0:T(8,128)} %r_in.1, f32[16,32,512]{2,1,0:T(8,128)} %s.1), custom_call_target="tpu_custom_call" | custom-call | tf_op jit(solution)/shard_map/pack_y/pallas_call | solution.py:504
  2.8 2.1 %collective-permute-start = (f32[192,512]{1,0:T(8,128)S(1)}, f32[192,512]{1,0:T(8,128)S(1)}, u32[]{:S(2)}, u32[]{:S(2)}) collective-permute-start(f32[192,512]{1,0:T(8,128)S(1)} %get-tuple-element.27), channel_id=1, source_target_pairs={{0,1},{2,3},{4,5},{6,7},{8,9},{10,11},{12,13},{14,15},{1,0},{3,2},... | collective-permute-start | bytes 1179656 | tf_op jit(solution)/shard_map/ppermute | solution.py:517
  4.9 4.3 %collective-permute-start.1 = (f32[192,512]{1,0:T(8,128)S(1)}, f32[192,512]{1,0:T(8,128)S(1)}, u32[]{:S(2)}, u32[]{:S(2)}) collective-permute-start(f32[192,512]{1,0:T(8,128)S(1)} %get-tuple-element.28), channel_id=1, source_target_pairs={{1,2},{3,4},{5,6},{7,8},{9,10},{11,12},{13,14},{15,0},{2,1},{4,3},... | collective-permute-start | bytes 1179656 | tf_op jit(solution)/shard_map/ppermute | solution.py:517
  9.2 9.7 %all_to_all.44 = f32[16,1,128]{2,1,0:T(1,128)S(1)} all-to-all(f32[16,1,128]{2,1,0:T(1,128)S(1)} %bitcast.27), channel_id=1, replica_groups=mesh['px'=16,'py'=16] {'py'}, dimensions={0} | all-to-all | bytes 16384 | tf_op jit(solution)/shard_map/all_to_all | solution.py:521
  18.9 0.0 collective-permute-done.first
  18.9 0.0 collective-permute-done.1.second
  18.9 0.0 copy-done
  18.9 0.8 pack_x.1
  19.7 2.4 %collective-permute-start.2 = (f32[6,48,512]{2,1,0:T(8,128)S(1)}, f32[6,48,512]{2,1,0:T(8,128)S(1)}, u32[]{:S(2)}, u32[]{:S(2)}) collective-permute-start(f32[6,48,512]{2,1,0:T(8,128)S(1)} %get-tuple-element.32), channel_id=1, source_target_pairs={{0,16},{32,48},{64,80},{96,112},{128,144},{160,176},{192,208},{224... | collective-permute-start | bytes 1769480 | tf_op jit(solution)/shard_map/ppermute | solution.py:517
  22.1 1.6 %collective-permute-start.3 = (f32[6,48,512]{2,1,0:T(8,128)S(1)}, f32[6,48,512]{2,1,0:T(8,128)S(1)}, u32[]{:S(2)}, u32[]{:S(2)}) collective-permute-start(f32[6,48,512]{2,1,0:T(8,128)S(1)} %get-tuple-element.33), channel_id=1, source_target_pairs={{16,32},{48,64},{80,96},{112,128},{144,160},{176,192},{208,224},{2... | collective-permute-start | bytes 1769480 | tf_op jit(solution)/shard_map/ppermute | solution.py:517
  23.7 14.5 %all_to_all.45 = f32[16,1,128]{2,1,0:T(1,128)S(1)} all-to-all(f32[16,1,128]{2,1,0:T(1,128)S(1)} %bitcast.26), channel_id=1, replica_groups=mesh['px'=16,'py'=16] {'px'}, dimensions={0} | all-to-all | bytes 16384 | tf_op jit(solution)/shard_map/all_to_all | solution.py:521
  38.2 0.0 collective-permute-done.2.first
  38.2 0.0 collective-permute-done.3.second
  38.2 0.0 copy-done.1
  38.2 4.7 %first.1 = (f32[6,48,512]{2,1,0:T(8,128)S(1)}, f32[6,48,512]{2,1,0:T(8,128)S(1)}, f32[22,48,512]{2,1,0:T(8,128)S(1)}, f32[16,48,512]{2,1,0:T(8,128)S(1)}, f32[22...) custom-call(s32[2]{0:T(128)S(1)} %pad_add_fusion.where, ...), custom_call_target="tpu_custom_call" | custom-call | tf_op jit(solution)/shard_map/first/pallas_call | solution.py:504
  43.0 0.7 collective-permute-start.4
  43.7 0.3 collective-permute-start.5
  44.0 21.6 %all_to_all.46 = f32[256,1,128]{2,1,0:T(1,128)S(1)} all-to-all(f32[256,1,128]{2,1,0:T(1,128)S(1)} %bitcast.21), channel_id=1, replica_groups=mesh['px'=16,'py'=16] {'px','py'}, dimensions={0} | all-to-all | bytes 262144 | tf_op jit(solution)/shard_map/all_to_all | solution.py:521
  65.6 0.0 collective-permute-done.4.vfirst
  65.6 0.0 collective-permute-done.5.vsecond
  65.6 5.4 %second.1 = (f32[22,48,512]{2,1,0:T(8,128)S(1)}, f32[22,48,512]{2,1,0:T(8,128)S(1)}, f32[22,48,512]{2,1,0:T(8,128)S(1)}, f32[16,32,512]{2,1,0:T(8,128)S(1)}, f32...) custom-call(s32[2]{0:T(128)S(1)} %pad_add_fusion.where, ...), custom_call_target="tpu_custom_call" | custom-call | tf_op jit(solution)/shard_map/second/pallas_call | solution.py:504
  71.0 18.4 %all_to_all.47 = f32[256,1,128]{2,1,0:T(1,128)S(1)} all-to-all(f32[256,1,128]{2,1,0:T(1,128)S(1)} %bitcast.22), channel_id=1, replica_groups=mesh['px'=16,'py'=16] {'px','py'}, dimensions={0} | all-to-all | bytes 262144 | tf_op jit(solution)/shard_map/all_to_all | solution.py:521
  89.4 2.6 %third.1 = (f32[16,32,512]{2,1,0:T(8,128)}, f32[16,32,512]{2,1,0:T(8,128)}) custom-call(s32[2]{0:T(128)S(1)} %pad_add_fusion.where, f32[16,48,512]{2,1,0:T(8,128)S(1)} %get-tuple-element.30.sown, f32[22,48,512]{2,1,0:T(8,128)S(1)} %get-tuple-element.35.u, f32[22,48,512]{2,1,0:T(8,128)S(1)} %get-tuple-element.43.r1, f32[22,48,512]{2,1,0:T(8,128)S(1)} %get-tuple-element.44.un, ...), custom_call_target="tpu_custom_call" | custom-call | tf_op jit(solution)/shard_map/third/pallas_call | solution.py:504
Async XLA Ops:
  0.6 18.3 %copy-start = (f32[16,32,512]{2,1,0:T(8,128)S(1)}, f32[16,32,512]{2,1,0:T(8,128)}, u32[]{:S(2)}) copy-start(f32[16,32,512]{2,1,0:T(8,128)} %s.1) | copy-start | bytes 3145732
  0.7 37.5 %copy-start.1 = (f32[8,2048]{1,0:T(8,128)S(1)}, f32[8,2048]{1,0:T(8,128)}, u32[]{:S(2)}) copy-start(f32[8,2048]{1,0:T(8,128)} %inverse.3) | copy-start | bytes 196612
  2.8 16.1 %collective-permute-start = (f32[192,512]{1,0:T(8,128)S(1)}, f32[192,512]{1,0:T(8,128)S(1)}, u32[]{:S(2)}, u32[]{:S(2)}) collective-permute-start(f32[192,512]{1,0:T(8,128)S(1)} %get-tuple-element.27), channel_id=1, source_target_pairs={{0,1},{2,3},{4,5},{6,7},{8,9},{10,11},{12,13},{14,15},{1,0},{3,2},... | collective-permute-start | bytes 1179656 | tf_op jit(solution)/shard_map/ppermute | solution.py:517
  4.9 14.0 %collective-permute-start.1 = (f32[192,512]{1,0:T(8,128)S(1)}, f32[192,512]{1,0:T(8,128)S(1)}, u32[]{:S(2)}, u32[]{:S(2)}) collective-permute-start(f32[192,512]{1,0:T(8,128)S(1)} %get-tuple-element.28), channel_id=1, source_target_pairs={{1,2},{3,4},{5,6},{7,8},{9,10},{11,12},{13,14},{15,0},{2,1},{4,3},... | collective-permute-start | bytes 1179656 | tf_op jit(solution)/shard_map/ppermute | solution.py:517
  19.7 18.5 %collective-permute-start.2 = (f32[6,48,512]{2,1,0:T(8,128)S(1)}, f32[6,48,512]{2,1,0:T(8,128)S(1)}, u32[]{:S(2)}, u32[]{:S(2)}) collective-permute-start(f32[6,48,512]{2,1,0:T(8,128)S(1)} %get-tuple-element.32), channel_id=1, source_target_pairs={{0,16},{32,48},{64,80},{96,112},{128,144},{160,176},{192,208},{224... | collective-permute-start | bytes 1769480 | tf_op jit(solution)/shard_map/ppermute | solution.py:517
  22.1 16.1 %collective-permute-start.3 = (f32[6,48,512]{2,1,0:T(8,128)S(1)}, f32[6,48,512]{2,1,0:T(8,128)S(1)}, u32[]{:S(2)}, u32[]{:S(2)}) collective-permute-start(f32[6,48,512]{2,1,0:T(8,128)S(1)} %get-tuple-element.33), channel_id=1, source_target_pairs={{16,32},{48,64},{80,96},{112,128},{144,160},{176,192},{208,224},{2... | collective-permute-start | bytes 1769480 | tf_op jit(solution)/shard_map/ppermute | solution.py:517
  43.0 22.6 %collective-permute-start.4 = (f32[3,48,512]{2,1,0:T(8,128)S(1)}, f32[3,48,512]{2,1,0:T(8,128)S(1)}, u32[]{:S(2)}, u32[]{:S(2)}) collective-permute-start(f32[3,48,512]{2,1,0:T(8,128)S(1)} %get-tuple-element.40), channel_id=1, source_target_pairs={{0,16},{32,48},{64,80},{96,112},{128,144},{160,176},{192,208},{224... | collective-permute-start | bytes 884744 | tf_op jit(solution)/shard_map/ppermute | solution.py:517
  43.7 21.9 %collective-permute-start.5 = (f32[3,48,512]{2,1,0:T(8,128)S(1)}, f32[3,48,512]{2,1,0:T(8,128)S(1)}, u32[]{:S(2)}, u32[]{:S(2)}) collective-permute-start(f32[3,48,512]{2,1,0:T(8,128)S(1)} %get-tuple-element.41), channel_id=1, source_target_pairs={{16,32},{48,64},{80,96},{112,128},{144,160},{176,192},{208,224},{2... | collective-permute-start | bytes 884744 | tf_op jit(solution)/shard_map/ppermute | solution.py:517
